TPU v7x, 32 devices: a whole 2x2x4 slice. The times are simulated.
32 devices in a mesh: width: 4 (over y, x), shard: 8 (over z, core).
Axes of the slice: x: 2, y: 2, z: 4, core: 2. Of those that a mesh axis runs over, the one named last changes fastest.
Arguments:
- layer_input: bfloat16 [32768, 768], P(('width', 'shard')), may hold values from -6 to 6
- segment_ids: int32 [64, 512], P(('width', 'shard')), may hold values from 0 to 3, never falling along the last dimension, each value on 1 to 256 neighbouring positions
- group_heads: int32 [4], P('width'), may hold values from 3 to 12, as said below
- w_query: float32 [768, 768], P('shard'), may hold values from -0.21875 to 0.21875
- b_query: float32 [768], P('shard'), may hold values from -3 to 3
- w_key: float32 [768, 768], P('shard'), may hold values from -0.21875 to 0.21875
- w_value: float32 [768, 768], P('shard'), may hold values from -0.21875 to 0.21875
- b_value: float32 [768], P('shard'), may hold values from -3 to 3
- w_out: float32 [768, 768], P('shard'), may hold values from -1.75 to 1.75
- b_out: float32 [768], P('shard'), may hold values from -2 to 2
- gain_one: float32 [768], P('shard'), may hold values from 0.25 to 1.75
- shift_one: float32 [768], P('shard'), may hold values from -2 to 2
- w_inner: float32 [768, 3072], P('shard'), may hold values from -0.21875 to 0.21875
- b_inner: float32 [3072], P('shard'), may hold values from -3 to 3
- w_outer: float32 [3072, 768], P('shard'), may hold values from -0.21875 to 0.21875
- b_outer: float32 [768], P('shard'), may hold values from -2 to 2
- gain_two: float32 [768], P('shard'), may hold values from 0.25 to 1.75
- shift_two: float32 [768], P('shard'), may hold values from -2 to 2
- out_grad: bfloat16 [32768, 768], P(('width', 'shard')), may hold values from -6 to 6
Outputs:
- layer_output: bfloat16 [32768, 768], P(('width', 'shard'))
- input_grad: bfloat16 [32768, 768], P(('width', 'shard'))
- w_query_grad: float32 [768, 768], P('shard')
- b_query_grad: float32 [768], P('shard')
- w_key_grad: float32 [768, 768], P('shard')
- w_value_grad: float32 [768, 768], P('shard')
- b_value_grad: float32 [768], P('shard')
- w_out_grad: float32 [768, 768], P('shard')
- b_out_grad: float32 [768], P('shard')
- gain_one_grad: float32 [768], P('shard')
- shift_one_grad: float32 [768], P('shard')
- w_inner_grad: float32 [768, 3072], P('shard')
- b_inner_grad: float32 [3072], P('shard')
- w_outer_grad: float32 [3072, 768], P('shard')
- b_outer_grad: float32 [768], P('shard')
- gain_two_grad: float32 [768], P('shard')
- shift_two_grad: float32 [768], P('shard')
Inputs may be any that keep to these rules, and one draw needn't show every extreme that they name: `group_heads`: the 4 groups keep 1, 2, 3 and 4 times 12 // 4 leading heads, each multiple on exactly one group, and 256 leading neurons for each kept head. `segment_ids`: within each row of 512 tokens the ids never fall; a token attends only to tokens of its own row with its own id.
All inputs are finite; a program needn't handle non-finite values.
Results may differ from a plain program's by a relative error of at most 0.017.
The roundings to bfloat16 on the way count: a program that leaves them out, or rounds other values in their place, can miss the bound.
Values may be sent and summed in bfloat16 or wider, within the bound.
A program may use at most 192 MiB of HBM per device.

v0:
```python
import jax
import jax.numpy as jnp
from jax import lax
from jax.sharding import PartitionSpec as P

HEADS = 12
HEAD_DIM = 64
FF = 3072
D = 768
SEQ = 512


def to_half(value):
    return value.astype(jnp.bfloat16)


def norm_parts(total):
    row_mean = jnp.mean(total, axis=-1, keepdims=True)
    centered = total - row_mean
    inverse = lax.rsqrt(jnp.mean(centered * centered, axis=-1, keepdims=True) + 1e-06)
    return (centered * inverse, inverse)


def norm_back(grad_normed, normed, inverse):
    first = jnp.mean(grad_normed, axis=-1, keepdims=True)
    second = jnp.mean(grad_normed * normed, axis=-1, keepdims=True)
    return inverse * (grad_normed - first - normed * second)


def row_scores(query_row, key_row, segment_row, score_scale):
    scores = (
        jnp.einsum("qhd,khd->hqk", query_row, key_row, preferred_element_type=jnp.float32)
        * score_scale
    )
    same_doc = segment_row[:, None] == segment_row[None, :]
    return jnp.where(same_doc[None], scores, -1e30)


def column_sum(value):
    return jnp.sum(value.astype(jnp.float32), axis=0)


def weight_grad(left, right):
    return jnp.einsum("ti,tj->ij", left, right, preferred_element_type=jnp.float32)


def back_product(grad_rows, weight):
    return jnp.einsum("tj,ij->ti", grad_rows, weight, preferred_element_type=jnp.float32)


def forward_product(rows_in, weight):
    return jnp.dot(rows_in, weight, preferred_element_type=jnp.float32)


def body(
    layer_input,
    segment_ids,
    group_heads,
    w_query,
    b_query,
    w_key,
    w_value,
    b_value,
    w_out,
    b_out,
    gain_one,
    shift_one,
    w_inner,
    b_inner,
    w_outer,
    b_outer,
    gain_two,
    shift_two,
    out_grad,
):
    score_scale = HEAD_DIM ** (-0.5)
    kept_heads = group_heads[0]
    head_mask = (jnp.arange(D) // HEAD_DIM < kept_heads).astype(jnp.float32)
    unit_mask = (jnp.arange(FF) // (FF // HEADS) < kept_heads).astype(jnp.float32)
    attn_full = (
        lax.all_gather(to_half(w_query), "shard", axis=0, tiled=True),
        lax.all_gather(to_half(w_key), "shard", axis=0, tiled=True),
        lax.all_gather(to_half(w_value), "shard", axis=0, tiled=True),
        lax.all_gather(to_half(w_out), "shard", axis=0, tiled=True),
        lax.all_gather(to_half(b_query), "shard", axis=0, tiled=True),
        lax.all_gather(to_half(b_value), "shard", axis=0, tiled=True),
        lax.all_gather(to_half(b_out), "shard", axis=0, tiled=True),
        lax.all_gather(to_half(gain_one), "shard", axis=0, tiled=True),
        lax.all_gather(to_half(shift_one), "shard", axis=0, tiled=True),
    )
    full_query, full_key, full_value, full_out = (
        attn_full[0],
        attn_full[1],
        attn_full[2],
        attn_full[3],
    )
    bias_query = attn_full[4].astype(jnp.float32)
    bias_value = attn_full[5].astype(jnp.float32)
    bias_out = attn_full[6].astype(jnp.float32)
    gain_first = attn_full[7].astype(jnp.float32)
    shift_first = attn_full[8].astype(jnp.float32)
    queries = to_half(forward_product(layer_input, full_query) + bias_query)
    keys = to_half(forward_product(layer_input, full_key))
    values = to_half(forward_product(layer_input, full_value) + bias_value)
    row_count = layer_input.shape[0] // SEQ
    attended_rows = []
    log_rows = []
    for row_index in range(row_count):
        window = slice(row_index * SEQ, (row_index + 1) * SEQ)
        query_row = queries[window].reshape(SEQ, HEADS, HEAD_DIM)
        key_row = keys[window].reshape(SEQ, HEADS, HEAD_DIM)
        value_row = values[window].reshape(SEQ, HEADS, HEAD_DIM)
        scores = row_scores(query_row, key_row, segment_ids[row_index], score_scale)
        top_score = jnp.max(scores, axis=-1, keepdims=True)
        expanded = jnp.exp(scores - top_score)
        denominator = jnp.sum(expanded, axis=-1, keepdims=True)
        probs_low = to_half(expanded / denominator)
        attended_rows.append(
            jnp.einsum(
                "hqk,khd->qhd", probs_low, value_row, preferred_element_type=jnp.float32
            ).reshape(SEQ, D)
        )
        log_rows.append(top_score + jnp.log(denominator))
    attended = to_half(jnp.concatenate(attended_rows, axis=0) * head_mask)
    branch = forward_product(attended, full_out) + bias_out
    normed_one, inverse_one = norm_parts(layer_input.astype(jnp.float32) + branch)
    hidden = normed_one * gain_first + shift_first
    hidden_low = to_half(hidden)
    ffn_full = (
        lax.all_gather(to_half(w_inner), "shard", axis=0, tiled=True),
        lax.all_gather(to_half(w_outer), "shard", axis=0, tiled=True),
        lax.all_gather(to_half(b_inner), "shard", axis=0, tiled=True),
        lax.all_gather(to_half(b_outer), "shard", axis=0, tiled=True),
        lax.all_gather(to_half(gain_two), "shard", axis=0, tiled=True),
        lax.all_gather(to_half(shift_two), "shard", axis=0, tiled=True),
    )
    full_inner, full_outer = (ffn_full[0], ffn_full[1])
    bias_inner = ffn_full[2].astype(jnp.float32)
    bias_outer = ffn_full[3].astype(jnp.float32)
    gain_second = ffn_full[4].astype(jnp.float32)
    shift_second = ffn_full[5].astype(jnp.float32)
    inner = forward_product(hidden_low, full_inner) + bias_inner

    def gelu_exact(value):
        return jax.nn.gelu(value, approximate=False)

    gelu_value, gelu_pull = jax.vjp(gelu_exact, inner)
    active = to_half(gelu_value * unit_mask)
    outer = forward_product(active, full_outer) + bias_outer
    normed_two, inverse_two = norm_parts(hidden + outer)
    layer_output = to_half(normed_two * gain_second + shift_second)
    top_grad = out_grad.astype(jnp.float32)
    shift_two_grad = jnp.sum(top_grad, axis=0)
    gain_two_grad = jnp.sum(top_grad * normed_two, axis=0)
    res_two_grad = norm_back(top_grad * gain_second, normed_two, inverse_two)
    outer_grad = to_half(res_two_grad)
    b_outer_grad = column_sum(outer_grad)
    w_outer_grad = weight_grad(active, outer_grad)
    active_grad = back_product(outer_grad, full_outer)
    inner_grad = to_half(gelu_pull(active_grad * unit_mask)[0])
    b_inner_grad = column_sum(inner_grad)
    w_inner_grad = weight_grad(hidden_low, inner_grad)
    hidden_grad = res_two_grad + back_product(inner_grad, full_inner)
    shift_one_grad = jnp.sum(hidden_grad, axis=0)
    gain_one_grad = jnp.sum(hidden_grad * normed_one, axis=0)
    res_one_grad = norm_back(hidden_grad * gain_first, normed_one, inverse_one)
    branch_grad = to_half(res_one_grad)
    b_out_grad = column_sum(branch_grad)
    w_out_grad = weight_grad(attended, branch_grad)
    attended_grad = to_half(back_product(branch_grad, full_out)) * to_half(head_mask)
    query_rows = []
    key_rows = []
    value_rows = []
    for row_index in range(row_count):
        window = slice(row_index * SEQ, (row_index + 1) * SEQ)
        query_row = queries[window].reshape(SEQ, HEADS, HEAD_DIM)
        key_row = keys[window].reshape(SEQ, HEADS, HEAD_DIM)
        value_row = values[window].reshape(SEQ, HEADS, HEAD_DIM)
        grad_row = attended_grad[window].reshape(SEQ, HEADS, HEAD_DIM)
        scores = row_scores(query_row, key_row, segment_ids[row_index], score_scale)
        probs = jnp.exp(scores - log_rows[row_index])
        prob_grad = jnp.einsum(
            "qhd,khd->hqk", grad_row, value_row, preferred_element_type=jnp.float32
        )
        value_rows.append(
            jnp.einsum(
                "hqk,qhd->khd", to_half(probs), grad_row, preferred_element_type=jnp.float32
            ).reshape(SEQ, D)
        )
        score_grad = to_half(
            probs * (prob_grad - jnp.sum(probs * prob_grad, axis=-1, keepdims=True))
        )
        query_rows.append(
            (
                jnp.einsum("hqk,khd->qhd", score_grad, key_row, preferred_element_type=jnp.float32)
                * score_scale
            ).reshape(SEQ, D)
        )
        key_rows.append(
            (
                jnp.einsum(
                    "hqk,qhd->khd", score_grad, query_row, preferred_element_type=jnp.float32
                )
                * score_scale
            ).reshape(SEQ, D)
        )
    query_grad = to_half(jnp.concatenate(query_rows, axis=0))
    key_grad = to_half(jnp.concatenate(key_rows, axis=0))
    value_grad = to_half(jnp.concatenate(value_rows, axis=0))
    b_query_grad = column_sum(query_grad)
    b_value_grad = column_sum(value_grad)
    w_query_grad = weight_grad(layer_input, query_grad)
    w_key_grad = weight_grad(layer_input, key_grad)
    w_value_grad = weight_grad(layer_input, value_grad)
    input_grad = to_half(
        res_one_grad
        + back_product(query_grad, full_query)
        + back_product(key_grad, full_key)
        + back_product(value_grad, full_value)
    )
    owned = (
        lax.psum_scatter(w_query_grad, "shard", scatter_dimension=0, tiled=True),
        lax.psum_scatter(w_key_grad, "shard", scatter_dimension=0, tiled=True),
        lax.psum_scatter(w_value_grad, "shard", scatter_dimension=0, tiled=True),
        lax.psum_scatter(w_out_grad, "shard", scatter_dimension=0, tiled=True),
        lax.psum_scatter(w_inner_grad, "shard", scatter_dimension=0, tiled=True),
        lax.psum_scatter(w_outer_grad, "shard", scatter_dimension=0, tiled=True),
        lax.psum_scatter(b_query_grad, "shard", scatter_dimension=0, tiled=True),
        lax.psum_scatter(b_value_grad, "shard", scatter_dimension=0, tiled=True),
        lax.psum_scatter(b_out_grad, "shard", scatter_dimension=0, tiled=True),
        lax.psum_scatter(gain_one_grad, "shard", scatter_dimension=0, tiled=True),
        lax.psum_scatter(shift_one_grad, "shard", scatter_dimension=0, tiled=True),
        lax.psum_scatter(b_inner_grad, "shard", scatter_dimension=0, tiled=True),
        lax.psum_scatter(b_outer_grad, "shard", scatter_dimension=0, tiled=True),
        lax.psum_scatter(gain_two_grad, "shard", scatter_dimension=0, tiled=True),
        lax.psum_scatter(shift_two_grad, "shard", scatter_dimension=0, tiled=True),
    )
    summed = (
        lax.psum(owned[0].astype(jnp.bfloat16), "width").astype(jnp.float32),
        lax.psum(owned[1].astype(jnp.bfloat16), "width").astype(jnp.float32),
        lax.psum(owned[2].astype(jnp.bfloat16), "width").astype(jnp.float32),
        lax.psum(owned[3].astype(jnp.bfloat16), "width").astype(jnp.float32),
        lax.psum(owned[4].astype(jnp.bfloat16), "width").astype(jnp.float32),
        lax.psum(owned[5].astype(jnp.bfloat16), "width").astype(jnp.float32),
        lax.psum(owned[6].astype(jnp.bfloat16), "width").astype(jnp.float32),
        lax.psum(owned[7].astype(jnp.bfloat16), "width").astype(jnp.float32),
        lax.psum(owned[8].astype(jnp.bfloat16), "width").astype(jnp.float32),
        lax.psum(owned[9].astype(jnp.bfloat16), "width").astype(jnp.float32),
        lax.psum(owned[10].astype(jnp.bfloat16), "width").astype(jnp.float32),
        lax.psum(owned[11].astype(jnp.bfloat16), "width").astype(jnp.float32),
        lax.psum(owned[12].astype(jnp.bfloat16), "width").astype(jnp.float32),
        lax.psum(owned[13].astype(jnp.bfloat16), "width").astype(jnp.float32),
        lax.psum(owned[14].astype(jnp.bfloat16), "width").astype(jnp.float32),
    )
    matrices = (summed[0], summed[1], summed[2], summed[3], summed[4], summed[5])
    vectors = (
        summed[6],
        summed[7],
        summed[8],
        summed[9],
        summed[10],
        summed[11],
        summed[12],
        summed[13],
        summed[14],
    )
    return (
        layer_output,
        input_grad,
        matrices[0],
        vectors[0],
        matrices[1],
        matrices[2],
        vectors[1],
        matrices[3],
        vectors[2],
        vectors[3],
        vectors[4],
        matrices[4],
        vectors[5],
        matrices[5],
        vectors[6],
        vectors[7],
        vectors[8],
    )


def solution(mesh):
    placed = (
        P(("width", "shard"), None),
        P(("width", "shard"), None),
        P("width"),
        P("shard", None),
        P("shard"),
        P("shard", None),
        P("shard", None),
        P("shard"),
        P("shard", None),
        P("shard"),
        P("shard"),
        P("shard"),
        P("shard", None),
        P("shard"),
        P("shard", None),
        P("shard"),
        P("shard"),
        P("shard"),
        P(("width", "shard"), None),
    )
    return jax.shard_map(
        body,
        mesh=mesh,
        in_specs=placed,
        out_specs=(
            P(("width", "shard"), None),
            P(("width", "shard"), None),
            P("shard", None),
            P("shard"),
            P("shard", None),
            P("shard", None),
            P("shard"),
            P("shard", None),
            P("shard"),
            P("shard"),
            P("shard"),
            P("shard", None),
            P("shard"),
            P("shard", None),
            P("shard"),
            P("shard"),
            P("shard"),
        ),
        check_vma=False,
    )
```

profile of v0, /device:TPU:0, one launch (start us, length us, event | category | flops | bytes accessed | tf_op | source)
XLA Modules:
  0.0 702.1 jit_solution(7718175819478079136)
XLA Ops:
  21.4 30.5 %all-reduce.18 = (bf16[768]{0:T(1024)(128)(2,1)S(1)}, bf16[768]{0:T(1024)(128)(2,1)S(1)}, bf16[768]{0:T(1024)(128)(2,1)S(1)}, bf16[768]{0:T(1024)(128)(2,1)S(1)}...) all-reduce(bf16[768]{0:T(1024)(128)(2,1)S(1)} %dynamic-update-slice, ...), channel_id=1, replica_groups=mesh['width'=4,'shard'=8] {'shard'}, use_global_device_ids=true, to_apply=%add.2 | all-reduce | flops 6144 | bytes 24576
  53.7 12.7 %all-gather = bf16[8,1,384]{2,1,0:T(2,128)(2,1)S(1)} all-gather(bf16[1,1,384]{2,1,0:T(2,128)(2,1)S(1)} %reshape.298), channel_id=1, replica_groups=mesh['width'=4,'shard'=8] {'shard'}, dimensions={0}, use_global_device_ids=true | all-gather | bytes 6912 | tf_op jit(solution)/shard_map/all_gather | solution.py:132
  79.4 5.1 all-gather.12.cloned.1.call-done
  94.6 4.6 fusion.17
  106.0 4.5 fusion.16
  115.3 46.7 %all-gather.16.cloned.1.call-done = bf16[768,3072]{1,0:T(8,128)(2,1)} async-done(((bf16[96,3072]{1,0:T(8,128)(2,1)}), bf16[768,3072]{1,0:T(8,128)(2,1)}) %all-gather.16.cloned.1.call-update) | async-done | bytes 4718608 | tf_op jit(solution)/shard_map/all_gather | solution.py:130
  162.0 38.3 %multiply_convert_fusion.2 = (bf16[1024,3072]{1,0:T(8,128)(2,1)}, f32[1024,3072]{1,0:T(8,128)}, f32[1024,3072]{1,0:T(8,128)}) fusion(f32[3072]{0:T(1024)S(1)} %fusion.43, f32[3072]{0:T(1024)S(1)} %bitcast.136, bf16[768,3072]{1,0:T(8,128)(2,1)} %all-gather.16.cloned.1.call-done, f32[1024,768]{0,1:T(8,128)S(1)} %get-tuple-element.115, ...), kind=kOutput, calls=%fused_computation.10 | convolution fusion | flops 5046534144 | bytes 39360512 | tf_op jit(solution)/shard_map/dot_general | solution.py:52
  200.3 13.7 %all-gather.18.cloned.1.call-done = bf16[3072,768]{1,0:T(8,128)(2,1)} async-done(((bf16[384,768]{1,0:T(8,128)(2,1)}), bf16[3072,768]{1,0:T(8,128)(2,1)}) %all-gather.18.cloned.1.call-update) | async-done | bytes 4718608 | tf_op jit(solution)/shard_map/all_gather | solution.py:131
  214.0 9.1 %fusion.82 = (f32[1024]{0:T(1024)S(1)}, f32[1024,768]{0,1:T(8,128)S(1)}) fusion(f32[768]{0:T(1024)S(1)} %copy-done.55, bf16[1024,3072]{1,0:T(8,128)(2,1)} %get-tuple-element.95, bf16[3072,768]{1,0:T(8,128)(2,1)} %all-gather.18.cloned.1.call-done, f32[768]{0:T(1024)S(1)} %convert_element_type.285, f32[768]{0:T(1024)S(1)} %convert_element_type.283, ...), kind=kOutput, calls=%fused_computation.159 | convolution fusion | flops 4837342208 | bytes 17323008 | tf_op jit(solution)/shard_map/dot_general | solution.py:52
  228.5 18.1 %convert_reduce_fusion = (f32[3072]{0:T(1024)S(1)}, bf16[1024,3072]{1,0:T(8,128)(2,1)}) fusion(f32[1024,3072]{1,0:T(8,128)} %get-tuple-element.96, f32[3072]{0:T(1024)S(1)} %fusion.43, bf16[1024,768]{0,1:T(8,128)(2,1)S(1)} %get-tuple-element.92, bf16[3072,768]{1,0:T(8,128)(2,1)} %all-gather.18.cloned.1.call-done, f32[1024,3072]{1,0:T(8,128)} %get-tuple-element.116, ...), kind=kOutput, calls=%fused_computation.2 | convolution fusion | flops 4888458240 | bytes 37785600 | tf_op jit(solution)/shard_map/tj,ij->ti/dot_general | solution.py:48
  246.6 11.7 %multiply_reduce_fusion.2 = (f32[768]{0:T(1024)S(1)}, f32[1024]{0:T(1024)S(1)}, f32[1024]{0:T(1024)S(1)}, f32[768]{0:T(1024)}, f32[1024,768]{0,1:T(8,128)S(1)}) fusion(f32[1024,768]{0,1:T(8,128)} %copy-done.5, f32[1024]{0:T(1024)S(1)} %add_rsqrt_fusion.1, f32[1024]{0:T(1024)S(1)} %broadcast_multiply_fusion.5, f32[768]{0:T(1024)S(1)} %convert_element_type.283, ...), kind=kOutput, calls=%fused_computation.55 | convolution fusion | flops 4845989888 | bytes 22065152 | tf_op jit(solution)/shard_map/tj,ij->ti/dot_general | solution.py:48
  266.3 7.6 %fusion.33 = bf16[12,64,512]{2,1,0:T(8,128)(2,1)S(1)} fusion(bf16[512,12,64]{0,2,1:T(8,128)(2,1)S(1)} %bitcast.116, f32[12,512]{1,0:T(8,128)S(1)} %log_add_fusion, f32[12,512,512]{1,2,0:T(8,128)} %copy-done, pred[512,512]{0,1:T(8,128)(4,1)S(1)} %copy-done.15), kind=kOutput, calls=%fused_computation.89 | convolution fusion | flops 415629312 | bytes 14442496 | tf_op jit(solution)/shard_map/hqk,qhd->khd/dot_general | solution.py:186
  283.8 13.6 %multiply_reduce_fusion.1 = (f32[12,512]{1,0:T(8,128)S(1)}, f32[12,512,512]{1,2,0:T(8,128)}) fusion(f32[12,512]{1,0:T(8,128)S(1)} %log_add_fusion.1, f32[12,512,512]{1,2,0:T(8,128)} %copy-done.1, pred[512,512]{0,1:T(8,128)(4,1)} %copy-done.16, bf16[512,12,64]{0,2,1:T(8,128)(2,1)} %bitcast.119, bf16[512,12,64]{0,2,1:T(8,128)(2,1)} %bitcast.114), kind=kOutput, calls=%fused_computation.7 | convolution fusion | flops 418375680 | bytes 27049984 | tf_op jit(solution)/shard_map/qhd,khd->hqk/dot_general | solution.py:182
  297.5 10.5 %multiply_convert_fusion.1 = bf16[12,512,512]{1,2,0:T(8,128)(2,1)S(1)} fusion(f32[12,512,512]{1,2,0:T(8,128)} %get-tuple-element.123, f32[12,512]{1,0:T(8,128)S(1)} %get-tuple-element.122, f32[12,512]{1,0:T(8,128)S(1)} %log_add_fusion.1, f32[12,512,512]{1,2,0:T(8,128)} %copy-done.1, pred[512,512]{0,1:T(8,128)(4,1)} %copy-done.16), kind=kLoop, calls=%fused_computation.6 | loop fusion | flops 18874368 | bytes 31768576 | tf_op jit(solution)/shard_map/convert_element_type | solution.py:14
  312.7 10.7 %multiply_reduce_fusion = (f32[12,512]{1,0:T(8,128)S(1)}, f32[12,512,512]{1,2,0:T(8,128)}) fusion(f32[12,512]{1,0:T(8,128)S(1)} %log_add_fusion, f32[12,512,512]{1,2,0:T(8,128)} %copy-done, pred[512,512]{0,1:T(8,128)(4,1)S(1)} %copy-done.15, bf16[512,12,64]{0,2,1:T(8,128)(2,1)S(1)} %bitcast.117, bf16[512,12,64]{0,2,1:T(8,128)(2,1)S(1)} %bitcast.113), kind=kOutput, calls=%fused_computation.4 | convolution fusion | flops 418375680 | bytes 27049984 | tf_op jit(solution)/shard_map/qhd,khd->hqk/dot_general | solution.py:182
  323.6 7.1 %multiply_convert_fusion = bf16[12,512,512]{1,2,0:T(8,128)(2,1)S(1)} fusion(f32[12,512,512]{1,2,0:T(8,128)} %get-tuple-element.121, f32[12,512]{1,0:T(8,128)S(1)} %get-tuple-element.120, f32[12,512]{1,0:T(8,128)S(1)} %log_add_fusion, f32[12,512,512]{1,2,0:T(8,128)S(1)} %bitcast.95, pred[512,512]{0,1:T(8,128)(4,1)S(1)} %copy-done.15), kind=kLoop, calls=%fused_computation.3 | loop fusion | flops 18874368 | bytes 31768576 | tf_op jit(solution)/shard_map/convert_element_type | solution.py:14
  355.7 10.8 %fusion.69 = f32[768,3072]{1,0:T(8,128)} fusion(bf16[1024,3072]{1,0:T(8,128)(2,1)} %get-tuple-element.125, f32[1024,768]{0,1:T(8,128)} %copy-done.5, f32[768]{0:T(1024)S(1)} %convert_element_type.285, f32[768]{0:T(1024)S(1)} %convert_element_type.283, f32[1024]{0:T(1024)S(1)} %add_rsqrt_fusion.1, f32[1024]{0:T(1024)S(1)} %broadcast_multiply_fusion.5), kind=kOutput, calls=%fused_computation.150 | convolution fusion | flops 4835770368 | bytes 18888704 | tf_op jit(solution)/shard_map/ti,tj->ij/dot_general | solution.py:44
  366.6 9.9 %fusion.83 = f32[3072,768]{1,0:T(8,128)} fusion(bf16[1024,3072]{1,0:T(8,128)(2,1)} %get-tuple-element.95, bf16[1024,768]{0,1:T(8,128)(2,1)} %copy-done.37), kind=kOutput, calls=%fused_computation.160 | convolution fusion | flops 4831838208 | bytes 17301504 | tf_op jit(solution)/shard_map/ti,tj->ij/dot_general | solution.py:44
  381.8 31.2 %reduce-scatter.19.cloned.1.call-done = f32[96,768]{1,0:T(8,128)} async-done(((f32[768,768]{1,0:T(8,128)}), f32[96,768]{1,0:T(8,128)}) %reduce-scatter.19.cloned.1.call-update) | async-done | bytes 294928
  414.8 99.4 %reduce-scatter.15.cloned.1.call-done = f32[96,3072]{1,0:T(8,128)} async-done(((f32[768,3072]{1,0:T(8,128)}), f32[96,3072]{1,0:T(8,128)}) %reduce-scatter.15.cloned.1.call-update) | async-done | bytes 1179664 | tf_op jit(solution)/shard_map/reduce_scatter | solution.py:226
  516.4 97.9 %reduce-scatter.17.cloned.1.call-done = f32[384,768]{1,0:T(8,128)} async-done(((f32[3072,768]{1,0:T(8,128)}), f32[384,768]{1,0:T(8,128)}) %reduce-scatter.17.cloned.1.call-update) | async-done | bytes 1179664 | tf_op jit(solution)/shard_map/reduce_scatter | solution.py:227
  624.1 26.4 %all-reduce.17 = (bf16[768]{0:T(1024)(128)(2,1)S(1)}, bf16[768]{0:T(1024)(128)(2,1)S(1)}, bf16[768]{0:T(1024)(128)(2,1)S(1)}, bf16[768]{0:T(1024)(128)(2,1)S(1)}...) all-reduce(f32[768]{0:T(1024)S(1)} %convert_reduce_fusion.5, ...), channel_id=3, replica_groups=mesh['width'=4,'shard'=8] {'shard'}, use_global_device_ids=true, to_apply=%region_17.18.clone | all-reduce | flops 9216 | bytes 55296
  651.2 10.0 %all-reduce.19 = (bf16[96]{0:T(256)(128)(2,1)S(1)}, bf16[96]{0:T(256)(128)(2,1)S(1)}, bf16[96]{0:T(256)(128)(2,1)S(1)}, bf16[96]{0:T(256)(128)(2,1)S(1)}, bf16[9...) all-reduce(bf16[96]{0:T(256)(128)(2,1)S(1)} %dynamic-slice.43, ...), channel_id=1, replica_groups=mesh['width'=4,'shard'=8] {'width'}, use_global_device_ids=true, to_apply=%region_18.19 | all-reduce | flops 1152 | bytes 4608 | tf_op jit(solution)/shard_map/psum | solution.py:245
  676.5 8.6 %all-reduce.23.cloned.1.call-done = (bf16[96,768]{0,1:T(8,128)(2,1)}, bf16[96,768]{0,1:T(8,128)(2,1)}, bf16[96,768]{0,1:T(8,128)(2,1)}, bf16[96,768]{1,0:T(8,128...) async-done(((bf16[96,768]{0,1:T(8,128)(2,1)}, bf16[96,768]{0,1:T(8,128)(2,1)}, bf16[96,768]{0,1:T(8,128)(2,1)}, bf16[96,768]{1,0:T(8,128)(2,1)}, ...) | async-done | bytes 1769488 | tf_op jit(solution)/shard_map/psum | solution.py:239
  (310 shorter events, 145.5 us)
Async XLA Ops:
  7.2 64.1 %all-gather.8.cloned.1.call-start = ((), (), s32[]{:S(2)}) async-start(), calls=%async_computation.6 | async-start | bytes 1327104 | tf_op jit(solution)/shard_map/all_gather | solution.py:83
  9.0 66.7 %all-gather.10.cloned.1.call-start = ((), (), s32[]{:S(2)}) async-start(), calls=%async_computation.7 | async-start | bytes 1327104 | tf_op jit(solution)/shard_map/all_gather | solution.py:81
  10.8 42.9 %copy-start.56 = (s32[2,512]{1,0:T(2,128)S(1)}, s32[2,512]{1,0:T(2,128)}, u32[]{:S(2)}) copy-start(s32[2,512]{1,0:T(2,128)} %param.20) | copy-start | bytes 12292
  10.8 73.6 %all-gather.12.cloned.1.call-start = ((), (), s32[]{:S(2)}) async-start(), calls=%async_computation.8 | async-start | bytes 1327104 | tf_op jit(solution)/shard_map/all_gather | solution.py:82
  12.5 54.4 %copy-start.32 = (bf16[1024,768]{1,0:T(8,128)(2,1)S(1)}, bf16[1024,768]{1,0:T(8,128)(2,1)}, u32[]{:S(2)}) copy-start(bf16[1024,768]{1,0:T(8,128)(2,1)} %param.37) | copy-start | bytes 4718596
  12.5 98.0 %all-gather.14.cloned.1.call-start = ((), (), s32[]{:S(2)}) async-start(), calls=%async_computation.9 | async-start | bytes 1327104 | tf_op jit(solution)/shard_map/all_gather | solution.py:84
  14.3 147.6 %all-gather.16.cloned.1.call-start = ((), (), s32[]{:S(2)}) async-start(), calls=%async_computation.10 | async-start | bytes 5308416 | tf_op jit(solution)/shard_map/all_gather | solution.py:130
  15.3 198.7 %all-gather.18.cloned.1.call-start = ((), (), s32[]{:S(2)}) async-start(), calls=%async_computation.11 | async-start | bytes 5308416 | tf_op jit(solution)/shard_map/all_gather | solution.py:131
  17.6 359.0 %reduce-scatter.13.cloned.1.call-start = ((), (), s32[]{:S(2)}) async-start(), calls=%async_computation.12 | async-start | bytes 2654208 | tf_op jit(solution)/shard_map/reduce_scatter | solution.py:225
  66.6 25.9 %copy-start.14 = (pred[512,512]{0,1:T(8,128)(4,1)}, pred[512,512]{0,1:T(8,128)(4,1)S(1)}, u32[]{:S(2)}) copy-start(pred[512,512]{0,1:T(8,128)(4,1)S(1)} %broadcast_compare_fusion) | copy-start | bytes 786436
  66.9 37.2 %copy-start.16 = (pred[512,512]{0,1:T(8,128)(4,1)}, pred[512,512]{0,1:T(8,128)(4,1)S(1)}, u32[]{:S(2)}) copy-start(pred[512,512]{0,1:T(8,128)(4,1)S(1)} %broadcast_compare_fusion.1) | copy-start | bytes 786436
  79.3 19.9 %copy-start.12 = (bf16[512,768]{0,1:T(8,128)(2,1)}, bf16[512,768]{0,1:T(8,128)(2,1)S(1)}, u32[]{:S(2)}) copy-start(bf16[512,768]{0,1:T(8,128)(2,1)S(1)} %get-tuple-element.102) | copy-start | bytes 2359300
  114.9 99.1 %copy-start.5 = (f32[1024,768]{0,1:T(8,128)}, f32[1024,768]{0,1:T(8,128)S(1)}, u32[]{:S(2)}) copy-start(f32[1024,768]{0,1:T(8,128)S(1)} %get-tuple-element.115) | copy-start | bytes 9437188
  162.0 52.1 %copy-start.55 = (f32[768]{0:T(1024)S(1)}, f32[768]{0:T(1024)}, u32[]{:S(2)}) copy-start(f32[768]{0:T(1024)} %convert_element_type.294) | copy-start | bytes 9220
  228.5 18.1 %copy-start.37 = (bf16[1024,768]{0,1:T(8,128)(2,1)}, bf16[1024,768]{0,1:T(8,128)(2,1)S(1)}, u32[]{:S(2)}) copy-start(bf16[1024,768]{0,1:T(8,128)(2,1)S(1)} %get-tuple-element.92) | copy-start | bytes 4718596
  263.1 115.1 %reduce-scatter.23.cloned.1.call-start = ((), (), s32[]{:S(2)}) async-start(), calls=%async_computation.17 | async-start | bytes 2654208
  297.4 82.6 %reduce-scatter.21.cloned.1.call-start = ((), (), s32[]{:S(2)}) async-start(), calls=%async_computation.16 | async-start | bytes 2654208
  297.5 13.2 %copy-start.13 = (bf16[512,768]{0,1:T(8,128)(2,1)S(1)}, bf16[512,768]{0,1:T(8,128)(2,1)}, u32[]{:S(2)}) copy-start(bf16[512,768]{0,1:T(8,128)(2,1)} %copy-done.12) | copy-start | bytes 2359300
  310.7 12.8 %slice-start = ((s8[12582912]{0:T(1024)(128)(4,1)}), s8[4194304]{0:T(1024)(128)(4,1)S(1)}, s32[]{:S(2)}) async-start(s8[12582912]{0:T(1024)(128)(4,1)} %bitcast.94), calls=%async_computation.19 | async-start | bytes 8388608
  312.7 20.8 %copy-start.42 = (bf16[12,64,512]{2,1,0:T(8,128)(2,1)}, bf16[12,64,512]{2,1,0:T(8,128)(2,1)S(1)}, u32[]{:S(2)}) copy-start(bf16[12,64,512]{2,1,0:T(8,128)(2,1)S(1)} %multiply_convert_fusion.4) | copy-start | bytes 2359300
  340.2 72.8 %reduce-scatter.19.cloned.1.call-start = ((), (), s32[]{:S(2)}) async-start(), calls=%async_computation.15 | async-start | bytes 2654208
  355.7 158.6 %reduce-scatter.15.cloned.1.call-start = ((), (), s32[]{:S(2)}) async-start(), calls=%async_computation.13 | async-start | bytes 10616832 | tf_op jit(solution)/shard_map/reduce_scatter | solution.py:226
  366.6 247.7 %reduce-scatter.17.cloned.1.call-start = ((), (), s32[]{:S(2)}) async-start(), calls=%async_computation.14 | async-start | bytes 10616832 | tf_op jit(solution)/shard_map/reduce_scatter | solution.py:227
  376.5 308.6 %all-reduce.23.cloned.1.call-start = ((), (), s32[]{:S(2)}) async-start(), calls=%async_computation.18 | async-start | bytes 3833856 | tf_op jit(solution)/shard_map/psum | solution.py:239
  (64 other events, 328.6 us)
Sparse Core Ops, SparseCore 0:
  10.2 25.4 all-gather.7
  37.9 22.3 all-gather.9
  62.0 22.4 all-gather.11
  86.5 22.4 all-gather.13
  110.4 51.4 all-gather.15
  163.4 50.5 all-gather.17
  263.3 35.1 reduce-scatter.12
  300.7 35.3 reduce-scatter.22
  340.4 35.1 reduce-scatter.20
  377.7 35.3 reduce-scatter.18
  415.4 98.8 reduce-scatter.14
  516.4 97.8 reduce-scatter.16
  618.7 66.3 all-reduce.22
where the time goes:
time: 707 us; the launch traced here: 702 us
  waiting for transfers between devices  303 us (43%)
  matrix products  194 us (27%)
  blocking collectives  79.6 us (11%)
  other arithmetic  60 us (8%)
  local copies, waits for them, and re-layouts  47.5 us (7%)
  between operations  17.9 us (3%)
    reduce_scatter x1, waiting for transfers between devices, body(): lax.psum_scatter(w_inner_grad, 'shard', scatter_dimension=0, tiled=True)  99.4 us
    reduce_scatter x1, waiting for transfers between devices, body(): lax.psum_scatter(w_outer_grad, 'shard', scatter_dimension=0, tiled=True)  97.9 us
    dot_general x6, matrix products, forward_product(): return jnp.dot(rows_in, weight, preferred_element_type=jnp.float32)  60.8 us
    unnamed x2, blocking collectives  56.9 us
    all_gather x1, waiting for transfers between devices, body(): lax.all_gather(to_half(w_inner), 'shard', axis=0, tiled=True)  46.7 us
    unnamed x190, local copies, waits for them, and re-layouts  45.9 us
    dot_general x6, matrix products, back_product(): jnp.einsum('tj,ij->ti', grad_rows, weight, preferred_element_type=jnp.flo...  40 us
    dot_general x6, matrix products, weight_grad(): jnp.einsum('ti,tj->ij', left, right, preferred_element_type=jnp.float32)  32.1 us
  transfers between devices with their start and end apart: 13, of which 7 were waited for; matrix products, arithmetic and copies ran while one was open for 32% of the time, Pallas kernels for 0%

commit v1 on v0

--- a/solution.py
+++ b/solution.py
@@ -1,6 +1,9 @@
+import functools
 import jax
 import jax.numpy as jnp
 from jax import lax
+from jax.experimental import pallas as pl
+from jax.experimental.pallas import tpu as pltpu
 from jax.sharding import PartitionSpec as P
 
 HEADS = 12
@@ -8,6 +11,450 @@
 FF = 3072
 D = 768
 SEQ = 512
+MESH = pl.DeviceIdType.MESH
+BF = jnp.bfloat16
+F32 = jnp.float32
+TR = 96
+HR = 48
+
+
+def places():
+    w = lax.axis_index("width")
+    s = lax.axis_index("shard")
+    return dict(
+        w=w,
+        s=s,
+        c=lax.rem(s, 2),
+        z=lax.div(s, 2),
+        sib=s + 1 - 2 * lax.rem(s, 2),
+        xw=w + 1 - 2 * lax.rem(w, 2),
+        yw=lax.rem(w + 2, 4),
+        dw=3 - w,
+        zp=lax.rem(s + 2, 8),
+        zm=lax.rem(s + 6, 8),
+        zo=lax.rem(s + 4, 8),
+    )
+
+
+class Copies:
+    def __init__(self, send, recv):
+        self.send, self.recv, self.count, self.all = send, recv, 0, []
+
+    def start(self, src, dst, device):
+        k = self.count
+        self.count += 1
+        copy = pltpu.make_async_remote_copy(
+            src_ref=src,
+            dst_ref=dst,
+            send_sem=self.send.at[k],
+            recv_sem=self.recv.at[k],
+            device_id=device,
+            device_id_type=MESH,
+        )
+        copy.start()
+        self.all.append(copy)
+        return copy
+
+    def finish(self):
+        for copy in self.all:
+            copy.wait_send()
+
+
+def greet(devices):
+    barrier = pltpu.get_barrier_semaphore()
+    for device in devices:
+        pl.semaphore_signal(barrier, inc=1, device_id=device, device_id_type=MESH)
+    pl.semaphore_wait(barrier, len(devices))
+
+
+def partners(p):
+    out = [(p["xw"], p["s"]), (p["yw"], p["s"]), (p["dw"], p["s"])]
+    for k in range(1, 8):
+        out.append((p["w"], lax.rem(p["s"] + k, 8)))
+    return out
+
+
+GATHER_COPIES = 67
+
+
+def slot(m, full, q, s):
+    return full.at[s, q] if m == 2 else full.at[q, s]
+
+
+def slots(m, full, s):
+    return full.at[s] if m == 2 else full.at[:, s]
+
+
+def gather_kernel(wq, wk, wv, wo, wi, wr, vec, fa, fi, fo, fv, own, ssem, rsem, lsem):
+    p = places()
+    w, s = p["w"], p["s"]
+    full = (fa, fi, fo)
+    for q, ref in enumerate((wq, wk, wv, wo)):
+        own[0, q] = ref[...].astype(BF)
+    for q in range(4):
+        own[1, q] = wi[:, q * D : (q + 1) * D].astype(BF)
+        own[2, q] = wr[q * TR : (q + 1) * TR, :].astype(BF)
+    greet(partners(p))
+    cp = Copies(ssem, rsem)
+    xdev, ydev = (p["xw"], s), (p["yw"], s)
+    zpdev, zmdev, sib = (w, p["zp"]), (w, p["zm"]), (w, p["sib"])
+    got = {}
+    for m in range(3):
+        got[m, "zm"] = cp.start(own.at[m, w], slot(m, full[m], w, s), zpdev)
+        got[m, "zp"] = cp.start(own.at[m, w], slot(m, full[m], w, s), zmdev)
+        got[m, "c"] = cp.start(own.at[m], slots(m, full[m], s), sib)
+    vcopies = [
+        cp.start(vec, fv.at[s], (w, lax.rem(s + k, 8))) for k in range(1, 8)
+    ]
+    local = [pltpu.make_async_copy(own.at[m], slots(m, full[m], s), lsem.at[m]) for m in range(3)]
+    local.append(pltpu.make_async_copy(vec, fv.at[s], lsem.at[3]))
+    for copy in local:
+        copy.start()
+
+    def half(ref, top):
+        return ref.at[0:HR] if top else ref.at[HR:TR]
+
+    def to_plane(m, name):
+        tile = slot(m, full[m], w, p[name])
+        got[m, name, "x"] = cp.start(tile, tile, xdev)
+        got[m, name, "y"] = cp.start(tile, tile, ydev)
+
+    def stage1(m):
+        got[m, "zm"].wait_recv()
+        tile = half(slot(m, full[m], w, p["zm"]), True)
+        got[m, "top"] = cp.start(tile, tile, zpdev)
+        to_plane(m, "zm")
+        got[m, "zp"].wait_recv()
+        tile = half(slot(m, full[m], w, p["zp"]), False)
+        got[m, "bot"] = cp.start(tile, tile, zmdev)
+        to_plane(m, "zp")
+
+    def stage2(m):
+        got[m, "top"].wait_recv()
+        got[m, "bot"].wait_recv()
+        to_plane(m, "zo")
+
+    def stage3(m):
+        for name in ("zm", "zp", "zo"):
+            got[m, name, "x"].wait_recv()
+            tile = half(slot(m, full[m], p["xw"], p[name]), True)
+            got[m, name, "dy"] = cp.start(tile, tile, ydev)
+            got[m, name, "y"].wait_recv()
+            tile = half(slot(m, full[m], p["yw"], p[name]), False)
+            got[m, name, "dx"] = cp.start(tile, tile, xdev)
+
+    def stage4(m):
+        for name in ("zm", "zp", "zo"):
+            got[m, name, "dy"].wait_recv()
+            got[m, name, "dx"].wait_recv()
+            block = slots(m, full[m], p[name])
+            got[m, name, "c"] = cp.start(block, block, sib)
+
+    stage1(0)
+    stage1(1)
+    stage2(0)
+    stage1(2)
+    stage2(1)
+    stage3(0)
+    stage2(2)
+    stage3(1)
+    stage4(0)
+    stage3(2)
+    stage4(1)
+    stage4(2)
+    for m in range(3):
+        got[m, "c"].wait_recv()
+        for name in ("zm", "zp", "zo"):
+            got[m, name, "c"].wait_recv()
+    for copy in vcopies:
+        copy.wait_recv()
+    for copy in local:
+        copy.wait()
+    cp.finish()
+    assert cp.count == GATHER_COPIES, cp.count
+
+
+def gather_fast(wq, wk, wv, wo, wi, wr, vec):
+    vm = pl.BlockSpec(memory_space=pltpu.VMEM)
+    anyspace = pl.BlockSpec(memory_space=pl.ANY)
+    return pl.pallas_call(
+        gather_kernel,
+        out_shape=(
+            jax.ShapeDtypeStruct((4, 8, TR, D), BF),
+            jax.ShapeDtypeStruct((4, 8, TR, D), BF),
+            jax.ShapeDtypeStruct((8, 4, TR, D), BF),
+            jax.ShapeDtypeStruct((8, 16, D), BF),
+        ),
+        in_specs=[vm] * 7,
+        out_specs=(anyspace,) * 4,
+        scratch_shapes=[
+            pltpu.VMEM((3, 4, TR, D), BF),
+            pltpu.SemaphoreType.DMA((GATHER_COPIES,)),
+            pltpu.SemaphoreType.DMA((GATHER_COPIES,)),
+            pltpu.SemaphoreType.DMA((4,)),
+        ],
+        compiler_params=pltpu.CompilerParams(
+            collective_id=0, has_side_effects=True, vmem_limit_bytes=60 << 20
+        ),
+        name="gather",
+    )(wq, wk, wv, wo, wi, wr, vec)
+
+
+REDUCE_COPIES = 6 + 3 * 15 + 7
+
+
+def reduce_kernel(
+    gq, gk, gv, go, gi, gr, gvec,
+    oq, ok, ov, oo, oi, our, ovec,
+    held, landed, dx, dy, rx, ry, qz, dzp, dzm, rzp, rzm, outb,
+    vheld, vrecv, vplane, vz,
+    ssem, rsem, lsem,
+):
+    p = places()
+    w, s, c, z = p["w"], p["s"], p["c"], p["z"]
+    greet(partners(p))
+    cp = Copies(ssem, rsem)
+    xdev, ydev, ddev = (p["xw"], s), (p["yw"], s), (p["dw"], s)
+    zpdev, zmdev, sib = (w, p["zp"]), (w, p["zm"]), (w, p["sib"])
+    zp, zm, zo = lax.rem(z + 1, 4), lax.rem(z + 3, 4), lax.rem(z + 2, 4)
+    got = {}
+    local = {}
+
+    def half_of(m, core):
+        if m == 0:
+            return [(g.at[:, core], (0, q)) for q, g in enumerate((gq, gk, gv, go))]
+        if m == 1:
+            return [(gi.at[:, :, core], (1,))]
+        return [(gr.at[:, core], (2,))]
+
+    count = 0
+    order = (2, 1, 0)
+    got["v", "c"] = cp.start(gvec.at[:, 1 - c], vrecv, sib)
+    for m in order:
+        got[m, "c"] = []
+        local[m] = []
+        for src, at in half_of(m, 1 - c):
+            got[m, "c"].append(cp.start(src, landed.at[at], sib))
+        for src, at in half_of(m, c):
+            copy = pltpu.make_async_copy(src, held.at[at], lsem.at[count])
+            copy.start()
+            local[m].append(copy)
+            count += 1
+
+    def quarter(m, q, rows=slice(None)):
+        return (m, slice(None), q, rows) if m == 2 else (m, q, slice(None), rows)
+
+    TOP, BOT = slice(0, HR), slice(HR, TR)
+
+    def add_pair(m):
+        for copy in local[m]:
+            copy.wait()
+        for copy in got[m, "c"]:
+            copy.wait_recv()
+
+        def one(i, _):
+            for j in range(4):
+                held[m, i, j] = (held[m, i, j].astype(F32) + landed[m, i, j].astype(F32)).astype(BF)
+            return 0
+
+        lax.fori_loop(0, 4, one, 0)
+
+    def plane1(m):
+        got[m, "dx"] = cp.start(held.at[quarter(m, p["dw"], TOP)], dx.at[m], xdev)
+        got[m, "dy"] = cp.start(held.at[quarter(m, p["dw"], BOT)], dy.at[m], ydev)
+        got[m, "x1"] = cp.start(held.at[quarter(m, p["xw"], TOP)], rx.at[m, :, TOP], xdev)
+        got[m, "y1"] = cp.start(held.at[quarter(m, p["yw"], BOT)], ry.at[m, :, BOT], ydev)
+
+    def plane2(m):
+        got[m, "dx"].wait_recv()
+        at = quarter(m, p["yw"], TOP)
+        held[at] = (held[at].astype(F32) + dx[m].astype(F32)).astype(BF)
+        got[m, "y2"] = cp.start(held.at[at], ry.at[m, :, TOP], ydev)
+        got[m, "dy"].wait_recv()
+        at = quarter(m, p["xw"], BOT)
+        held[at] = (held[at].astype(F32) + dy[m].astype(F32)).astype(BF)
+        got[m, "x2"] = cp.start(held.at[at], rx.at[m, :, BOT], xdev)
+
+    def plane3(m):
+        for name in ("x1", "y1", "x2", "y2"):
+            got[m, name].wait_recv()
+        qz[m] = (held[quarter(m, w)].astype(F32) + rx[m].astype(F32) + ry[m].astype(F32)).astype(BF)
+
+    def ring1(m):
+        got[m, "dzp"] = cp.start(qz.at[m, zo, TOP], dzp.at[m], zpdev)
+        got[m, "dzm"] = cp.start(qz.at[m, zo, BOT], dzm.at[m], zmdev)
+        got[m, "p1"] = cp.start(qz.at[m, zp, BOT], rzp.at[m, BOT], zpdev)
+        got[m, "m1"] = cp.start(qz.at[m, zm, TOP], rzm.at[m, TOP], zmdev)
+
+    def ring2(m):
+        got[m, "dzp"].wait_recv()
+        qz[m, zp, TOP] = (qz[m, zp, TOP].astype(F32) + dzp[m].astype(F32)).astype(BF)
+        got[m, "p2"] = cp.start(qz.at[m, zp, TOP], rzp.at[m, TOP], zpdev)
+        got[m, "dzm"].wait_recv()
+        qz[m, zm, BOT] = (qz[m, zm, BOT].astype(F32) + dzm[m].astype(F32)).astype(BF)
+        got[m, "m2"] = cp.start(qz.at[m, zm, BOT], rzm.at[m, BOT], zmdev)
+
+    def ring3(m):
+        for name in ("p1", "m1", "p2", "m2"):
+            got[m, name].wait_recv()
+        outb[m, w] = (qz[m, z].astype(F32) + rzp[m].astype(F32) + rzm[m].astype(F32)).astype(BF)
+        tile = outb.at[m, w]
+        got[m, "gx"] = cp.start(tile, tile, xdev)
+        got[m, "gy"] = cp.start(tile, tile, ydev)
+        got[m, "gd"] = cp.start(tile, tile, ddev)
+
+    def last(m):
+        for name in ("gx", "gy", "gd"):
+            got[m, name].wait_recv()
+        if m == 0:
+            for q, ref in enumerate((oq, ok, ov, oo)):
+                ref[...] = outb[0, q].astype(F32)
+        for q in range(4):
+            if m == 1:
+                oi[:, q * D : (q + 1) * D] = outb[1, q].astype(F32)
+            if m == 2:
+                our[q * TR : (q + 1) * TR, :] = outb[2, q].astype(F32)
+
+    def vec_plane():
+        got["v", "c"].wait_recv()
+        vheld[...] = gvec[:, c] + vrecv[...]
+        vplane[w] = vheld[...]
+        got["v", "plane"] = [cp.start(vheld, vplane.at[w], d) for d in (xdev, ydev, ddev)]
+
+    def vec_ring():
+        for copy in got["v", "plane"]:
+            copy.wait_recv()
+        vheld2 = (vplane[0] + vplane[1]) + (vplane[2] + vplane[3])
+        vheld[...] = vheld2
+        vz[z] = vheld[z]
+        got["v", "z"] = [
+            cp.start(vheld.at[t], vz.at[z], (w, 2 * t + c)) for t in (zp, zm, zo)
+        ]
+
+    def vec_last():
+        for copy in got["v", "z"]:
+            copy.wait_recv()
+        ovec[...] = (vz[0] + vz[1]) + (vz[2] + vz[3])
+
+    a, b, d = order
+    add_pair(a)
+    plane1(a)
+    add_pair(b)
+    plane1(b)
+    add_pair(d)
+    plane1(d)
+    vec_plane()
+    plane2(a)
+    plane2(b)
+    plane3(a)
+    ring1(a)
+    plane2(d)
+    plane3(b)
+    ring1(b)
+    ring2(a)
+    for copy in got["v", "plane"]:
+        copy.wait_send()
+    cp.all = [copy for copy in cp.all if all(copy is not other for other in got["v", "plane"])]
+    vec_ring()
+    plane3(d)
+    ring1(d)
+    ring3(a)
+    ring2(b)
+    ring3(b)
+    ring2(d)
+    last(a)
+    ring3(d)
+    last(b)
+    vec_last()
+    last(d)
+    cp.finish()
+    assert cp.count == REDUCE_COPIES, cp.count
+
+
+def reduce_fast(gq, gk, gv, go, gi, gr, gvec):
+    vm = pl.BlockSpec(memory_space=pltpu.VMEM)
+    anyspace = pl.BlockSpec(memory_space=pl.ANY)
+    square = (4, 2, TR, D)
+    return pl.pallas_call(
+        reduce_kernel,
+        out_shape=tuple(jax.ShapeDtypeStruct((TR, D), F32) for _ in range(4))
+        + (
+            jax.ShapeDtypeStruct((TR, FF), F32),
+            jax.ShapeDtypeStruct((FF // 8, D), F32),
+            jax.ShapeDtypeStruct((8, D), F32),
+        ),
+        in_specs=[anyspace] * 6 + [vm],
+        out_specs=(vm,) * 7,
+        scratch_shapes=[
+            pltpu.VMEM((3, 4, 4, TR, D), BF),
+            pltpu.VMEM((3, 4, 4, TR, D), BF),
+            pltpu.VMEM((3, 4, HR, D), BF),
+            pltpu.VMEM((3, 4, HR, D), BF),
+            pltpu.VMEM((3, 4, TR, D), BF),
+            pltpu.VMEM((3, 4, TR, D), BF),
+            pltpu.VMEM((3, 4, TR, D), BF),
+            pltpu.VMEM((3, HR, D), BF),
+            pltpu.VMEM((3, HR, D), BF),
+            pltpu.VMEM((3, TR, D), BF),
+            pltpu.VMEM((3, TR, D), BF),
+            pltpu.VMEM((3, 4, TR, D), BF),
+            pltpu.VMEM((4, 8, D), F32),
+            pltpu.VMEM((4, 8, D), F32),
+            pltpu.VMEM((4, 4, 8, D), F32),
+            pltpu.VMEM((4, 8, D), F32),
+            pltpu.SemaphoreType.DMA((REDUCE_COPIES,)),
+            pltpu.SemaphoreType.DMA((REDUCE_COPIES,)),
+            pltpu.SemaphoreType.DMA((6,)),
+        ],
+        compiler_params=pltpu.CompilerParams(
+            collective_id=1, has_side_effects=True, vmem_limit_bytes=60 << 20
+        ),
+        name="reduce",
+    )(
+        gq.reshape(square), gk.reshape(square), gv.reshape(square), go.reshape(square),
+        gi.reshape((4,) + square), gr.reshape((4, 2, 4, TR, D)), gvec.reshape((4, 2, 8, D)),
+    )
+
+def kernels_fit():
+    return lax.axis_size("width") == 4 and lax.axis_size("shard") == 8
+
+
+def gather(wq, wk, wv, wo, wi, wr, eight, b_inner):
+    if kernels_fit():
+        vec = jnp.pad(
+            jnp.stack([jnp.concatenate(eight), jnp.pad(b_inner, (0, D - FF // 8))]), ((0, 14), (0, 0))
+        ).astype(BF)
+        fa, fi, fo, fv = gather_fast(wq, wk, wv, wo, wi, wr, vec)
+        fa, fi, fo = fa.reshape(4, D, D), fi.reshape(4, D, D), fo.reshape(FF, D)
+        rows = fv[:, 0].reshape(8, 8, TR).astype(F32)
+        vectors = tuple(rows[:, k].reshape(D) for k in range(8))
+        return (*(fa[q] for q in range(4)), fi, fo, vectors, fv[:, 1, : FF // 8].reshape(FF).astype(F32))
+
+    def whole(a):
+        return lax.all_gather(a.astype(BF), "shard", axis=0, tiled=True)
+
+    fi = whole(wi)
+    fi = jnp.stack([fi[:, q * D : (q + 1) * D] for q in range(4)])
+    vectors = tuple(whole(a).astype(F32) for a in eight)
+    return (whole(wq), whole(wk), whole(wv), whole(wo), fi, whole(wr), vectors, whole(b_inner).astype(F32))
+
+
+def reduce(gq, gk, gv, go, gi, gr, eight, b_inner):
+    if kernels_fit():
+        first = jnp.stack([a.reshape(8, TR) for a in eight], axis=1).reshape(8, 1, D)
+        second = jnp.pad(b_inner.reshape(8, 1, FF // 8), ((0, 0), (0, 0), (0, D - FF // 8)))
+        vec = jnp.pad(jnp.concatenate([first, second], axis=1), ((0, 0), (0, 6), (0, 0)))
+        *matrices, ovec = reduce_fast(gq, gk, gv, go, gi, gr, vec)
+        vectors = tuple(ovec[0, k * TR : (k + 1) * TR] for k in range(8))
+        return matrices, vectors, ovec[1, : FF // 8]
+
+    def owned(a):
+        a = lax.psum_scatter(a, "shard", scatter_dimension=0, tiled=True)
+        return lax.psum(a.astype(BF), "width").astype(F32)
+
+    gi = jnp.concatenate([gi[q] for q in range(4)], axis=1)
+    matrices = tuple(owned(a.astype(F32)) for a in (gq, gk, gv, go, gi, gr))
+    return matrices, tuple(owned(a) for a in eight), owned(b_inner)
 
 
 def to_half(value):
@@ -77,28 +524,9 @@
     kept_heads = group_heads[0]
     head_mask = (jnp.arange(D) // HEAD_DIM < kept_heads).astype(jnp.float32)
     unit_mask = (jnp.arange(FF) // (FF // HEADS) < kept_heads).astype(jnp.float32)
-    attn_full = (
-        lax.all_gather(to_half(w_query), "shard", axis=0, tiled=True),
-        lax.all_gather(to_half(w_key), "shard", axis=0, tiled=True),
-        lax.all_gather(to_half(w_value), "shard", axis=0, tiled=True),
-        lax.all_gather(to_half(w_out), "shard", axis=0, tiled=True),
-        lax.all_gather(to_half(b_query), "shard", axis=0, tiled=True),
-        lax.all_gather(to_half(b_value), "shard", axis=0, tiled=True),
-        lax.all_gather(to_half(b_out), "shard", axis=0, tiled=True),
-        lax.all_gather(to_half(gain_one), "shard", axis=0, tiled=True),
-        lax.all_gather(to_half(shift_one), "shard", axis=0, tiled=True),
-    )
-    full_query, full_key, full_value, full_out = (
-        attn_full[0],
-        attn_full[1],
-        attn_full[2],
-        attn_full[3],
-    )
-    bias_query = attn_full[4].astype(jnp.float32)
-    bias_value = attn_full[5].astype(jnp.float32)
-    bias_out = attn_full[6].astype(jnp.float32)
-    gain_first = attn_full[7].astype(jnp.float32)
-    shift_first = attn_full[8].astype(jnp.float32)
+    gathered = gather(w_query, w_key, w_value, w_out, w_inner, w_outer, (b_query, b_value, b_out, gain_one, shift_one, b_outer, gain_two, shift_two), b_inner)
+    full_query, full_key, full_value, full_out, full_inner, full_outer, vectors, bias_inner = gathered
+    bias_query, bias_value, bias_out, gain_first, shift_first, bias_outer, gain_second, shift_second = vectors
     queries = to_half(forward_product(layer_input, full_query) + bias_query)
     keys = to_half(forward_product(layer_input, full_key))
     values = to_half(forward_product(layer_input, full_value) + bias_value)
@@ -126,20 +554,7 @@
     normed_one, inverse_one = norm_parts(layer_input.astype(jnp.float32) + branch)
     hidden = normed_one * gain_first + shift_first
     hidden_low = to_half(hidden)
-    ffn_full = (
-        lax.all_gather(to_half(w_inner), "shard", axis=0, tiled=True),
-        lax.all_gather(to_half(w_outer), "shard", axis=0, tiled=True),
-        lax.all_gather(to_half(b_inner), "shard", axis=0, tiled=True),
-        lax.all_gather(to_half(b_outer), "shard", axis=0, tiled=True),
-        lax.all_gather(to_half(gain_two), "shard", axis=0, tiled=True),
-        lax.all_gather(to_half(shift_two), "shard", axis=0, tiled=True),
-    )
-    full_inner, full_outer = (ffn_full[0], ffn_full[1])
-    bias_inner = ffn_full[2].astype(jnp.float32)
-    bias_outer = ffn_full[3].astype(jnp.float32)
-    gain_second = ffn_full[4].astype(jnp.float32)
-    shift_second = ffn_full[5].astype(jnp.float32)
-    inner = forward_product(hidden_low, full_inner) + bias_inner
+    inner = jnp.concatenate([forward_product(hidden_low, full_inner[q]) for q in range(4)], axis=1) + bias_inner
 
     def gelu_exact(value):
         return jax.nn.gelu(value, approximate=False)
@@ -159,8 +574,8 @@
     active_grad = back_product(outer_grad, full_outer)
     inner_grad = to_half(gelu_pull(active_grad * unit_mask)[0])
     b_inner_grad = column_sum(inner_grad)
-    w_inner_grad = weight_grad(hidden_low, inner_grad)
-    hidden_grad = res_two_grad + back_product(inner_grad, full_inner)
+    w_inner_grad = jnp.stack([to_half(weight_grad(hidden_low, inner_grad[:, q * D : (q + 1) * D])) for q in range(4)])
+    hidden_grad = res_two_grad + sum(back_product(inner_grad[:, q * D : (q + 1) * D], full_inner[q]) for q in range(4))
     shift_one_grad = jnp.sum(hidden_grad, axis=0)
     gain_one_grad = jnp.sum(hidden_grad * normed_one, axis=0)
     res_one_grad = norm_back(hidden_grad * gain_first, normed_one, inverse_one)
@@ -218,52 +633,9 @@
         + back_product(key_grad, full_key)
         + back_product(value_grad, full_value)
     )
-    owned = (
-        lax.psum_scatter(w_query_grad, "shard", scatter_dimension=0, tiled=True),
-        lax.psum_scatter(w_key_grad, "shard", scatter_dimension=0, tiled=True),
-        lax.psum_scatter(w_value_grad, "shard", scatter_dimension=0, tiled=True),
-        lax.psum_scatter(w_out_grad, "shard", scatter_dimension=0, tiled=True),
-        lax.psum_scatter(w_inner_grad, "shard", scatter_dimension=0, tiled=True),
-        lax.psum_scatter(w_outer_grad, "shard", scatter_dimension=0, tiled=True),
-        lax.psum_scatter(b_query_grad, "shard", scatter_dimension=0, tiled=True),
-        lax.psum_scatter(b_value_grad, "shard", scatter_dimension=0, tiled=True),
-        lax.psum_scatter(b_out_grad, "shard", scatter_dimension=0, tiled=True),
-        lax.psum_scatter(gain_one_grad, "shard", scatter_dimension=0, tiled=True),
-        lax.psum_scatter(shift_one_grad, "shard", scatter_dimension=0, tiled=True),
-        lax.psum_scatter(b_inner_grad, "shard", scatter_dimension=0, tiled=True),
-        lax.psum_scatter(b_outer_grad, "shard", scatter_dimension=0, tiled=True),
-        lax.psum_scatter(gain_two_grad, "shard", scatter_dimension=0, tiled=True),
-        lax.psum_scatter(shift_two_grad, "shard", scatter_dimension=0, tiled=True),
-    )
-    summed = (
-        lax.psum(owned[0].astype(jnp.bfloat16), "width").astype(jnp.float32),
-        lax.psum(owned[1].astype(jnp.bfloat16), "width").astype(jnp.float32),
-        lax.psum(owned[2].astype(jnp.bfloat16), "width").astype(jnp.float32),
-        lax.psum(owned[3].astype(jnp.bfloat16), "width").astype(jnp.float32),
-        lax.psum(owned[4].astype(jnp.bfloat16), "width").astype(jnp.float32),
-        lax.psum(owned[5].astype(jnp.bfloat16), "width").astype(jnp.float32),
-        lax.psum(owned[6].astype(jnp.bfloat16), "width").astype(jnp.float32),
-        lax.psum(owned[7].astype(jnp.bfloat16), "width").astype(jnp.float32),
-        lax.psum(owned[8].astype(jnp.bfloat16), "width").astype(jnp.float32),
-        lax.psum(owned[9].astype(jnp.bfloat16), "width").astype(jnp.float32),
-        lax.psum(owned[10].astype(jnp.bfloat16), "width").astype(jnp.float32),
-        lax.psum(owned[11].astype(jnp.bfloat16), "width").astype(jnp.float32),
-        lax.psum(owned[12].astype(jnp.bfloat16), "width").astype(jnp.float32),
-        lax.psum(owned[13].astype(jnp.bfloat16), "width").astype(jnp.float32),
-        lax.psum(owned[14].astype(jnp.bfloat16), "width").astype(jnp.float32),
-    )
-    matrices = (summed[0], summed[1], summed[2], summed[3], summed[4], summed[5])
-    vectors = (
-        summed[6],
-        summed[7],
-        summed[8],
-        summed[9],
-        summed[10],
-        summed[11],
-        summed[12],
-        summed[13],
-        summed[14],
-    )
+    matrices, vectors, b_inner_grad = reduce(
+        to_half(w_query_grad), to_half(w_key_grad), to_half(w_value_grad), to_half(w_out_grad), w_inner_grad, to_half(w_outer_grad),
+        (b_query_grad, b_value_grad, b_out_grad, gain_one_grad, shift_one_grad, b_outer_grad, gain_two_grad, shift_two_grad), b_inner_grad)
     return (
         layer_output,
         input_grad,
@@ -277,11 +649,11 @@
         vectors[3],
         vectors[4],
         matrices[4],
+        b_inner_grad,
+        matrices[5],
         vectors[5],
-        matrices[5],
         vectors[6],
         vectors[7],
-        vectors[8],
     )
 
 

time: 707 us -> 465 us (0.66)
  waiting for transfers between devices: 303 us -> 0 us
  Pallas kernels: 0 us -> 177 us
  blocking collectives: 79.6 us -> 0 us
  matrix products: 194 us -> 149 us
  other arithmetic: 60 us -> 87.3 us
  between operations: 17.9 us -> 2.63 us
    reduce_scatter x3 -> x0, waiting for transfers between devices: 197 us -> none  [the longest x1 99.4 us: body(): lax.psum_scatter(w_inner_grad, 'shard', scatter_dimension=0, tiled=True)]
    pallas_call x0 -> x2, Pallas kernels: none -> 177 us  [the longest x1 107 us: reduce_fast(): pl.pallas_call(reduce_kernel, out_shape=tuple((jax.ShapeDtypeStruct((TR,...]
    all_gather x6 -> x0, waiting for transfers between devices: 65.4 us -> none  [the longest x1 46.7 us: body(): lax.all_gather(to_half(w_inner), 'shard', axis=0, tiled=True)]
    unnamed x2 -> x0, blocking collectives: 56.9 us -> none
    dot_general x6 -> x9, matrix products: 60.8 us -> 24.6 us  [forward_product(): return jnp.dot(rows_in, weight, preferred_element_type=jnp.float32)]
    unnamed x16 -> x0, waiting for transfers between devices: 31.4 us -> none
    convert_element_type x18 -> x4, other arithmetic: 27.5 us -> 57.3 us  [to_half(): return value.astype(jnp.bfloat16)]
    convert_element_type x24 -> x2, other arithmetic: 17.3 us -> 1.84 us  [the longest x1 0.96 us: gather(): rows = fv[:, 0].reshape(8, 8, TR).astype(F32)]
  transfers between devices with their start and end apart: 13 -> 0, of which waited for: 7 -> 0; matrix products, arithmetic and copies ran while one was open for 32% -> 0% of each run, Pallas kernels for 0% -> 0%
where the time goes in v1:
time: 465 us; the launch traced here: 462 us
  Pallas kernels  177 us (38%)
  matrix products  149 us (32%)
  other arithmetic  87.3 us (19%)
  local copies, waits for them, and re-layouts  46.1 us (10%)
    pallas_call x1, Pallas kernels, reduce_fast(): pl.pallas_call(reduce_kernel, out_shape=tuple((jax.ShapeDtypeStruct((TR,...  107 us
    pallas_call x1, Pallas kernels, gather_fast(): pl.pallas_call(gather_kernel, out_shape=(jax.ShapeDtypeStruct((4, 8, TR,...  69.8 us
    convert_element_type x4, other arithmetic, to_half(): return value.astype(jnp.bfloat16)  57.3 us
    dot_general x9, matrix products, back_product(): jnp.einsum('tj,ij->ti', grad_rows, weight, preferred_element_type=jnp.flo...  42.4 us
    unnamed x168, local copies, waits for them, and re-layouts  30.6 us
    dot_general x9, matrix products, weight_grad(): jnp.einsum('ti,tj->ij', left, right, preferred_element_type=jnp.float32)  28.5 us
    dot_general x9, matrix products, forward_product(): return jnp.dot(rows_in, weight, preferred_element_type=jnp.float32)  24.6 us
    dot_general x2, matrix products, body(): jnp.einsum('qhd,khd->hqk', grad_row, value_row, preferred_element_type=jn...  17.9 us

profile of v1, /device:TPU:0, one launch (start us, length us, event | category | flops | bytes accessed | tf_op | source)
XLA Modules:
  0.0 461.8 jit_solution(6794753804974296640)
XLA Ops:
  15.0 69.8 %gather.1 = (bf16[4,8,96,768]{3,2,1,0:T(8,128)(2,1)}, bf16[4,8,96,768]{3,2,1,0:T(8,128)(2,1)}, bf16[8,4,96,768]{3,2,1,0:T(8,128)(2,1)}, bf16[8,16,768]{2,1,0:T(8,128)(2,1)}) custom-call(f32[96,768]{1,0:T(8,128)} %wq.1, f32[96,768]{1,0:T(8,128)} %wk.1, f32[96,768]{1,0:T(8,128)} %wv.1, f32[96,768]{1,0:T(8,128)} %wo.1, f32[96,3072]{1,0:T(8,128)} %wi.1, ...), custom_call_target="tpu_custom_call" | custom-call | tf_op jit(solution)/shard_map/gather/pallas_call | solution.py:180
  84.7 6.8 %fusion.88 = (bf16[1,8,96,768]{3,2,1,0:T(8,128)(2,1)}, bf16[1,8,96,768]{3,2,1,0:T(8,128)(2,1)}, bf16[1,8,96,768]{3,2,1,0:T(8,128)(2,1)}, bf16[1,8,96,768]{3,2,1,...) fusion(bf16[4,8,96,768]{3,2,1,0:T(8,128)(2,1)} %get-tuple-eleme, ...), kind=kLoop, calls=%fused_computation.187 | loop fusion | bytes 18874368 | tf_op jit(solution)/shard_map/slice | solution.py:557
  110.7 4.9 %fusion.17 = f32[12,64,512]{2,1,0:T(8,128)} fusion(bf16[512,12,64]{0,2,1:T(8,128)(2,1)S(1)} %bitcast.169, f32[12,512]{1,0:T(8,128)S(1)} %fusion.7, f32[12,512]{1,0:T(8,128)S(1)} %get-tuple-element.105, f32[12,512,512]{1,2,0:T(8,128)S(1)} %get-tuple-element.106, pred[512,512]{0,1:T(8,128)(4,1)S(1)} %broadcast_compare_fusion), kind=kOutput, calls=%fused_computation.40 | convolution fusion | flops 418381824 | bytes 15253504 | tf_op jit(solution)/shard_map/hqk,khd->qhd/dot_general | solution.py:547
  122.3 4.1 fusion.16
  139.1 38.8 %multiply_convert_fusion.2 = (bf16[1024,3072]{0,1:T(8,128)(2,1)S(1)}, f32[1024,3072]{0,1:T(8,128)}) fusion(f32[3072]{0:T(1024)S(1)} %fusion.61, f32[3072]{0:T(1024)S(1)} %bitcast.210, f32[1024,768]{0,1:T(8,128)S(1)} %fusion.100, f32[1024,768]{0,1:T(8,128)S(1)} %fusion.99, f32[1024,768]{0,1:T(8,128)S(1)} %fusion.98, f32[1024,768]{0,1:T(8,128)} %fusion.97), kind=kLoop, calls=%fused_computation.11 | loop fusion | flops 220200960 | bytes 31481856 | tf_op jit(solution)/shard_map/convert_element_type | solution.py:461
  177.9 9.4 %fusion.96 = (f32[1024]{0:T(1024)S(1)}, f32[1024,768]{0,1:T(8,128)S(1)}) fusion(f32[768]{0:T(1024)S(1)} %add.166, bf16[1024,3072]{0,1:T(8,128)(2,1)S(1)} %get-tuple-element.76, bf16[3072,768]{1,0:T(8,128)(2,1)} %bitcast.215, f32[768]{0:T(1024)S(1)} %add.161, f32[768]{0:T(1024)S(1)} %mul.205, f32[1024]{0:T(1024)S(1)} %add_rsqrt_fusion.1, ...), kind=kOutput, calls=%fused_computation.195 | convolution fusion | flops 4837342208 | bytes 17323008 | tf_op jit(solution)/shard_map/dot_general | solution.py:499
  192.6 4.3 convert_reduce_fusion.2
  196.8 18.4 %convert_reduce_fusion = (f32[3072]{0:T(1024)S(1)}, bf16[1024,3072]{0,1:T(8,128)(2,1)}) fusion(f32[1024,3072]{0,1:T(8,128)} %get-tuple-element.77, f32[3072]{0:T(1024)S(1)} %fusion.61, bf16[3072,768]{1,0:T(8,128)(2,1)} %bitcast.216, bf16[1024,768]{0,1:T(8,128)(2,1)S(1)} %get-tuple-element.73, f32[3072]{0:T(1024)S(1)} %bitcast.211, ...), kind=kOutput, calls=%fused_computation.3 | convolution fusion | flops 4897895424 | bytes 37785600 | tf_op jit(solution)/shard_map/tj,ij->ti/dot_general | solution.py:495
  215.3 7.0 %convolution_convert_fusion = bf16[3072,768]{1,0:T(8,128)(2,1)} fusion(bf16[1024,3072]{0,1:T(8,128)(2,1)S(1)} %bitcast.163, bf16[1024,768]{0,1:T(8,128)(2,1)S(1)} %get-tuple-element.73), kind=kOutput, calls=%fused_computation.41 | convolution fusion | flops 4834197504 | bytes 12582912 | tf_op jit(solution)/shard_map/ti,tj->ij/dot_general | solution.py:491
  222.4 3.5 convolution_convert_fusion.5
  236.1 3.3 fusion.42
  245.1 5.1 %multiply_reduce_fusion.2 = (f32[768]{0:T(1024)S(1)}, f32[1024]{0:T(1024)S(1)}, f32[1024]{0:T(1024)S(1)}, f32[768]{0:T(1024)S(1)}, f32[1024,768]{0,1:T(8,128)}) fusion(f32[1024,768]{0,1:T(8,128)S(1)} %get-tuple-element.110, f32[1024]{0:T(1024)S(1)} %add_rsqrt_fusion.1, f32[1024]{0:T(1024)S(1)} %broadcast_multiply_fusion.5, f32[768]{0:T(1024)S(1)} %mul.205, ...), kind=kOutput, calls=%fused_computation.58 | convolution fusion | flops 1224471040 | bytes 23246848 | tf_op jit(solution)/shard_map/tj,ij->ti/dot_general | solution.py:495
  256.2 3.4 fusion.29
  259.8 6.5 %fusion.36 = bf16[12,64,512]{2,1,0:T(8,128)(2,1)S(1)} fusion(bf16[512,12,64]{0,2,1:T(8,128)(2,1)S(1)} %bitcast.173, f32[12,512]{1,0:T(8,128)S(1)} %copy-done.57, f32[12,512,512]{1,2,0:T(8,128)} %copy-done, pred[512,512]{0,1:T(8,128)(4,1)S(1)} %copy-done.17), kind=kOutput, calls=%fused_computation.100 | convolution fusion | flops 415629312 | bytes 14442496 | tf_op jit(solution)/shard_map/hqk,qhd->khd/dot_general | solution.py:601
  271.1 4.4 convolution_convert_fusion.8
  275.5 11.0 %multiply_reduce_fusion.1 = (f32[12,512]{1,0:T(8,128)S(1)}, f32[12,512,512]{1,2,0:T(8,128)}) fusion(f32[12,512]{1,0:T(8,128)S(1)} %copy-done.58, f32[12,512,512]{1,2,0:T(8,128)} %copy-done.1, pred[512,512]{0,1:T(8,128)(4,1)S(1)} %broadcast_compare_fusion.1, bf16[512,12,64]{0,2,1:T(8,128)(2,1)S(1)} %bitcast.176, bf16[512,12,64]{0,2,1:T(8,128)(2,1)S(1)} %bitcast.172), kind=kOutput, calls=%fused_computation.8 | convolution fusion | flops 418375680 | bytes 27049984 | tf_op jit(solution)/shard_map/qhd,khd->hqk/dot_general | solution.py:597
  288.2 10.9 %multiply_convert_fusion.1 = bf16[12,512,512]{1,2,0:T(8,128)(2,1)} fusion(f32[12,512,512]{1,2,0:T(8,128)} %get-tuple-element.117, f32[12,512]{1,0:T(8,128)S(1)} %get-tuple-element.116, f32[12,512]{1,0:T(8,128)S(1)} %copy-done.58, f32[12,512,512]{1,2,0:T(8,128)S(1)} %bitcast.147, pred[512,512]{0,1:T(8,128)(4,1)S(1)} %broadcast_compare_fusion.1), kind=kLoop, calls=%fused_computation.7 | loop fusion | flops 18874368 | bytes 31768576 | tf_op jit(solution)/shard_map/convert_element_type | solution.py:461
  299.1 4.9 %multiply_convert_fusion.4 = bf16[12,64,512]{2,1,0:T(8,128)(2,1)S(1)} fusion(bf16[512,12,64]{0,2,1:T(8,128)(2,1)S(1)} %bitcast.155, bf16[12,512,512]{1,2,0:T(8,128)(2,1)} %multiply_convert_fusion.1), kind=kOutput, calls=%fused_computation.84 | convolution fusion | flops 403439616 | bytes 7864320 | tf_op jit(solution)/shard_map/hqk,qhd->khd/dot_general | solution.py:616
  304.1 4.0 multiply_convert_fusion.6
  308.1 6.9 %multiply_reduce_fusion = (f32[12,512]{1,0:T(8,128)S(1)}, f32[12,512,512]{1,2,0:T(8,128)}) fusion(f32[12,512]{1,0:T(8,128)S(1)} %copy-done.57, f32[12,512,512]{1,2,0:T(8,128)S(1)} %bitcast.143, pred[512,512]{0,1:T(8,128)(4,1)S(1)} %copy-done.17, bf16[512,12,64]{0,2,1:T(8,128)(2,1)S(1)} %bitcast.174, bf16[512,12,64]{0,2,1:T(8,128)(2,1)S(1)} %bitcast.170), kind=kOutput, calls=%fused_computation.5 | convolution fusion | flops 418375680 | bytes 27049984 | tf_op jit(solution)/shard_map/qhd,khd->hqk/dot_general | solution.py:597
  315.0 7.0 %multiply_convert_fusion = bf16[12,512,512]{1,2,0:T(8,128)(2,1)S(1)} fusion(f32[12,512,512]{1,2,0:T(8,128)} %get-tuple-element.115, f32[12,512]{1,0:T(8,128)S(1)} %get-tuple-element.114, f32[12,512]{1,0:T(8,128)S(1)} %copy-done.57, f32[12,512,512]{1,2,0:T(8,128)S(1)} %bitcast.143, pred[512,512]{0,1:T(8,128)(4,1)S(1)} %copy-done.17), kind=kLoop, calls=%fused_computation.4 | loop fusion | flops 18874368 | bytes 31768576 | tf_op jit(solution)/shard_map/convert_element_type | solution.py:461
  327.4 4.2 convolution_convert_fusion.9
  337.2 106.9 %reduce.37 = (f32[96,768]{1,0:T(8,128)}, f32[96,768]{1,0:T(8,128)}, f32[96,768]{1,0:T(8,128)}, f32[96,768]{1,0:T(8,128)}, f32[96,3072]{1,0:T(8,128)}, /*index=5*/f32[384,768]{1,0:T(8,128)}, f32[8,768]{1,0:T(8,128)}) custom-call(bf16[4,2,96,768]{3,2,1,0:T(8,128)(2,1)} %bitcast.198, bf16[4,2,96,768]{3,2,1,0:T(8,128)(2,1)} %bitcast.197, ...), custom_call_target="tpu_custom_call" | custom-call | tf_op jit(solution)/shard_map/reduce/pallas_call | solution.py:378
  449.5 3.5 add_convert_fusion.1
  (264 shorter events, 110.1 us)
Async XLA Ops:
  9.6 100.6 %copy-start.16 = (pred[512,512]{0,1:T(8,128)(4,1)}, pred[512,512]{0,1:T(8,128)(4,1)S(1)}, u32[]{:S(2)}) copy-start(pred[512,512]{0,1:T(8,128)(4,1)S(1)} %broadcast_compare_fusion) | copy-start | bytes 786436
  91.6 6.9 %copy-start.40 = (bf16[1,8,96,768]{3,2,1,0:T(8,128)(2,1)}, bf16[1,8,96,768]{3,2,1,0:T(8,128)(2,1)S(1)}, u32[]{:S(2)}) copy-start(bf16[1,8,96,768]{3,2,1,0:T(8,128)(2,1)S(1)} %get-tuple-element.121) | copy-start | bytes 3538948
  100.8 14.8 %copy-start.14 = (bf16[512,768]{0,1:T(8,128)(2,1)}, bf16[512,768]{0,1:T(8,128)(2,1)S(1)}, u32[]{:S(2)}) copy-start(bf16[512,768]{0,1:T(8,128)(2,1)S(1)} %get-tuple-element.91) | copy-start | bytes 2359300
  104.0 11.6 %copy-start.10 = (bf16[512,768]{0,1:T(8,128)(2,1)}, bf16[512,768]{0,1:T(8,128)(2,1)S(1)}, u32[]{:S(2)}) copy-start(bf16[512,768]{0,1:T(8,128)(2,1)S(1)} %get-tuple-element.89) | copy-start | bytes 2359300
  131.7 7.4 %copy-start.31 = (f32[1024,768]{0,1:T(8,128)}, f32[1024,768]{0,1:T(8,128)S(1)}, u32[]{:S(2)}) copy-start(f32[1024,768]{0,1:T(8,128)S(1)} %fusion.100) | copy-start | bytes 9437188
  177.9 9.4 %copy-start.18 = (bf16[1024,3072]{0,1:T(8,128)(2,1)}, bf16[1024,3072]{0,1:T(8,128)(2,1)S(1)}, u32[]{:S(2)}) copy-start(bf16[1024,3072]{0,1:T(8,128)(2,1)S(1)} %get-tuple-element.76) | copy-start | bytes 18874372
  192.6 22.7 %slice-start.9 = ((s8[6291456]{0:T(1024)(128)(4,1)}), s8[4194304]{0:T(1024)(128)(4,1)S(1)}, s32[]{:S(2)}) async-start(s8[6291456]{0:T(1024)(128)(4,1)} %bitcast.162), calls=%async_computation.9 | async-start | bytes 8388608
  196.8 18.4 %slice-start.10 = ((s8[6291456]{0:T(1024)(128)(4,1)}), s8[2097152]{0:T(1024)(128)(4,1)S(1)}, s32[]{:S(2)}) async-start(s8[6291456]{0:T(1024)(128)(4,1)} %bitcast.162), calls=%async_computation.10 | async-start | bytes 4194304
  236.1 6.3 %slice-start.11 = ((s8[6291456]{0:T(1024)(128)(4,1)}), s8[4194304]{0:T(1024)(128)(4,1)S(1)}, s32[]{:S(2)}) async-start(s8[6291456]{0:T(1024)(128)(4,1)} %bitcast.208), calls=%async_computation.11 | async-start | bytes 8388608
  256.2 10.1 %slice-start.3 = ((s8[12582912]{0:T(1024)(128)(4,1)}), s8[4194304]{0:T(1024)(128)(4,1)S(1)}, s32[]{:S(2)}) async-start(s8[12582912]{0:T(1024)(128)(4,1)} %bitcast.144), calls=%async_computation.3 | async-start | bytes 8388608
  259.6 6.7 %slice-start.4 = ((s8[12582912]{0:T(1024)(128)(4,1)}), s8[4194304]{0:T(1024)(128)(4,1)S(1)}, s32[]{:S(2)}) async-start(s8[12582912]{0:T(1024)(128)(4,1)} %bitcast.144), calls=%async_computation.4 | async-start | bytes 8388608
  259.7 7.0 %slice-start.5 = ((s8[12582912]{0:T(1024)(128)(4,1)}), s8[4194304]{0:T(1024)(128)(4,1)S(1)}, s32[]{:S(2)}) async-start(s8[12582912]{0:T(1024)(128)(4,1)} %bitcast.144), calls=%async_computation.5 | async-start | bytes 8388608
  259.8 7.0 %copy-start.58 = (f32[12,512]{1,0:T(8,128)S(1)}, f32[12,512]{1,0:T(8,128)}, u32[]{:S(2)}) copy-start(f32[12,512]{1,0:T(8,128)} %log_add_fusion.1) | copy-start | bytes 73732
  275.5 11.0 %slice-start.6 = ((s8[12582912]{0:T(1024)(128)(4,1)}), s8[4194304]{0:T(1024)(128)(4,1)S(1)}, s32[]{:S(2)}) async-start(s8[12582912]{0:T(1024)(128)(4,1)} %bitcast.146), calls=%async_computation.6 | async-start | bytes 8388608
  275.5 11.0 %slice-start.7 = ((s8[12582912]{0:T(1024)(128)(4,1)}), s8[4194304]{0:T(1024)(128)(4,1)S(1)}, s32[]{:S(2)}) async-start(s8[12582912]{0:T(1024)(128)(4,1)} %bitcast.146), calls=%async_computation.7 | async-start | bytes 8388608
  275.5 12.6 %slice-start.8 = ((s8[12582912]{0:T(1024)(128)(4,1)}), s8[4194304]{0:T(1024)(128)(4,1)S(1)}, s32[]{:S(2)}) async-start(s8[12582912]{0:T(1024)(128)(4,1)} %bitcast.146), calls=%async_computation.8 | async-start | bytes 8388608
  288.2 10.9 %copy-start.15 = (bf16[512,768]{0,1:T(8,128)(2,1)S(1)}, bf16[512,768]{0,1:T(8,128)(2,1)}, u32[]{:S(2)}) copy-start(bf16[512,768]{0,1:T(8,128)(2,1)} %copy-done.14) | copy-start | bytes 2359300
  288.2 19.9 %slice-start = ((s8[12582912]{0:T(1024)(128)(4,1)}), s8[4194304]{0:T(1024)(128)(4,1)S(1)}, s32[]{:S(2)}) async-start(s8[12582912]{0:T(1024)(128)(4,1)} %bitcast.142), calls=%async_computation | async-start | bytes 8388608
  288.2 19.9 %slice-start.1 = ((s8[12582912]{0:T(1024)(128)(4,1)}), s8[4194304]{0:T(1024)(128)(4,1)S(1)}, s32[]{:S(2)}) async-start(s8[12582912]{0:T(1024)(128)(4,1)} %bitcast.142), calls=%async_computation.1 | async-start | bytes 8388608
  299.1 9.0 %slice-start.2 = ((s8[12582912]{0:T(1024)(128)(4,1)}), s8[4194304]{0:T(1024)(128)(4,1)S(1)}, s32[]{:S(2)}) async-start(s8[12582912]{0:T(1024)(128)(4,1)} %bitcast.142), calls=%async_computation.2 | async-start | bytes 8388608
  315.0 7.1 %copy-start.13 = (bf16[512,768]{0,1:T(8,128)(2,1)S(1)}, bf16[512,768]{0,1:T(8,128)(2,1)}, u32[]{:S(2)}) copy-start(bf16[512,768]{0,1:T(8,128)(2,1)} %copy-done.12) | copy-start | bytes 2359300
  337.2 109.6 %copy-start.41 = (bf16[1,8,96,768]{3,2,1,0:T(8,128)(2,1)S(1)}, bf16[1,8,96,768]{3,2,1,0:T(8,128)(2,1)}, u32[]{:S(2)}) copy-start(bf16[1,8,96,768]{3,2,1,0:T(8,128)(2,1)} %copy-done.40) | copy-start | bytes 3538948
  453.0 5.8 %copy-start.55 = (f32[96,768]{1,0:T(8,128)S(1)}, f32[96,768]{1,0:T(8,128)}, u32[]{:S(2)}) copy-start(f32[96,768]{1,0:T(8,128)} %get-tuple-element.150) | copy-start | bytes 884740
  453.0 7.5 %copy-start.51 = (f32[384,768]{1,0:T(8,128)S(1)}, f32[384,768]{1,0:T(8,128)}, u32[]{:S(2)}) copy-start(f32[384,768]{1,0:T(8,128)} %get-tuple-element.156) | copy-start | bytes 3538948
  (55 other events, 179.1 us)

commit v2 on v1

--- a/solution.py
+++ b/solution.py
@@ -415,6 +415,343 @@
         gi.reshape((4,) + square), gr.reshape((4, 2, 4, TR, D)), gvec.reshape((4, 2, 8, D)),
     )
 
+
+NT = (((1,), (1,)), ((), ()))
+TN = (((0,), (0,)), ((), ()))
+NN = (((1,), (0,)), ((), ()))
+EPS = 1e-06
+RSQRT2 = 0.7071067811865476
+RSQRT2PI = 0.3989422804014327
+
+
+def mm(a, b, dims=NN):
+    return lax.dot_general(a, b, dims, preferred_element_type=F32)
+
+
+def rows_of(i, size):
+    return pl.ds(pl.multiple_of(i * size, size), size)
+
+
+def column_mask(kept, shape, width):
+    return jnp.where(lax.broadcasted_iota(jnp.int32, shape, 1) < kept * width, 1.0, 0.0).astype(F32)
+
+
+def mean_of(v):
+    return jnp.sum(v, axis=1, keepdims=True) * (1.0 / D)
+
+
+def norm_rows(total):
+    centered = total - mean_of(total)
+    inverse = lax.rsqrt(mean_of(centered * centered) + EPS)
+    return centered * inverse, inverse
+
+
+def norm_back(grad, normed, inverse):
+    return inverse * (grad - mean_of(grad) - normed * mean_of(grad * normed))
+
+
+def expand_vectors(fv, rows, binner):
+    lane = lax.broadcasted_iota(jnp.int32, (128, D), 0)
+    column = lax.broadcasted_iota(jnp.int32, (128, D), 1)
+    total = jnp.zeros((16, D), F32)
+    for s in range(8):
+        pick = jnp.where((column == lane + TR * s) & (lane < TR), 1.0, 0.0).astype(BF)
+        total = total + mm(fv[s], pick)
+    rows[...] = total[0:8]
+    for s in range(8):
+        tile = fv[s].astype(F32)
+        for r in range(3):
+            binner[0:1, 128 * (3 * s + r) : 128 * (3 * s + r + 1)] = tile[8 + r : 9 + r]
+
+
+def project(x, fa, rows, q, k, v, block=256):
+    def one(i, _):
+        at = rows_of(i, block)
+        xb = x[at]
+        q[at] = ((mm(xb, fa[0]) + rows[0:1]) * 0.125).astype(BF)
+        k[at] = mm(xb, fa[1]).astype(BF)
+        v[at] = (mm(xb, fa[2]) + rows[1:2]).astype(BF)
+        return 0
+
+    lax.fori_loop(0, x.shape[0] // block, one, 0)
+
+
+def low_lanes(n):
+    return lax.broadcasted_iota(jnp.int32, (n, 128), 1) < HEAD_DIM
+
+
+def attend(i, qkv, segc, segr, kept, att, inv, ebuf, qb=512):
+    q, k, v = qkv
+    r, pair = lax.div(i, 6), lax.rem(i, 6)
+    lanes = pl.ds(pl.multiple_of(pair * 128, 128), 128)
+    rows = rows_of(r, SEQ)
+    kp, vp = k[rows, lanes], v[rows, lanes]
+    low = low_lanes(SEQ)
+    ones = jnp.ones_like(vp)
+    vs = (jnp.where(low, vp, ones), jnp.where(low, ones, vp))
+    ids = segr[r]
+    lowq = low_lanes(qb)
+    for b in range(SEQ // qb):
+        at = pl.ds(pl.multiple_of(r * SEQ + b * qb, qb), qb)
+        qp = q[at, lanes]
+        zero = jnp.zeros_like(qp)
+        same = segc[r, b * qb : (b + 1) * qb] == ids
+        out = []
+        for h in range(2):
+            qh = jnp.where(lowq, qp, zero) if h == 0 else jnp.where(lowq, zero, qp)
+            scores = jnp.where(same, mm(qh, kp, NT), -1e30)
+            top = jnp.max(scores, axis=1, keepdims=True)
+            e = jnp.exp(scores - top).astype(BF)
+            ebuf[h, b * qb : (b + 1) * qb] = e
+            out.append(mm(e, vs[h]))
+        inverse = 1.0 / pltpu.roll(jnp.where(lowq, out[1], out[0]), HEAD_DIM, 1)
+        column = lax.broadcasted_iota(jnp.int32, (1, 128), 1) + pair * 128
+        mask = jnp.where(column < kept * HEAD_DIM, 1.0, 0.0).astype(F32)
+        att[at, lanes] = (jnp.where(lowq, out[0], out[1]) * (inverse * mask)).astype(BF)
+        inv[at, lanes] = inverse
+
+
+def branch_out(x, att, fa, rows, t1, block=256):
+    def one(i, _):
+        at = rows_of(i, block)
+        t1[at] = x[at].astype(F32) + (mm(att[at], fa[3]) + rows[2:3])
+        return 0
+
+    lax.fori_loop(0, x.shape[0] // block, one, 0)
+
+
+def feed_forward(t1, grad, rows, binner, wi, wr, wo, inv, kept, y, res, bg, dos, hl, act, ig, og, gp, sums, bsum, block=256):
+    b_outer, gain_two, shift_two = rows[5:6], rows[6:7], rows[7:8]
+    gain_one, shift_one = rows[3:4], rows[4:5]
+    sums[...] = jnp.zeros_like(sums)
+    bsum[...] = jnp.zeros_like(bsum)
+    heads = column_mask(kept, (1, D), HEAD_DIM)
+
+    def add(k, value):
+        sums[k : k + 1] += jnp.sum(value, axis=0, keepdims=True)
+
+    def one(i, _):
+        at = rows_of(i, block)
+        n1, inv1 = norm_rows(t1[at])
+        hidden = n1 * gain_one + shift_one
+        low = hidden.astype(BF)
+        hl[at] = low
+        outer = jnp.zeros((block, D), F32)
+        for j in range(4):
+            cols = slice(j * D, (j + 1) * D)
+            inner = mm(low, wi[j]) + binner[:, cols]
+            keep = column_mask(kept * 256 - j * D, (1, D), 1)
+            phi = 0.5 + 0.5 * lax.erf(inner * RSQRT2)
+            masked = inner * keep
+            a = (masked * phi).astype(BF)
+            gp[:, cols] = (keep * phi + masked * (RSQRT2PI * jnp.exp(-0.5 * (inner * inner)))).astype(BF)
+            act[at, cols] = a
+            outer = outer + mm(a, wr[cols])
+        n2, inv2 = norm_rows(hidden + (outer + b_outer))
+        y[at] = (n2 * gain_two + shift_two).astype(BF)
+        top = grad[at].astype(F32)
+        add(7, top)
+        add(6, top * n2)
+        res2 = norm_back(top * gain_two, n2, inv2)
+        o = res2.astype(BF)
+        og[at] = o
+        add(5, o.astype(F32))
+        hg = res2
+        for j in range(4):
+            cols = slice(j * D, (j + 1) * D)
+            g = (mm(o, wr[cols], NT) * gp[:, cols].astype(F32)).astype(BF)
+            ig[at, cols] = g
+            bsum[:, cols] += jnp.sum(g.astype(F32), axis=0, keepdims=True)
+            hg = hg + mm(g, wi[j], NT)
+        add(4, hg)
+        n1, inv1 = norm_rows(t1[at])
+        add(3, hg * n1)
+        res1 = norm_back(hg * gain_one, n1, inv1)
+        res[at] = res1
+        b = res1.astype(BF)
+        bg[at] = b
+        add(2, b.astype(F32))
+        dos[at] = (mm(b, wo[...], NT) * (inv[at] * heads)).astype(BF)
+        return 0
+
+    lax.fori_loop(0, t1.shape[0] // block, one, 0)
+
+
+def inner_grads(j, hl, ig, gi):
+    cols = pl.ds(pl.multiple_of(j * D, D), D)
+    gi[j] = mm(hl[...], ig[:, cols], TN).astype(BF)
+
+
+def outer_grads(j, act, og, gr, block=512):
+    cols = pl.ds(pl.multiple_of(j * block, block), block)
+    gr[cols] = mm(act[:, cols], og[...], TN).astype(BF)
+
+
+def attend_back(i, qkv, dos, att, ebuf, dq, dk, dv):
+    q, k, v = qkv
+    r, pair = lax.div(i, 6), lax.rem(i, 6)
+    lanes = pl.ds(pl.multiple_of(pair * 128, 128), 128)
+    rows = rows_of(r, SEQ)
+    qp, kp, vp, dp = q[rows, lanes], k[rows, lanes], v[rows, lanes], dos[rows, lanes]
+    low = low_lanes(SEQ)
+    zero = jnp.zeros_like(qp)
+    product = dp.astype(F32) * att[rows, lanes].astype(F32)
+    gq = jnp.zeros((SEQ, 128), F32)
+    gk = jnp.zeros((SEQ, 128), F32)
+    gv = jnp.zeros((SEQ, 128), F32)
+    for h in range(2):
+        mine = low if h == 0 else jnp.logical_not(low)
+        dh = jnp.where(mine, dp, zero)
+        delta = jnp.sum(jnp.where(mine, product, 0.0), axis=1, keepdims=True)
+        e = ebuf[h]
+        ds = (e.astype(F32) * (mm(dh, vp, NT) - delta)).astype(BF)
+        gv = gv + mm(e, dh, TN)
+        gk = gk + mm(ds, jnp.where(mine, qp, zero), TN)
+        gq = gq + mm(ds, jnp.where(mine, kp, zero))
+    dq[rows, lanes] = (gq * 0.125).astype(BF)
+    dk[rows, lanes] = gk.astype(BF)
+    dv[rows, lanes] = gv.astype(BF)
+
+
+def input_back(res, dq, dk, dv, fa, out, sums, block=256):
+    sums[0:2] = jnp.zeros((2, D), F32)
+
+    def one(i, _):
+        at = rows_of(i, block)
+        a, b, c = dq[at], dk[at], dv[at]
+        out[at] = (res[at] + mm(a, fa[0], NT) + mm(b, fa[1], NT) + mm(c, fa[2], NT)).astype(BF)
+        sums[0:1] += jnp.sum(a.astype(F32), axis=0, keepdims=True)
+        sums[1:2] += jnp.sum(c.astype(F32), axis=0, keepdims=True)
+        return 0
+
+    lax.fori_loop(0, res.shape[0] // block, one, 0)
+
+
+VM = pl.BlockSpec(memory_space=pltpu.VMEM)
+SM = pl.BlockSpec(memory_space=pltpu.SMEM)
+ANY = pl.BlockSpec(memory_space=pl.ANY)
+
+
+def params(**more):
+    return pltpu.CompilerParams(vmem_limit_bytes=62 << 20, **more)
+
+
+def shape(*dims, dtype=BF):
+    return jax.ShapeDtypeStruct(dims, dtype)
+
+
+def forward_kernel(x, segc, segr, kept, fa, rows, q, k, v, att, inv, e_out, t1, ebuf, sem):
+    project(x, fa, rows, q, k, v)
+    keep = kept[0]
+
+    def out_copy(i, slot):
+        r, pair = lax.div(i, 6), lax.rem(i, 6)
+        return pltpu.make_async_copy(ebuf.at[slot], e_out.at[r, pair], sem.at[slot])
+
+    def one(i, _):
+        slot = lax.rem(i, 2)
+
+        @pl.when(i >= 2)
+        def _():
+            out_copy(i - 2, slot).wait()
+
+        attend(i, (q, k, v), segc, segr, keep, att, inv, ebuf.at[slot])
+        out_copy(i, slot).start()
+        return 0
+
+    n = 6 * (x.shape[0] // SEQ)
+    lax.fori_loop(0, n, one, 0)
+    branch_out(x, att, fa, rows, t1)
+    out_copy(n - 2, (n - 2) % 2).wait()
+    out_copy(n - 1, (n - 1) % 2).wait()
+
+
+def forward_attention(x, segment_ids, kept, fa, rows):
+    t = x.shape[0]
+    n = t // SEQ
+    return pl.pallas_call(
+        forward_kernel,
+        out_shape=(shape(t, D), shape(t, D), shape(t, D), shape(t, D), shape(t, D, dtype=F32),
+                   shape(n, 6, 2, SEQ, SEQ), shape(t, D, dtype=F32)),
+        in_specs=[VM, VM, VM, SM, VM, VM],
+        out_specs=(VM, VM, VM, VM, VM, ANY, VM),
+        scratch_shapes=[pltpu.VMEM((2, 2, SEQ, SEQ), BF), pltpu.SemaphoreType.DMA((2,))],
+        compiler_params=params(),
+        name="attention",
+    )(x, segment_ids.reshape(n, SEQ, 1), segment_ids.reshape(n, 1, SEQ), kept, fa, rows)
+
+
+def ffn_kernel(t1, grad, rows, binner, wi, wr, wo, inv, kept, y, res, bg, dos, gi, gr, sums, bsum, hl, act, ig, og, gp):
+    feed_forward(t1, grad, rows, binner, wi, wr, wo, inv, kept[0], y, res, bg, dos, hl, act, ig, og, gp, sums, bsum)
+
+    def one(j, _):
+        inner_grads(j, hl, ig, gi)
+        return 0
+
+    lax.fori_loop(0, 4, one, 0)
+
+    def two(j, _):
+        outer_grads(j, act, og, gr)
+        return 0
+
+    lax.fori_loop(0, FF // 512, two, 0)
+
+
+def ffn(t1, grad, rows, binner, wi, wr, wo, inv, kept):
+    t = t1.shape[0]
+    return pl.pallas_call(
+        ffn_kernel,
+        out_shape=(shape(t, D), shape(t, D, dtype=F32), shape(t, D), shape(t, D),
+                   shape(4, D, D), shape(FF, D), shape(8, D, dtype=F32), shape(1, FF, dtype=F32)),
+        in_specs=[VM] * 8 + [SM],
+        out_specs=(VM,) * 8,
+        scratch_shapes=[pltpu.VMEM((t, D), BF), pltpu.VMEM((t, FF), BF), pltpu.VMEM((t, FF), BF),
+                        pltpu.VMEM((t, D), BF), pltpu.VMEM((256, FF), BF)],
+        compiler_params=params(),
+        name="ffn",
+    )(t1, grad, rows, binner, wi, wr, wo, inv, kept)
+
+
+def backward_kernel(x, q, k, v, e_in, att, dos, bg, res, fa, sums_in, out, gq, gk, gv, go, sums, dq, dk, dv, ebuf, sem):
+    def in_copy(i, slot):
+        r, pair = lax.div(i, 6), lax.rem(i, 6)
+        return pltpu.make_async_copy(e_in.at[r, pair], ebuf.at[slot], sem.at[slot])
+
+    n = 6 * (x.shape[0] // SEQ)
+    in_copy(0, 0).start()
+    sums[...] = sums_in[...]
+    go[...] = mm(att[...], bg[...], TN).astype(BF)
+
+    def one(i, _):
+        slot = lax.rem(i, 2)
+
+        @pl.when(i + 1 < n)
+        def _():
+            in_copy(i + 1, 1 - slot).start()
+
+        in_copy(i, slot).wait()
+        attend_back(i, (q, k, v), dos, att, ebuf.at[slot], dq, dk, dv)
+        return 0
+
+    lax.fori_loop(0, n, one, 0)
+    gq[...] = mm(x[...], dq[...], TN).astype(BF)
+    gk[...] = mm(x[...], dk[...], TN).astype(BF)
+    gv[...] = mm(x[...], dv[...], TN).astype(BF)
+    input_back(res, dq, dk, dv, fa, out, sums)
+
+
+def backward_attention(x, q, k, v, e, att, dos, bg, res, fa, sums):
+    t = x.shape[0]
+    return pl.pallas_call(
+        backward_kernel,
+        out_shape=(shape(t, D), shape(D, D), shape(D, D), shape(D, D), shape(D, D), shape(8, D, dtype=F32)),
+        in_specs=[VM] * 4 + [ANY] + [VM] * 6,
+        out_specs=(VM,) * 6,
+        scratch_shapes=[pltpu.VMEM((t, D), BF)] * 3 + [pltpu.VMEM((2, 2, SEQ, SEQ), BF), pltpu.SemaphoreType.DMA((2,))],
+        compiler_params=params(),
+        name="attention_back",
+    )(x, q, k, v, e, att, dos, bg, res, fa, sums)
+
 def kernels_fit():
     return lax.axis_size("width") == 4 and lax.axis_size("shard") == 8
 
@@ -427,8 +764,8 @@
         fa, fi, fo, fv = gather_fast(wq, wk, wv, wo, wi, wr, vec)
         fa, fi, fo = fa.reshape(4, D, D), fi.reshape(4, D, D), fo.reshape(FF, D)
         rows = fv[:, 0].reshape(8, 8, TR).astype(F32)
-        vectors = tuple(rows[:, k].reshape(D) for k in range(8))
-        return (*(fa[q] for q in range(4)), fi, fo, vectors, fv[:, 1, : FF // 8].reshape(FF).astype(F32))
+        rows = rows.transpose(1, 0, 2).reshape(8, D)
+        return fa, fi, fo, rows, fv[:, 1, : FF // 8].reshape(1, FF).astype(F32)
 
     def whole(a):
         return lax.all_gather(a.astype(BF), "shard", axis=0, tiled=True)
@@ -436,7 +773,8 @@
     fi = whole(wi)
     fi = jnp.stack([fi[:, q * D : (q + 1) * D] for q in range(4)])
     vectors = tuple(whole(a).astype(F32) for a in eight)
-    return (whole(wq), whole(wk), whole(wv), whole(wo), fi, whole(wr), vectors, whole(b_inner).astype(F32))
+    fa = jnp.stack([whole(wq), whole(wk), whole(wv), whole(wo)])
+    return fa, fi, whole(wr), jnp.stack(vectors), whole(b_inner).astype(F32).reshape(1, FF)
 
 
 def reduce(gq, gk, gv, go, gi, gr, eight, b_inner):
@@ -457,203 +795,20 @@
     return matrices, tuple(owned(a) for a in eight), owned(b_inner)
 
 
-def to_half(value):
-    return value.astype(jnp.bfloat16)
-
-
-def norm_parts(total):
-    row_mean = jnp.mean(total, axis=-1, keepdims=True)
-    centered = total - row_mean
-    inverse = lax.rsqrt(jnp.mean(centered * centered, axis=-1, keepdims=True) + 1e-06)
-    return (centered * inverse, inverse)
-
-
-def norm_back(grad_normed, normed, inverse):
-    first = jnp.mean(grad_normed, axis=-1, keepdims=True)
-    second = jnp.mean(grad_normed * normed, axis=-1, keepdims=True)
-    return inverse * (grad_normed - first - normed * second)
-
-
-def row_scores(query_row, key_row, segment_row, score_scale):
-    scores = (
-        jnp.einsum("qhd,khd->hqk", query_row, key_row, preferred_element_type=jnp.float32)
-        * score_scale
-    )
-    same_doc = segment_row[:, None] == segment_row[None, :]
-    return jnp.where(same_doc[None], scores, -1e30)
-
-
-def column_sum(value):
-    return jnp.sum(value.astype(jnp.float32), axis=0)
-
-
-def weight_grad(left, right):
-    return jnp.einsum("ti,tj->ij", left, right, preferred_element_type=jnp.float32)
-
-
-def back_product(grad_rows, weight):
-    return jnp.einsum("tj,ij->ti", grad_rows, weight, preferred_element_type=jnp.float32)
-
-
-def forward_product(rows_in, weight):
-    return jnp.dot(rows_in, weight, preferred_element_type=jnp.float32)
-
-
 def body(
-    layer_input,
-    segment_ids,
-    group_heads,
-    w_query,
-    b_query,
-    w_key,
-    w_value,
-    b_value,
-    w_out,
-    b_out,
-    gain_one,
-    shift_one,
-    w_inner,
-    b_inner,
-    w_outer,
-    b_outer,
-    gain_two,
-    shift_two,
-    out_grad,
+    layer_input, segment_ids, group_heads,
+    w_query, b_query, w_key, w_value, b_value, w_out, b_out, gain_one, shift_one,
+    w_inner, b_inner, w_outer, b_outer, gain_two, shift_two, out_grad,
 ):
-    score_scale = HEAD_DIM ** (-0.5)
-    kept_heads = group_heads[0]
-    head_mask = (jnp.arange(D) // HEAD_DIM < kept_heads).astype(jnp.float32)
-    unit_mask = (jnp.arange(FF) // (FF // HEADS) < kept_heads).astype(jnp.float32)
-    gathered = gather(w_query, w_key, w_value, w_out, w_inner, w_outer, (b_query, b_value, b_out, gain_one, shift_one, b_outer, gain_two, shift_two), b_inner)
-    full_query, full_key, full_value, full_out, full_inner, full_outer, vectors, bias_inner = gathered
-    bias_query, bias_value, bias_out, gain_first, shift_first, bias_outer, gain_second, shift_second = vectors
-    queries = to_half(forward_product(layer_input, full_query) + bias_query)
-    keys = to_half(forward_product(layer_input, full_key))
-    values = to_half(forward_product(layer_input, full_value) + bias_value)
-    row_count = layer_input.shape[0] // SEQ
-    attended_rows = []
-    log_rows = []
-    for row_index in range(row_count):
-        window = slice(row_index * SEQ, (row_index + 1) * SEQ)
-        query_row = queries[window].reshape(SEQ, HEADS, HEAD_DIM)
-        key_row = keys[window].reshape(SEQ, HEADS, HEAD_DIM)
-        value_row = values[window].reshape(SEQ, HEADS, HEAD_DIM)
-        scores = row_scores(query_row, key_row, segment_ids[row_index], score_scale)
-        top_score = jnp.max(scores, axis=-1, keepdims=True)
-        expanded = jnp.exp(scores - top_score)
-        denominator = jnp.sum(expanded, axis=-1, keepdims=True)
-        probs_low = to_half(expanded / denominator)
-        attended_rows.append(
-            jnp.einsum(
-                "hqk,khd->qhd", probs_low, value_row, preferred_element_type=jnp.float32
-            ).reshape(SEQ, D)
-        )
-        log_rows.append(top_score + jnp.log(denominator))
-    attended = to_half(jnp.concatenate(attended_rows, axis=0) * head_mask)
-    branch = forward_product(attended, full_out) + bias_out
-    normed_one, inverse_one = norm_parts(layer_input.astype(jnp.float32) + branch)
-    hidden = normed_one * gain_first + shift_first
-    hidden_low = to_half(hidden)
-    inner = jnp.concatenate([forward_product(hidden_low, full_inner[q]) for q in range(4)], axis=1) + bias_inner
-
-    def gelu_exact(value):
-        return jax.nn.gelu(value, approximate=False)
-
-    gelu_value, gelu_pull = jax.vjp(gelu_exact, inner)
-    active = to_half(gelu_value * unit_mask)
-    outer = forward_product(active, full_outer) + bias_outer
-    normed_two, inverse_two = norm_parts(hidden + outer)
-    layer_output = to_half(normed_two * gain_second + shift_second)
-    top_grad = out_grad.astype(jnp.float32)
-    shift_two_grad = jnp.sum(top_grad, axis=0)
-    gain_two_grad = jnp.sum(top_grad * normed_two, axis=0)
-    res_two_grad = norm_back(top_grad * gain_second, normed_two, inverse_two)
-    outer_grad = to_half(res_two_grad)
-    b_outer_grad = column_sum(outer_grad)
-    w_outer_grad = weight_grad(active, outer_grad)
-    active_grad = back_product(outer_grad, full_outer)
-    inner_grad = to_half(gelu_pull(active_grad * unit_mask)[0])
-    b_inner_grad = column_sum(inner_grad)
-    w_inner_grad = jnp.stack([to_half(weight_grad(hidden_low, inner_grad[:, q * D : (q + 1) * D])) for q in range(4)])
-    hidden_grad = res_two_grad + sum(back_product(inner_grad[:, q * D : (q + 1) * D], full_inner[q]) for q in range(4))
-    shift_one_grad = jnp.sum(hidden_grad, axis=0)
-    gain_one_grad = jnp.sum(hidden_grad * normed_one, axis=0)
-    res_one_grad = norm_back(hidden_grad * gain_first, normed_one, inverse_one)
-    branch_grad = to_half(res_one_grad)
-    b_out_grad = column_sum(branch_grad)
-    w_out_grad = weight_grad(attended, branch_grad)
-    attended_grad = to_half(back_product(branch_grad, full_out)) * to_half(head_mask)
-    query_rows = []
-    key_rows = []
-    value_rows = []
-    for row_index in range(row_count):
-        window = slice(row_index * SEQ, (row_index + 1) * SEQ)
-        query_row = queries[window].reshape(SEQ, HEADS, HEAD_DIM)
-        key_row = keys[window].reshape(SEQ, HEADS, HEAD_DIM)
-        value_row = values[window].reshape(SEQ, HEADS, HEAD_DIM)
-        grad_row = attended_grad[window].reshape(SEQ, HEADS, HEAD_DIM)
-        scores = row_scores(query_row, key_row, segment_ids[row_index], score_scale)
-        probs = jnp.exp(scores - log_rows[row_index])
-        prob_grad = jnp.einsum(
-            "qhd,khd->hqk", grad_row, value_row, preferred_element_type=jnp.float32
-        )
-        value_rows.append(
-            jnp.einsum(
-                "hqk,qhd->khd", to_half(probs), grad_row, preferred_element_type=jnp.float32
-            ).reshape(SEQ, D)
-        )
-        score_grad = to_half(
-            probs * (prob_grad - jnp.sum(probs * prob_grad, axis=-1, keepdims=True))
-        )
-        query_rows.append(
-            (
-                jnp.einsum("hqk,khd->qhd", score_grad, key_row, preferred_element_type=jnp.float32)
-                * score_scale
-            ).reshape(SEQ, D)
-        )
-        key_rows.append(
-            (
-                jnp.einsum(
-                    "hqk,qhd->khd", score_grad, query_row, preferred_element_type=jnp.float32
-                )
-                * score_scale
-            ).reshape(SEQ, D)
-        )
-    query_grad = to_half(jnp.concatenate(query_rows, axis=0))
-    key_grad = to_half(jnp.concatenate(key_rows, axis=0))
-    value_grad = to_half(jnp.concatenate(value_rows, axis=0))
-    b_query_grad = column_sum(query_grad)
-    b_value_grad = column_sum(value_grad)
-    w_query_grad = weight_grad(layer_input, query_grad)
-    w_key_grad = weight_grad(layer_input, key_grad)
-    w_value_grad = weight_grad(layer_input, value_grad)
-    input_grad = to_half(
-        res_one_grad
-        + back_product(query_grad, full_query)
-        + back_product(key_grad, full_key)
-        + back_product(value_grad, full_value)
-    )
-    matrices, vectors, b_inner_grad = reduce(
-        to_half(w_query_grad), to_half(w_key_grad), to_half(w_value_grad), to_half(w_out_grad), w_inner_grad, to_half(w_outer_grad),
-        (b_query_grad, b_value_grad, b_out_grad, gain_one_grad, shift_one_grad, b_outer_grad, gain_two_grad, shift_two_grad), b_inner_grad)
+    eight = (b_query, b_value, b_out, gain_one, shift_one, b_outer, gain_two, shift_two)
+    fa, fi, fo, rows, binner = gather(w_query, w_key, w_value, w_out, w_inner, w_outer, eight, b_inner)
+    q, k, v, att, inv, e, t1 = forward_attention(layer_input, segment_ids, group_heads, fa, rows)
+    y, res, bg, dos, gi, gr, sums, bsum = ffn(t1, out_grad, rows, binner, fi, fo, fa[3], inv, group_heads)
+    input_grad, gq, gk, gv, go, sums = backward_attention(layer_input, q, k, v, e, att, dos, bg, res, fa, sums)
+    matrices, vectors, b_inner_grad = reduce(gq, gk, gv, go, gi, gr, tuple(sums[i] for i in range(8)), bsum[0])
     return (
-        layer_output,
-        input_grad,
-        matrices[0],
-        vectors[0],
-        matrices[1],
-        matrices[2],
-        vectors[1],
-        matrices[3],
-        vectors[2],
-        vectors[3],
-        vectors[4],
-        matrices[4],
-        b_inner_grad,
-        matrices[5],
-        vectors[5],
-        vectors[6],
-        vectors[7],
+        y, input_grad, matrices[0], vectors[0], matrices[1], matrices[2], vectors[1], matrices[3], vectors[2],
+        vectors[3], vectors[4], matrices[4], b_inner_grad, matrices[5], vectors[5], vectors[6], vectors[7],
     )
 
 

time: 465 us -> 324 us (0.70)
  matrix products: 149 us -> 0 us
  Pallas kernels: 177 us -> 294 us
  other arithmetic: 87.3 us -> 8.17 us
  local copies, waits for them, and re-layouts: 46.1 us -> 20.2 us
    dot_general x39 -> x0, matrix products: 149 us -> none  [the longest x9 42.4 us: back_product(): jnp.einsum('tj,ij->ti', grad_rows, weight, preferred_element_type=jnp.flo...]
    pallas_call x0 -> x3, Pallas kernels: none -> 117 us  [the longest x1 53.1 us: ffn(): pl.pallas_call(ffn_kernel, out_shape=(shape(t, D), shape(t, D, dtype=F32)...]
    convert_element_type x8 -> x1, other arithmetic: 59.7 us -> 0.61 us  [gather(): return (fa, fi, fo, rows, fv[:, 1, :FF // 8].reshape(1, FF).astype(F32))]
    unnamed x168 -> x21, local copies, waits for them, and re-layouts: 30.6 us -> 7.86 us
    reduce_sum x9 -> x0, other arithmetic: 15.2 us -> none  [the longest x4 7.95 us: column_sum(): return jnp.sum(value.astype(jnp.float32), axis=0)]
    slice x7 -> x3, local copies, waits for them, and re-layouts: 9.36 us -> 4.27 us  [the longest x1 2.36 us: body(): fa[3]]
where the time goes in v2:
time: 324 us
  Pallas kernels  294 us (91%)
  local copies, waits for them, and re-layouts  20.2 us (6%)
  other arithmetic  8.17 us (3%)
    pallas_call x1, Pallas kernels, reduce_fast(): pl.pallas_call(reduce_kernel, out_shape=tuple((jax.ShapeDtypeStruct((TR,...  107 us
    pallas_call x1, Pallas kernels, gather_fast(): pl.pallas_call(gather_kernel, out_shape=(jax.ShapeDtypeStruct((4, 8, TR,...  69.8 us
    pallas_call x1, Pallas kernels, ffn(): pl.pallas_call(ffn_kernel, out_shape=(shape(t, D), shape(t, D, dtype=F32)...  53.1 us
    pallas_call x1, Pallas kernels, backward_attention(): pl.pallas_call(backward_kernel, out_shape=(shape(t, D), shape(D, D), shap...  34.5 us
    pallas_call x1, Pallas kernels, forward_attention(): pl.pallas_call(forward_kernel, out_shape=(shape(t, D), shape(t, D), shape...  29.9 us
    unnamed x21, local copies, waits for them, and re-layouts  7.86 us

profile of v2, /device:TPU:0, one launch (start us, length us, event | category | flops | bytes accessed | tf_op | source)
XLA Modules:
  0.0 323.7 jit_solution(490333078880835940)
XLA Ops:
  1.3 0.7 convert.38
  5.9 0.7 convert.45
  6.7 0.7 convert.46
  7.4 1.3 reshape.97.segr
  9.3 1.7 copy.40.segc
  11.0 69.8 %gather.1 = (bf16[4,8,96,768]{3,2,1,0:T(8,128)(2,1)}, bf16[4,8,96,768]{3,2,1,0:T(8,128)(2,1)}, bf16[8,4,96,768]{3,2,1,0:T(8,128)(2,1)}, bf16[8,16,768]{2,1,0:T(8,128)(2,1)}) custom-call(f32[96,768]{1,0:T(8,128)} %wq.1, f32[96,768]{1,0:T(8,128)} %wk.1, f32[96,768]{1,0:T(8,128)} %wv.1, f32[96,768]{1,0:T(8,128)} %wo.1, f32[96,3072]{1,0:T(8,128)} %wi.1, ...), custom_call_target="tpu_custom_call" | custom-call | tf_op jit(solution)/shard_map/gather/pallas_call | solution.py:180
  80.8 0.8 slice.62
  81.6 1.0 convert_reduce_fusion
  83.2 0.7 reshape.112.rows
  83.9 2.4 slice.63
  86.3 29.9 %attention.1 = (bf16[1024,768]{1,0:T(8,128)(2,1)}, bf16[1024,768]{1,0:T(8,128)(2,1)}, bf16[1024,768]{1,0:T(8,128)(2,1)}, bf16[1024,768]{1,0:T(8,128)(2,1)}, f32[...) custom-call(bf16[1024,768]{1,0:T(8,128)(2,1)} %x.11, s32[2,512,1]{2,1,0:T(8,128)} %copy.40.segc, ...), custom_call_target="tpu_custom_call" | custom-call | tf_op jit(solution)/shard_map/attention/pallas_call | solution.py:672
  116.2 53.1 %ffn.1 = (bf16[1024,768]{1,0:T(8,128)(2,1)}, f32[1024,768]{1,0:T(8,128)}, bf16[1024,768]{1,0:T(8,128)(2,1)}, bf16[1024,768]{1,0:T(8,128)(2,1)}, bf16[4,768,768]{...) custom-call(f32[1024,768]{1,0:T(8,128)} %get-tuple-element.51.t1, ...), custom_call_target="tpu_custom_call" | custom-call | tf_op jit(solution)/shard_map/ffn/pallas_call | solution.py:702
  169.3 34.5 %attention_back.1 = (bf16[1024,768]{1,0:T(8,128)(2,1)}, bf16[768,768]{1,0:T(8,128)(2,1)}, bf16[768,768]{1,0:T(8,128)(2,1)}, bf16[768,768]{1,0:T(8,128)(2,1)}, bf...) custom-call(bf16[1024,768]{1,0:T(8,128)(2,1)} %x.11, bf16[1024,768]{1,0:T(8,128)(2,1)} %get-tuple-element.56.q, ...), custom_call_target="tpu_custom_call" | custom-call | tf_op jit(solution)/shard_map/attention_back/pallas_call | solution.py:745
  203.8 1.1 slice_reduce_fusion
  205.7 0.7 pad.21
  206.4 106.6 %reduce.21 = (f32[96,768]{1,0:T(8,128)}, f32[96,768]{1,0:T(8,128)}, f32[96,768]{1,0:T(8,128)}, f32[96,768]{1,0:T(8,128)}, f32[96,3072]{1,0:T(8,128)}, /*index=5*/f32[384,768]{1,0:T(8,128)}, f32[8,768]{1,0:T(8,128)}) custom-call(bf16[4,2,96,768]{3,2,1,0:T(8,128)(2,1)} %bitcast.41, bf16[4,2,96,768]{3,2,1,0:T(8,128)(2,1)} %bitcast.42, ...), custom_call_target="tpu_custom_call" | custom-call | tf_op jit(solution)/shard_map/reduce/pallas_call | solution.py:378
  313.1 1.4 slice_reduce_fusion.8
  314.5 1.4 slice_bitcast_fusion
  315.8 1.7 copy.59
  317.5 1.7 copy.60
  319.2 1.7 copy.61
  320.9 0.7 copy.62
  321.7 1.0 copy.63
  322.7 1.0 copy.64
  (41 shorter events, 6.1 us)
Async XLA Ops:
  169.3 36.4 %copy-start.3 = (f32[1,3072]{1,0:T(1,128)S(1)}, f32[1,3072]{1,0:T(1,128)}, u32[]{:S(2)}) copy-start(f32[1,3072]{1,0:T(1,128)} %get-tuple-element.73) | copy-start | bytes 36868
  313.0 7.9 %copy-start.2 = (f32[96,768]{1,0:T(8,128)S(1)}, f32[96,768]{1,0:T(8,128)}, u32[]{:S(2)}) copy-start(f32[96,768]{1,0:T(8,128)} %get-tuple-element.121) | copy-start | bytes 884740
  313.0 8.6 %copy-start.1 = (f32[96,3072]{1,0:T(8,128)S(1)}, f32[96,3072]{1,0:T(8,128)}, u32[]{:S(2)}) copy-start(f32[96,3072]{1,0:T(8,128)} %get-tuple-element.125) | copy-start | bytes 3538948
  320.9 1.7 copy-start

commit v3 on v0

v3 whole, which is shorter than its diff:
```python
import functools
import jax
import jax.numpy as jnp
from jax import lax
from jax.experimental import pallas as pl
from jax.experimental.pallas import tpu as pltpu
from jax.sharding import PartitionSpec as P

HEADS = 12
HEAD_DIM = 64
FF = 3072
D = 768
SEQ = 512
MESH = pl.DeviceIdType.MESH
BF = jnp.bfloat16
F32 = jnp.float32
TR = 96
CW = 256
NT = (((1,), (1,)), ((), ()))
TN = (((0,), (0,)), ((), ()))
NN = (((1,), (0,)), ((), ()))
EPS = 1e-06
RSQRT2 = 0.7071067811865476
RSQRT2PI = 0.3989422804014327
VM = pl.BlockSpec(memory_space=pltpu.VMEM)
SM = pl.BlockSpec(memory_space=pltpu.SMEM)
ANY = pl.BlockSpec(memory_space=pl.ANY)


def params(**more):
    return pltpu.CompilerParams(vmem_limit_bytes=62 << 20, **more)


def shape(*dims, dtype=BF):
    return jax.ShapeDtypeStruct(dims, dtype)


class Place:
    def __init__(self):
        self.w = w = lax.axis_index("width")
        self.s = s = lax.axis_index("shard")
        self.c = c = lax.rem(s, 2)
        self.z = lax.div(s, 2)
        xw, yw = w + 1 - 2 * lax.rem(w, 2), lax.rem(w + 2, 4)
        up, down = lax.rem(s + 2, 8), lax.rem(s + 6, 8)
        self.wa = jnp.where(c == 0, xw, yw)
        self.wb = jnp.where(c == 0, yw, xw)
        self.wd = 3 - w
        self.sa = jnp.where(c == 0, up, down)
        self.sb = jnp.where(c == 0, down, up)
        self.so = lax.rem(s + 4, 8)
        self.sib = (w, s + 1 - 2 * c)
        self.plane_a, self.plane_b = (self.wa, s), (self.wb, s)
        self.ring_a, self.ring_b = (w, self.sa), (w, self.sb)


def greet(p, devices):
    barrier = pltpu.get_barrier_semaphore()
    for device in devices:
        pl.semaphore_signal(barrier, inc=1, device_id=device, device_id_type=MESH)
    pl.semaphore_wait(barrier, len(devices))


def others(p):
    return [(p.wa, p.s), (p.wb, p.s), (p.wd, p.s)] + [(p.w, lax.rem(p.s + k, 8)) for k in range(1, 8)]


class Net:
    def __init__(self, send, recv):
        self.send, self.recv, self.made = send, recv, {}

    def define(self, name, make):
        assert name not in self.made
        self.made[name] = (len(self.made), make)

    def copy(self, name):
        k, make = self.made[name]
        src, dst, device = make()
        return pltpu.make_async_remote_copy(
            src_ref=src, dst_ref=dst, send_sem=self.send.at[k], recv_sem=self.recv.at[k],
            device_id=device, device_id_type=MESH,
        )

    def start(self, *names):
        for name in names:
            self.copy(name).start()

    def wait(self, *names):
        for name in names:
            self.copy(name).wait_recv()

    def finish(self):
        for name in self.made:
            self.copy(name).wait_send()


def quarter(w):
    return pl.ds(pl.multiple_of(48 * lax.rem(w, 2), 48), 48), pl.ds(pl.multiple_of(384 * lax.div(w, 2), 384), 384)


def mm(a, b, dims=NN):
    return lax.dot_general(a, b, dims, preferred_element_type=F32)


def rows_of(i, size):
    return pl.ds(pl.multiple_of(i * size, size), size)


def column_mask(kept, shape, width):
    return jnp.where(lax.broadcasted_iota(jnp.int32, shape, 1) < kept * width, 1.0, 0.0).astype(F32)


def mean_of(v):
    return jnp.sum(v, axis=1, keepdims=True) * (1.0 / D)


def norm_rows(total):
    centered = total - mean_of(total)
    inverse = lax.rsqrt(mean_of(centered * centered) + EPS)
    return centered * inverse, inverse


def norm_back(grad, normed, inverse):
    return inverse * (grad - mean_of(grad) - normed * mean_of(grad * normed))


def low_lanes(n):
    return lax.broadcasted_iota(jnp.int32, (n, 128), 1) < HEAD_DIM


def place_of(i):
    return lax.div(i, 4), lax.rem(i, 2), lax.rem(lax.div(i, 2), 2)


def pair_lanes(pair, part):
    return pl.ds(pl.multiple_of(part * CW + pair * 128, 128), 128)


def chunk_bias(rows, c):
    lanes = slice(c * CW, (c + 1) * CW)
    return jnp.concatenate([rows[0:1, lanes], jnp.zeros((1, CW), F32), rows[1:2, lanes]], axis=1)


def project(x, fa, rows, qkv, block=256):
    scale = jnp.where(lax.broadcasted_iota(jnp.int32, (1, D), 1) < CW, 0.125, 1.0)

    def one(i, _):
        at = rows_of(i, block)
        xb = x[at]
        for c in range(3):
            weight = fa[c].reshape(D, D)
            qkv[c, at] = ((mm(xb, weight) + chunk_bias(rows, c)) * scale).astype(BF)
        return 0

    lax.fori_loop(0, x.shape[0] // block, one, 0)


def turn_ids(seg, segt):
    for r in range(seg.shape[0]):
        row = seg[r : r + 1, :].astype(F32)
        segt[r] = jnp.broadcast_to(row, (128, SEQ)).T


def attend(i, qkv, seg, segt, kept, att, inv, ebuf, qb=512):
    c, r, pair = place_of(i)
    base = r * SEQ
    rows = pl.ds(pl.multiple_of(base, SEQ), SEQ)
    kp, vp = qkv[c, rows, pair_lanes(pair, 1)], qkv[c, rows, pair_lanes(pair, 2)]
    low = low_lanes(SEQ)
    ones = jnp.ones_like(vp)
    vs = (jnp.where(low, vp, ones), jnp.where(low, ones, vp))
    ids = seg[pl.ds(r, 1), :].astype(F32)
    lowq = low_lanes(qb)
    lanes = pl.ds(pl.multiple_of(c * CW + pair * 128, 128), 128)
    column = lax.broadcasted_iota(jnp.int32, (1, 128), 1) + (c * CW + pair * 128)
    mask = jnp.where(column < kept * HEAD_DIM, 1.0, 0.0).astype(F32)
    for b in range(SEQ // qb):
        at = pl.ds(pl.multiple_of(base + b * qb, qb), qb)
        qp = qkv[c, at, pair_lanes(pair, 0)]
        zero = jnp.zeros_like(qp)
        own = segt[r, b * qb : (b + 1) * qb]
        same = jnp.concatenate([own == ids[:, j * 128 : (j + 1) * 128] for j in range(4)], axis=1)
        out = []
        for h in range(2):
            qh = jnp.where(lowq, qp, zero) if h == 0 else jnp.where(lowq, zero, qp)
            scores = jnp.where(same, mm(qh, kp, NT), -1e30)
            top = jnp.max(scores, axis=1, keepdims=True)
            e = jnp.exp(scores - top).astype(BF)
            ebuf[h, b * qb : (b + 1) * qb] = e
            out.append(mm(e, vs[h]))
        inverse = 1.0 / pltpu.roll(jnp.where(lowq, out[1], out[0]), HEAD_DIM, 1)
        att[at, lanes] = (jnp.where(lowq, out[0], out[1]) * (inverse * mask)).astype(BF)
        inv[at, lanes] = inverse


def expand_vectors(fv, rows, binner):
    lane = lax.broadcasted_iota(jnp.int32, (128, D), 0)
    column = lax.broadcasted_iota(jnp.int32, (128, D), 1)
    total = jnp.zeros((16, D), F32)
    for s in range(8):
        pick = jnp.where((column == lane + TR * s) & (lane < TR), 1.0, 0.0).astype(BF)
        total = total + mm(fv[s], pick)
        tile = fv[s].astype(F32)
        for r in range(3):
            binner[0:1, 128 * (3 * s + r) : 128 * (3 * s + r + 1)] = tile[8 + r : 9 + r]
    rows[...] = total[0:8]


HIER = (True, False, True, False)
GATHER_COPIES = sum(16 if hier else 7 for hier in HIER) + 7


def gather_net(p, own, fa, fi, fo, vec, fv, ssem, rsem):
    net = Net(ssem, rsem)
    units = (slice(0, 3), slice(3, 4), slice(4, 8), slice(8, 12))
    every = (slice(None), slice(None))

    def piece(g, s, part):
        if g < 2:
            return fa.at[(units[g], s, *part)]
        return fi.at[(slice(None), s, *part)] if g == 2 else fo.at[(s, slice(None), *part)]

    for g in range(4):
        mine = quarter(p.w) if HIER[g] else every
        first = quarter(p.wa)

        def add(name, src, dst, device):
            net.define((g, *name), lambda: (src(), dst(), device))

        def same(name, g, s, part, device):
            add(name, lambda: piece(g, s, part), lambda: piece(g, s, part), device)

        add(("zb",), lambda g=g, mine=mine: own.at[(units[g], *mine)], lambda g=g, mine=mine: piece(g, p.s, mine), p.ring_a)
        add(("za",), lambda g=g, mine=mine: own.at[(units[g], *mine)], lambda g=g, mine=mine: piece(g, p.s, mine), p.ring_b)
        same(("zo",), g, p.sb, mine, p.ring_a)
        add(("own", "c"), lambda g=g: own.at[units[g]], lambda g=g: piece(g, p.s, every), p.sib)
        for name, s in (("zb", p.sb), ("za", p.sa), ("zo", p.so)):
            if HIER[g]:
                same((name, "xa"), g, s, mine, p.plane_a)
                same((name, "xb"), g, s, mine, p.plane_b)
                same((name, "xd"), g, s, first, p.plane_b)
            same((name, "c"), g, s, every, p.sib)
    for k in range(1, 8):
        net.define(("v", k), lambda k=k: (vec, fv.at[p.s], (p.w, lax.rem(p.s + k, 8))))
    assert len(net.made) == GATHER_COPIES
    return net


def forward_kernel(
    x, seg, kept, wq, wk, wv, wo, wi, wr, vec,
    fi, fo, fa_out, qkv_out, att_out, inv_out, e_out, t1_out, rows, binner,
    own, fa, fv, qkv, att, inv, t1, segt, ebuf, ssem, rsem, lsem, esem,
):
    p = Place()
    for c in range(3):
        for part, ref in enumerate((wq, wk, wv)):
            own[c, :, part * CW : (part + 1) * CW] = ref[:, c * CW : (c + 1) * CW].astype(BF)
    greet(p, others(p))
    net = gather_net(p, own, fa, fi, fo, vec, fv, ssem, rsem)
    names = ("zb", "za", "zo")
    net.start((0, "zb"), (0, "za"), (0, "own", "c"))
    own[3] = wo[...].astype(BF)
    for q in range(4):
        own[4 + q] = wi[:, q * D : (q + 1) * D].astype(BF)
        own[8 + q] = wr[q * TR : (q + 1) * TR, :].astype(BF)
    net.start(*[("v", k) for k in range(1, 8)])
    local = {}

    def put(name, k, src, dst):
        local[name] = lambda: pltpu.make_async_copy(src(), dst(), lsem.at[k])

    put("own a", 0, lambda: own.at[0:4], lambda: fa.at[:, p.s])
    put("own i", 1, lambda: own.at[4:8], lambda: fi.at[:, p.s])
    put("own o", 2, lambda: own.at[8:12], lambda: fo.at[p.s])
    put("vec", 3, lambda: vec, lambda: fv.at[p.s])
    put("qkv", 4, lambda: qkv, lambda: qkv_out)
    put("fa", 5, lambda: fa, lambda: fa_out)
    put("att", 6, lambda: att, lambda: att_out)
    put("inv", 7, lambda: inv, lambda: inv_out)
    put("t1", 8, lambda: t1, lambda: t1_out)
    for name in ("own a", "own i", "own o", "vec"):
        local[name]().start()

    def ring1(g):
        net.wait((g, "zb"))
        net.start((g, "zo"))
        if HIER[g]:
            net.start((g, "zb", "xa"), (g, "zb", "xb"))
        net.wait((g, "za"))
        if HIER[g]:
            net.start((g, "za", "xa"), (g, "za", "xb"))

    def ring2(g):
        net.wait((g, "zo"))
        if HIER[g]:
            net.start((g, "zo", "xa"), (g, "zo", "xb"))

    def relay(g, name):
        net.wait((g, name, "xa"))
        net.start((g, name, "xd"))

    def share(g, name):
        if HIER[g]:
            net.wait((g, name, "xb"), (g, name, "xd"))
        net.start((g, name, "c"))

    def landed(g):
        net.wait((g, "own", "c"), *[(g, name, "c") for name in names])

    ring1(0)
    net.start((2, "zb"), (2, "za"), (1, "zb"), (1, "za"), (1, "own", "c"), (2, "own", "c"), (3, "own", "c"))
    ring2(0)
    turn_ids(seg, segt)
    relay(0, "zb")
    relay(0, "za")
    share(0, "zb")
    net.start((3, "zb"), (3, "za"))
    relay(0, "zo")
    share(0, "za")
    net.wait(*[("v", k) for k in range(1, 8)])
    local["vec"]().wait()
    expand_vectors(fv, rows, binner)
    share(0, "zo")
    ring1(2)
    ring1(1)
    local["own a"]().wait()
    landed(0)

    project(x, fa, rows, qkv)
    local["qkv"]().start()
    ring2(2)
    ring2(1)
    for name in names:
        share(1, name)
    keep = kept[0]

    def out_copy(i, slot):
        c, r, pair = place_of(i)
        return pltpu.make_async_copy(ebuf.at[slot], e_out.at[c, r, pair], esem.at[slot])

    steps = {
        0: lambda: relay(2, "zb"),
        1: lambda: relay(2, "za"),
        2: lambda: (share(2, "zb"), ring1(3)),
        3: lambda: relay(2, "zo"),
        4: lambda: share(2, "za"),
        6: lambda: (share(2, "zo"), share(3, "zb"), share(3, "za")),
        9: lambda: (ring2(3), share(3, "zo")),
    }

    def one(i, _):
        slot = lax.rem(i, 2)

        @pl.when(i >= 2)
        def _():
            out_copy(i - 2, slot).wait()

        attend(i, qkv, seg, segt, keep, att, inv, ebuf.at[slot])
        out_copy(i, slot).start()
        for k, step in steps.items():
            @pl.when(i == k)
            def _(step=step):
                step()
        return 0

    n = 6 * (x.shape[0] // SEQ)
    lax.fori_loop(0, n, one, 0)
    local["att"]().start()
    local["inv"]().start()
    landed(1)
    local["fa"]().start()

    def last(i, _):
        at = rows_of(i, 256)
        t1[at] = x[at].astype(F32) + (mm(att[at], fa[3].reshape(D, D)) + rows[2:3])
        return 0

    lax.fori_loop(0, x.shape[0] // 256, last, 0)
    local["t1"]().start()
    out_copy(n - 2, (n - 2) % 2).wait()
    out_copy(n - 1, (n - 1) % 2).wait()
    landed(2)
    landed(3)
    for name in ("own i", "own o", "qkv", "fa", "att", "inv", "t1"):
        local[name]().wait()
    net.finish()


def forward(x, seg, kept, wq, wk, wv, wo, wi, wr, vec):
    t = x.shape[0]
    n = t // SEQ
    return pl.pallas_call(
        forward_kernel,
        out_shape=(
            shape(4, 8, TR, D), shape(8, 4, TR, D), shape(4, 8, TR, D), shape(3, t, D), shape(t, D), shape(t, D, dtype=F32),
            shape(3, n, 2, 2, SEQ, SEQ), shape(t, D, dtype=F32), shape(8, D, dtype=F32), shape(1, FF, dtype=F32),
        ),
        in_specs=[VM, VM, SM] + [VM] * 7,
        out_specs=(ANY,) * 8 + (VM, VM),
        scratch_shapes=[
            pltpu.VMEM((12, TR, D), BF),
            pltpu.VMEM((4, 8, TR, D), BF),
            pltpu.VMEM((8, 16, 128), BF),
            pltpu.VMEM((3, t, D), BF),
            pltpu.VMEM((t, D), BF),
            pltpu.VMEM((t, D), F32),
            pltpu.VMEM((t, D), F32),
            pltpu.VMEM((n, SEQ, 128), F32),
            pltpu.VMEM((2, 2, SEQ, SEQ), BF),
            pltpu.SemaphoreType.DMA((GATHER_COPIES,)),
            pltpu.SemaphoreType.DMA((GATHER_COPIES,)),
            pltpu.SemaphoreType.DMA((9,)),
            pltpu.SemaphoreType.DMA((2,)),
        ],
        compiler_params=params(collective_id=0, has_side_effects=True),
        name="forward",
    )(x, seg, kept, wq, wk, wv, wo, wi, wr, vec)


def ffn_kernel(
    t1, grad, rows, binner, kept, inv, fi, fo, fa,
    y, res, bg, dos, sums, bsum, g_out,
    wi, wr, wo, hl, act, ig, og, gp, gbuf, lsem, gsem, block=256,
):
    load = [
        pltpu.make_async_copy(fi, wi, lsem.at[0]),
        pltpu.make_async_copy(fo, wr, lsem.at[1]),
        pltpu.make_async_copy(fa.at[3], wo, lsem.at[2]),
    ]
    for copy in load:
        copy.start()
    keep_heads = kept[0]
    b_outer, gain_two, shift_two = rows[5:6], rows[6:7], rows[7:8]
    gain_one, shift_one = rows[3:4], rows[4:5]
    sums[...] = jnp.zeros_like(sums)
    bsum[...] = jnp.zeros_like(bsum)
    heads = column_mask(keep_heads, (1, D), HEAD_DIM)
    for copy in load:
        copy.wait()

    def add(k, value):
        sums[k : k + 1] += jnp.sum(value, axis=0, keepdims=True)

    def inner_weight(j):
        return wi[j].reshape(D, D)

    def outer_weight(j):
        return wr[2 * j : 2 * j + 2].reshape(D, D)

    def one(i, _):
        at = rows_of(i, block)
        n1, inv1 = norm_rows(t1[at])
        hidden = n1 * gain_one + shift_one
        low = hidden.astype(BF)
        hl[at] = low
        outer = jnp.zeros((block, D), F32)
        for j in range(4):
            cols = slice(j * D, (j + 1) * D)
            inner = mm(low, inner_weight(j)) + binner[:, cols]
            keep = column_mask(keep_heads * 256 - j * D, (1, D), 1)
            phi = 0.5 + 0.5 * lax.erf(inner * RSQRT2)
            masked = inner * keep
            a = (masked * phi).astype(BF)
            gp[:, cols] = (keep * phi + masked * (RSQRT2PI * jnp.exp(-0.5 * (inner * inner)))).astype(BF)
            act[at, cols] = a
            outer = outer + mm(a, outer_weight(j))
        n2, inv2 = norm_rows(hidden + (outer + b_outer))
        y[at] = (n2 * gain_two + shift_two).astype(BF)
        top = grad[at].astype(F32)
        add(7, top)
        add(6, top * n2)
        res2 = norm_back(top * gain_two, n2, inv2)
        o = res2.astype(BF)
        og[at] = o
        add(5, o.astype(F32))
        hg = res2
        for j in range(4):
            cols = slice(j * D, (j + 1) * D)
            g = (mm(o, outer_weight(j), NT) * gp[:, cols].astype(F32)).astype(BF)
            ig[at, cols] = g
            bsum[:, cols] += jnp.sum(g.astype(F32), axis=0, keepdims=True)
            hg = hg + mm(g, inner_weight(j), NT)
        add(4, hg)
        n1, inv1 = norm_rows(t1[at])
        add(3, hg * n1)
        res1 = norm_back(hg * gain_one, n1, inv1)
        res[at] = res1
        b = res1.astype(BF)
        bg[at] = b
        add(2, b.astype(F32))
        dos[at] = (mm(b, wo[...].reshape(D, D), NT) * (inv[at] * heads)).astype(BF)
        return 0

    lax.fori_loop(0, t1.shape[0] // block, one, 0)

    def outer_out(j):
        return pltpu.make_async_copy(gbuf.at[j], g_out.at[lax.div(j, 2), pl.ds(2 * lax.rem(j, 2), 2), 0:4], gsem.at[j])

    def inner_out(j):
        return pltpu.make_async_copy(gbuf.at[4 + j], g_out.at[:, :, 4 + j], gsem.at[4 + j])

    def two(j, _):
        cols = rows_of(j, D)
        gbuf[j] = mm(act[:, cols], og[...], TN).astype(BF).reshape(2, 4, TR, D)
        outer_out(j).start()
        return 0

    lax.fori_loop(0, 4, two, 0)

    def three(j, _):
        cols = rows_of(j, D)
        gbuf[4 + j] = mm(hl[...], ig[:, cols], TN).astype(BF).reshape(2, 4, TR, D)
        inner_out(j).start()
        return 0

    lax.fori_loop(0, 4, three, 0)
    for j in range(4):
        outer_out(j).wait()
        inner_out(j).wait()


def ffn(t1, grad, rows, binner, kept, inv, fi, fo, fa):
    t = t1.shape[0]
    return pl.pallas_call(
        ffn_kernel,
        out_shape=(
            shape(t, D), shape(t, D, dtype=F32), shape(t, D), shape(t, D),
            shape(8, D, dtype=F32), shape(1, FF, dtype=F32), shape(2, 4, 8, TR, D),
        ),
        in_specs=[VM] * 4 + [SM, VM] + [ANY] * 3,
        out_specs=(VM,) * 6 + (ANY,),
        scratch_shapes=[
            pltpu.VMEM((4, 8, TR, D), BF),
            pltpu.VMEM((8, 4, TR, D), BF),
            pltpu.VMEM((8, TR, D), BF),
            pltpu.VMEM((t, D), BF),
            pltpu.VMEM((t, FF), BF),
            pltpu.VMEM((t, FF), BF),
            pltpu.VMEM((t, D), BF),
            pltpu.VMEM((256, FF), BF),
            pltpu.VMEM((8, 2, 4, TR, D), BF),
            pltpu.SemaphoreType.DMA((3,)),
            pltpu.SemaphoreType.DMA((8,)),
        ],
        compiler_params=params(),
        name="ffn",
    )(t1, grad, rows, binner, kept, inv, fi, fo, fa)


def attend_back(i, qkv, dos, att, ebuf, dqkv):
    c, r, pair = place_of(i)
    rows = rows_of(r, SEQ)
    lanes = pl.ds(pl.multiple_of(c * CW + pair * 128, 128), 128)
    qp, kp, vp = (qkv[c, rows, pair_lanes(pair, part)] for part in range(3))
    dp = dos[rows, lanes]
    low = low_lanes(SEQ)
    zero = jnp.zeros_like(qp)
    product = dp.astype(F32) * att[rows, lanes].astype(F32)
    gq = jnp.zeros((SEQ, 128), F32)
    gk = jnp.zeros((SEQ, 128), F32)
    gv = jnp.zeros((SEQ, 128), F32)
    for h in range(2):
        mine = low if h == 0 else jnp.logical_not(low)
        dh = jnp.where(mine, dp, zero)
        delta = jnp.sum(jnp.where(mine, product, 0.0), axis=1, keepdims=True)
        e = ebuf[h]
        ds = (e.astype(F32) * (mm(dh, vp, NT) - delta)).astype(BF)
        gv = gv + mm(e, dh, TN)
        gk = gk + mm(ds, jnp.where(mine, qp, zero), TN)
        gq = gq + mm(ds, jnp.where(mine, kp, zero))
    dqkv[c, rows, pair_lanes(pair, 0)] = (gq * 0.125).astype(BF)
    dqkv[c, rows, pair_lanes(pair, 1)] = gk.astype(BF)
    dqkv[c, rows, pair_lanes(pair, 2)] = gv.astype(BF)


def chunk_grads(c, x, dqkv, gx, sums):
    gx[c] = mm(x[...], dqkv[c], TN).astype(BF).reshape(4, 2, 1, TR, D)
    part = dqkv[c].astype(F32)
    total = jnp.sum(part, axis=0, keepdims=True)
    lanes = pl.ds(pl.multiple_of(c * CW, CW), CW)
    sums[0:1, lanes] = total[:, 0:CW]
    sums[1:2, lanes] = total[:, 2 * CW :]


def input_back(res, dqkv, fa, out, block=256):
    def one(i, _):
        at = rows_of(i, block)
        total = res[at]
        for c in range(3):
            total = total + mm(dqkv[c, at], fa[c].reshape(D, D), NT)
        out[at] = total.astype(BF)
        return 0

    lax.fori_loop(0, res.shape[0] // block, one, 0)


JOBS = ((0, 4, True), (4, 4, False), (8, 1, True), (9, 1, False), (10, 1, True), (11, 1, False))
REDUCE_COPIES = 10 * len(JOBS) + 7
JOB_BUFFERS = 7


def job_shapes(units, ring_first):
    big, part, tile = (4, units, TR, D), (units, 48, 384), (units, TR, D)
    first = tile if ring_first else (4, *part)
    return [big, big, first, first, first, first, part, part, part]


class Job:
    def __init__(self, net, p, k, first, units, ring_first, source, bufs, result):
        self.net, self.p, self.k, self.ring_first = net, p, k, ring_first
        self.held, self.landed, self.d1, self.a1, self.b1, self.mid, self.d2, self.a2, self.b2 = bufs
        self.result = result
        self.units = slice(first, first + units)
        held, mid = self.held, self.mid
        z, za, zb, zo = p.z, lax.div(p.sa, 2), lax.div(p.sb, 2), lax.div(p.so, 2)
        self.z = z
        ring = (za, zb, zo, p.ring_a, p.ring_a, p.ring_b)
        plane = (p.wb, p.wa, p.wd, p.plane_a, p.plane_b, p.plane_a)

        def tile(t):
            return held, (t,)

        def plane_quarter(w):
            return held, (slice(None), slice(None), *quarter(w))

        def mid_quarter(w):
            return mid, (slice(None), *quarter(w))

        def mid_tile(t):
            return mid, (t,)

        one, two = (ring, plane) if ring_first else (plane, ring)
        self.at1, self.at2 = (tile, mid_quarter) if ring_first else (plane_quarter, mid_tile)
        self.one, self.two = one, two
        self.own1 = z if ring_first else p.w
        self.own2 = p.w if ring_first else z
        net.define((k, "c"), lambda: (source(1 - p.c), self.landed, p.sib))
        for stage, at, way, d, a, b in ((1, self.at1, one, self.d1, self.a1, self.b1), (2, self.at2, two, self.d2, self.a2, self.b2)):
            relayed, direct, opposite, dev_o, dev_r, dev_d = way

            def send(name, index, dst, device, at=at):
                def make():
                    ref, where = at(index)
                    return ref.at[where], dst, device

                net.define((k, name), make)

            send(("d", stage), opposite, d, dev_o)
            send(("b", stage), direct, b, dev_d)
            send(("a", stage), relayed, a, dev_r)

        def share(name, w, device):
            def make():
                ref = result.at[(self.units, *quarter(w))]
                return ref, ref, device

            net.define((k, name), make)

        share("ga", p.w, p.plane_a)
        share("gb", p.w, p.plane_b)
        share("gd", p.wa, p.plane_b)

    def start(self, *names):
        self.net.start(*[(self.k, name) for name in names])

    def wait(self, *names):
        self.net.wait(*[(self.k, name) for name in names])

    def send(self):
        self.start("c")

    def pair(self):
        self.wait("c")
        held, landed = self.held, self.landed

        def one(t, _):
            held[t] = (held[t].astype(F32) + landed[t].astype(F32)).astype(BF)
            return 0

        lax.fori_loop(0, 4, one, 0)
        self.start(("d", 1), ("b", 1))

    def relay(self, stage):
        at, way, d = (self.at1, self.one, self.d1) if stage == 1 else (self.at2, self.two, self.d2)
        self.wait(("d", stage))
        ref, where = at(way[0])
        ref[where] = (ref[where].astype(F32) + d[...].astype(F32)).astype(BF)
        self.start(("a", stage))

    def total(self, stage):
        at, own, a, b = (self.at1, self.own1, self.a1, self.b1) if stage == 1 else (self.at2, self.own2, self.a2, self.b2)
        self.wait(("a", stage), ("b", stage))
        ref, where = at(own)
        return (ref[where].astype(F32) + a[...].astype(F32) + b[...].astype(F32)).astype(BF)

    def turn(self):
        self.mid[...] = self.total(1)
        self.start(("d", 2), ("b", 2))

    def share(self):
        self.result[(self.units, *quarter(self.p.w))] = self.total(2)
        self.start("ga", "gb")

    def pass_on(self):
        self.wait("ga")
        self.start("gd")

    def end(self):
        self.wait("gb", "gd")


def backward_kernel(
    x, qkv_in, e_in, att_in, dos_in, bg_in, res_in, fa_in, g_in, sums_in, bsum,
    out, result, ovec,
    qkv, att, dos, bg, res, fa, dqkv, gx, go, ebuf, sums, vt, vheld, vrecv, vplane, vz, *rest,
):
    bufs, (ssem, rsem, lsem, esem) = rest[:-4], rest[-4:]
    p = Place()
    n = 6 * (x.shape[0] // SEQ)
    load = {}

    def get(name, k, src, dst):
        load[name] = pltpu.make_async_copy(src, dst, lsem.at[k])
        load[name].start()

    def in_copy(i, slot):
        c, r, pair = place_of(i)
        return pltpu.make_async_copy(e_in.at[c, r, pair], ebuf.at[slot], esem.at[slot])

    jobs = []
    net = Net(ssem, rsem)
    g4 = g_in
    per = 9
    for k, (first, units, ring_first) in enumerate(JOBS):
        if k < 2:
            source = lambda core, first=first, units=units: g4.at[:, core, first : first + units]
        elif k == 2:
            source = lambda core: go.at[:, core]
        else:
            source = lambda core, c=k - 3: gx.at[c, :, core]
        jobs.append(Job(net, p, k, first, units, ring_first, source, bufs[per * k : per * (k + 1)], result))
    get("att", 0, att_in, att)
    get("bg", 1, bg_in, bg)
    get("h0", 2, g4.at[:, p.c, 0:4], jobs[0].held)
    get("h1", 3, g4.at[:, p.c, 4:8], jobs[1].held)
    get("qkv", 4, qkv_in, qkv)
    get("dos", 5, dos_in, dos)
    in_copy(0, 0).start()
    get("res", 6, res_in, res)
    get("fa", 7, fa_in.at[0:3], fa)
    net.define(("v", "c"), lambda: (vt.at[:, 1 - p.c], vrecv, p.sib))
    for k, device in enumerate((p.plane_a, p.plane_b, (p.wd, p.s))):
        net.define(("v", "p", k), lambda device=device: (vheld.at[0], vplane.at[p.w], device))
    for k in range(1, 4):
        to = lax.rem(p.z + k, 4)
        net.define(("v", "z", k), lambda to=to: (vheld.at[1, to], vz.at[p.z], (p.w, 2 * to + p.c)))
    assert len(net.made) == REDUCE_COPIES, len(net.made)

    greet(p, others(p))
    jobs[0].send()
    jobs[1].send()
    sums[...] = sums_in[...]
    load["att"].wait()
    load["bg"].wait()
    go[...] = mm(att[...], bg[...], TN).astype(BF).reshape(4, 2, 1, TR, D)
    jobs[2].send()
    load["h0"].wait()
    jobs[0].pair()
    load["h1"].wait()
    jobs[1].pair()

    def own_half(k, source):
        jobs[k].held[...] = source[:, p.c]

    own_half(2, go)
    load["qkv"].wait()
    load["dos"].wait()
    jobs[2].pair()

    def begin(k):
        own_half(k, gx.at[k - 3])
        jobs[k].pair()

    a, b, w, c0, c1, c2 = jobs
    steps = {
        2: lambda: w.relay(1),
        3: lambda: c0.send(),
        4: lambda: (b.relay(1), begin(3), w.turn()),
        5: lambda: a.relay(1),
        6: lambda: (w.relay(2), c0.relay(1)),
        7: lambda: (c1.send(), w.share()),
        8: lambda: (b.turn(), begin(4), c0.turn()),
        9: lambda: (a.turn(), b.relay(2), w.pass_on()),
        10: lambda: (c1.relay(1), c0.relay(2), b.share()),
        11: lambda: (c2.send(), a.relay(2), c0.share(), c1.turn()),
    }

    def one(i, _):
        slot = lax.rem(i, 2)

        @pl.when(i + 1 < n)
        def _():
            in_copy(i + 1, 1 - slot).start()

        in_copy(i, slot).wait()
        attend_back(i, qkv, dos, att, ebuf.at[slot], dqkv)

        @pl.when(lax.rem(i, 4) == 3)
        def _():
            chunk_grads(lax.div(i, 4), x, dqkv, gx, sums)

        for k, step in steps.items():
            @pl.when(i == k)
            def _(step=step):
                step()
        return 0

    lax.fori_loop(0, n, one, 0)

    for s in range(8):
        vt[s // 2, s % 2] = jnp.zeros((16, 128), F32)
        vt[s // 2, s % 2, 0:8, 0:TR] = sums[:, TR * s : TR * (s + 1)]
        for r in range(3):
            vt[s // 2, s % 2, 8 + r : 9 + r] = bsum[0:1, 128 * (3 * s + r) : 128 * (3 * s + r + 1)]
    net.start(("v", "c"))
    begin(5)
    a.share()
    b.pass_on()
    c0.pass_on()
    c1.relay(2)
    net.wait(("v", "c"))
    vheld[0] = vt[:, p.c] + vrecv[...]
    vplane[p.w] = vheld[0]
    net.start(*[("v", "p", k) for k in range(3)])
    load["res"].wait()
    load["fa"].wait()
    c2.relay(1)

    def back(i):
        at = pl.ds(256 * i, 256)
        total = res[at]
        for c in range(3):
            total = total + mm(dqkv[c, at], fa[c].reshape(D, D), NT)
        out[at] = total.astype(BF)

    back(0)
    a.pass_on()
    c1.share()
    c2.turn()
    net.wait(*[("v", "p", k) for k in range(3)])
    vheld[1] = (vplane[0] + vplane[1]) + (vplane[2] + vplane[3])
    vz[p.z] = vheld[1, p.z]
    net.start(*[("v", "z", k) for k in range(1, 4)])
    back(1)
    c1.pass_on()
    c2.relay(2)
    back(2)
    c2.share()
    back(3)
    net.wait(*[("v", "z", k) for k in range(1, 4)])
    ovec[...] = (vz[0] + vz[1]) + (vz[2] + vz[3])
    c2.pass_on()
    for job in jobs:
        job.end()
    net.finish()


def backward(x, qkv, e, att, dos, bg, res, fa, g, sums, bsum):
    t = x.shape[0]
    job_scratch = [pltpu.VMEM(s, BF) for _, units, ring_first in JOBS for s in job_shapes(units, ring_first)]
    return pl.pallas_call(
        backward_kernel,
        out_shape=(shape(t, D), shape(12, TR, D), shape(16, 128, dtype=F32)),
        in_specs=[VM] + [ANY] * 8 + [VM, VM],
        out_specs=(VM,) * 3,
        scratch_shapes=[
            pltpu.VMEM((3, t, D), BF),
            pltpu.VMEM((t, D), BF),
            pltpu.VMEM((t, D), BF),
            pltpu.VMEM((t, D), BF),
            pltpu.VMEM((t, D), F32),
            pltpu.VMEM((3, 8, TR, D), BF),
            pltpu.VMEM((3, t, D), BF),
            pltpu.VMEM((3, 4, 2, 1, TR, D), BF),
            pltpu.VMEM((4, 2, 1, TR, D), BF),
            pltpu.VMEM((2, 2, SEQ, SEQ), BF),
            pltpu.VMEM((8, D), F32),
            pltpu.VMEM((4, 2, 16, 128), F32),
            pltpu.VMEM((2, 4, 16, 128), F32),
            pltpu.VMEM((4, 16, 128), F32),
            pltpu.VMEM((4, 4, 16, 128), F32),
            pltpu.VMEM((4, 16, 128), F32),
        ]
        + job_scratch
        + [
            pltpu.SemaphoreType.DMA((REDUCE_COPIES,)),
            pltpu.SemaphoreType.DMA((REDUCE_COPIES,)),
            pltpu.SemaphoreType.DMA((8,)),
            pltpu.SemaphoreType.DMA((2,)),
        ],
        compiler_params=params(collective_id=1, has_side_effects=True),
        name="backward",
    )(x, qkv, e, att, dos, bg, res, fa, g.reshape(4, 2, 8, TR, D), sums, bsum)


def finish_kernel(result, ovec, inp, oq, ok, ov, oo, oi, our, out, *vectors):
    for c in range(3):
        tile = result[9 + c].astype(F32)
        for part, ref in enumerate((oq, ok, ov)):
            ref[:, c * CW : (c + 1) * CW] = tile[:, part * CW : (part + 1) * CW]
    oo[...] = result[8].astype(F32)
    for q in range(4):
        oi[:, q * D : (q + 1) * D] = result[4 + q].astype(F32)
        our[q * TR : (q + 1) * TR, :] = result[q].astype(F32)
    out[...] = inp[...]
    for k in range(8):
        vectors[k][...] = ovec[k, 0:TR]
    for r in range(3):
        vectors[8][128 * r : 128 * (r + 1)] = ovec[8 + r]


def finish(result, ovec, inp):
    t = inp.shape[0]
    return pl.pallas_call(
        finish_kernel,
        out_shape=tuple(shape(TR, D, dtype=F32) for _ in range(4))
        + (shape(TR, FF, dtype=F32), shape(4 * TR, D, dtype=F32), shape(t, D))
        + tuple(shape(TR, dtype=F32) for _ in range(8))
        + (shape(4 * TR, dtype=F32),),
        in_specs=[VM] * 3,
        out_specs=(VM,) * 16,
        compiler_params=params(),
        name="finish",
    )(result, ovec, inp)


def forward_local_kernel(x, seg, kept, fa, rows, qkv, att, inv, e_out, t1, segt, ebuf, esem):
    turn_ids(seg, segt)
    project(x, fa, rows, qkv)
    keep = kept[0]

    def one(i, _):
        c, r, pair = place_of(i)
        attend(i, qkv, seg, segt, keep, att, inv, ebuf)
        copy = pltpu.make_async_copy(ebuf, e_out.at[c, r, pair], esem.at[0])
        copy.start()
        copy.wait()
        return 0

    lax.fori_loop(0, 6 * (x.shape[0] // SEQ), one, 0)
    t1[...] = x[...].astype(F32) + (mm(att[...], fa[3].reshape(D, D)) + rows[2:3])


def forward_local(x, seg, kept, fa, rows):
    t = x.shape[0]
    n = t // SEQ
    return pl.pallas_call(
        forward_local_kernel,
        out_shape=(shape(3, t, D), shape(t, D), shape(t, D, dtype=F32), shape(3, n, 2, 2, SEQ, SEQ), shape(t, D, dtype=F32)),
        in_specs=[VM, VM, SM, VM, VM],
        out_specs=(VM, VM, VM, ANY, VM),
        scratch_shapes=[
            pltpu.VMEM((n, SEQ, 128), F32), pltpu.VMEM((2, SEQ, SEQ), BF), pltpu.SemaphoreType.DMA((1,)),
        ],
        compiler_params=params(),
        name="forward_local",
    )(x, seg, kept, fa, rows)


def backward_local_kernel(x, qkv, e_in, att, dos, bg, res, fa, sums_in, out, gx, go, sums, dqkv, ebuf, esem):
    sums[...] = sums_in[...]
    go[...] = mm(att[...], bg[...], TN).astype(BF).reshape(4, 2, 1, TR, D)

    def one(i, _):
        c, r, pair = place_of(i)
        copy = pltpu.make_async_copy(e_in.at[c, r, pair], ebuf, esem.at[0])
        copy.start()
        copy.wait()
        attend_back(i, qkv, dos, att, ebuf, dqkv)

        @pl.when(lax.rem(i, 4) == 3)
        def _():
            chunk_grads(lax.div(i, 4), x, dqkv, gx, sums)

        return 0

    lax.fori_loop(0, 6 * (x.shape[0] // SEQ), one, 0)
    input_back(res, dqkv, fa, out)


def backward_local(x, qkv, e, att, dos, bg, res, fa, sums):
    t = x.shape[0]
    return pl.pallas_call(
        backward_local_kernel,
        out_shape=(shape(t, D), shape(3, 4, 2, 1, TR, D), shape(4, 2, 1, TR, D), shape(8, D, dtype=F32)),
        in_specs=[VM, VM, ANY] + [VM] * 6,
        out_specs=(VM,) * 4,
        scratch_shapes=[pltpu.VMEM((3, t, D), BF), pltpu.VMEM((2, SEQ, SEQ), BF), pltpu.SemaphoreType.DMA((1,))],
        compiler_params=params(),
        name="backward_local",
    )(x, qkv, e, att, dos, bg, res, fa, sums)


def gather_lax(wq, wk, wv, wo, wi, wr, eight, b_inner):
    def whole(a):
        return lax.all_gather(a.astype(BF), "shard", axis=0, tiled=True)

    wq, wk, wv, wo, wi, wr = (whole(a) for a in (wq, wk, wv, wo, wi, wr))
    chunks = [jnp.concatenate([a[:, c * CW : (c + 1) * CW] for a in (wq, wk, wv)], axis=1) for c in range(3)]
    fa = jnp.stack(chunks + [wo]).reshape(4, 8, TR, D)
    fi = jnp.stack([wi[:, q * D : (q + 1) * D] for q in range(4)]).reshape(4, 8, TR, D)
    rows = jnp.stack([whole(a) for a in eight]).astype(F32)
    return fa, fi, wr.reshape(8, 4, TR, D), rows, whole(b_inner).astype(F32).reshape(1, FF)


def reduce_lax(g, gx, go, sums, bsum):
    g = g.reshape(8, 8, TR, D)
    gr = g[:, 0:4].reshape(FF, D)
    gi = jnp.concatenate([g[:, 4 + j].reshape(D, D) for j in range(4)], axis=1)
    gx = gx.reshape(3, D, 3, CW)
    squares = [jnp.concatenate([gx[c, :, part] for c in range(3)], axis=1) for part in range(3)]

    def owned(a):
        a = lax.psum_scatter(a.astype(F32), "shard", scatter_dimension=0, tiled=True)
        return lax.psum(a.astype(BF), "width").astype(F32)

    matrices = [owned(a) for a in (*squares, go.reshape(D, D), gi, gr)]
    return matrices, [owned(sums[k]) for k in range(8)] + [owned(bsum[0])]


def body(
    layer_input, segment_ids, group_heads,
    w_query, b_query, w_key, w_value, b_value, w_out, b_out, gain_one, shift_one,
    w_inner, b_inner, w_outer, b_outer, gain_two, shift_two, out_grad,
):
    eight = (b_query, b_value, b_out, gain_one, shift_one, b_outer, gain_two, shift_two)
    weights = (w_query, w_key, w_value, w_out, w_inner, w_outer)
    own_kernels = lax.axis_size("width") == 4 and lax.axis_size("shard") == 8
    if own_kernels:
        vec = jnp.concatenate([jnp.stack(eight), jnp.zeros((8, 128 - TR), F32)], axis=1)
        vec = jnp.concatenate([vec, b_inner.reshape(3, 128), jnp.zeros((5, 128), F32)], axis=0).astype(BF)
        fi, fo, fa, qkv, att, inv, e, t1, rows, binner = forward(layer_input, segment_ids, group_heads, *weights, vec)
    else:
        fa, fi, fo, rows, binner = gather_lax(*weights, eight, b_inner)
        qkv, att, inv, e, t1 = forward_local(layer_input, segment_ids, group_heads, fa, rows)
    y, res, bg, dos, sums, bsum, g = ffn(t1, out_grad, rows, binner, group_heads, inv, fi, fo, fa)
    if own_kernels:
        input_grad, result, ovec = backward(layer_input, qkv, e, att, dos, bg, res, fa, g, sums, bsum)
        gq, gk, gv, go, gi, gr, input_grad, *vectors = finish(result, ovec, input_grad)
    else:
        input_grad, gx, go, sums = backward_local(layer_input, qkv, e, att, dos, bg, res, fa[0:3], sums)
        (gq, gk, gv, go, gi, gr), vectors = reduce_lax(g, gx, go, sums, bsum)
    return (
        y, input_grad, gq, vectors[0], gk, gv, vectors[1], go, vectors[2],
        vectors[3], vectors[4], gi, vectors[8], gr, vectors[5], vectors[6], vectors[7],
    )


def solution(mesh):
    placed = (
        P(("width", "shard"), None),
        P(("width", "shard"), None),
        P("width"),
        P("shard", None),
        P("shard"),
        P("shard", None),
        P("shard", None),
        P("shard"),
        P("shard", None),
        P("shard"),
        P("shard"),
        P("shard"),
        P("shard", None),
        P("shard"),
        P("shard", None),
        P("shard"),
        P("shard"),
        P("shard"),
        P(("width", "shard"), None),
    )
    return jax.shard_map(
        body,
        mesh=mesh,
        in_specs=placed,
        out_specs=(
            P(("width", "shard"), None),
            P(("width", "shard"), None),
            P("shard", None),
            P("shard"),
            P("shard", None),
            P("shard", None),
            P("shard"),
            P("shard", None),
            P("shard"),
            P("shard"),
            P("shard"),
            P("shard", None),
            P("shard"),
            P("shard", None),
            P("shard"),
            P("shard"),
            P("shard"),
        ),
        check_vma=False,
    )
```

time: 707 us -> 273 us (0.39)
  waiting for transfers between devices: 303 us -> 0 us
  Pallas kernels: 0 us -> 267 us
  matrix products: 194 us -> 0 us
  blocking collectives: 79.6 us -> 0 us
  other arithmetic: 60 us -> 4.05 us
  local copies, waits for them, and re-layouts: 47.5 us -> 0.11 us
  between operations: 17.9 us -> 1.49 us
    pallas_call x0 -> x4, Pallas kernels: none -> 267 us  [the longest x1 118 us: backward(): pl.pallas_call(backward_kernel, out_shape=(shape(t, D), shape(12, TR, D),...]
    reduce_scatter x3 -> x0, waiting for transfers between devices: 197 us -> none  [the longest x1 99.4 us: body(): lax.psum_scatter(w_inner_grad, 'shard', scatter_dimension=0, tiled=True)]
    dot_general x30 -> x0, matrix products: 194 us -> none  [the longest x6 60.8 us: forward_product(): return jnp.dot(rows_in, weight, preferred_element_type=jnp.float32)]
    all_gather x6 -> x0, waiting for transfers between devices: 65.4 us -> none  [the longest x1 46.7 us: body(): lax.all_gather(to_half(w_inner), 'shard', axis=0, tiled=True)]
    unnamed x2 -> x0, blocking collectives: 56.9 us -> none
    unnamed x190 -> x0, local copies, waits for them, and re-layouts: 45.9 us -> none
    convert_element_type x44 -> x0, other arithmetic: 44.8 us -> none  [the longest x18 27.5 us: to_half(): return value.astype(jnp.bfloat16)]
    unnamed x16 -> x0, waiting for transfers between devices: 31.4 us -> none
  transfers between devices with their start and end apart: 13 -> 0, of which waited for: 7 -> 0; matrix products, arithmetic and copies ran while one was open for 32% -> 0% of each run, Pallas kernels for 0% -> 0%
where the time goes in v3:
time: 273 us; the launch traced here: 272 us
  Pallas kernels  267 us (98%)
  other arithmetic  4.05 us (1%)
    pallas_call x1, Pallas kernels, backward(): pl.pallas_call(backward_kernel, out_shape=(shape(t, D), shape(12, TR, D),...  118 us
    pallas_call x1, Pallas kernels, forward(): pl.pallas_call(forward_kernel, out_shape=(shape(4, 8, TR, D), shape(8, 4,...  91.6 us
    pallas_call x1, Pallas kernels, ffn(): pl.pallas_call(ffn_kernel, out_shape=(shape(t, D), shape(t, D, dtype=F32)...  53.1 us

profile of v3, /device:TPU:0, one launch (start us, length us, event | category | flops | bytes accessed | tf_op | source)
XLA Modules:
  0.0 272.3 jit_solution(16835196079943202435)
XLA Ops:
  1.3 0.1 pad.4.clone
  1.4 0.7 convert_bitcast_fusion
  2.1 0.7 convert_bitcast_fusion.7
  2.7 0.7 convert_bitcast_fusion.5
  3.4 0.7 convert_bitcast_fusion.3
  4.1 0.7 convert_bitcast_fusion.1
  4.8 0.7 fusion.2.vec
  5.5 91.6 %forward.1 = (bf16[4,8,96,768]{3,2,1,0:T(8,128)(2,1)}, bf16[8,4,96,768]{3,2,1,0:T(8,128)(2,1)}, bf16[4,8,96,768]{3,2,1,0:T(8,128)(2,1)}, bf16[3,1024,768]{2,1,0:...) custom-call(bf16[1024,768]{1,0:T(8,128)(2,1)} %x.5, ...), custom_call_target="tpu_custom_call" | custom-call | tf_op jit(solution)/shard_map/forward/pallas_call | solution.py:392
  97.1 53.1 %ffn.1 = (bf16[1024,768]{1,0:T(8,128)(2,1)}, f32[1024,768]{1,0:T(8,128)}, bf16[1024,768]{1,0:T(8,128)(2,1)}, bf16[1024,768]{1,0:T(8,128)(2,1)}, f32[8,768]{1,0:T...) custom-call(f32[1024,768]{1,0:T(8,128)} %get-tuple-element.53.t1, bf16[1024,768]{1,0:T(8,128)(2,1)} %grad.1, ...), custom_call_target="tpu_custom_call" | custom-call | tf_op jit(solution)/shard_map/ffn/pallas_call | solution.py:524
  150.2 117.6 %backward.1 = (bf16[1024,768]{1,0:T(8,128)(2,1)}, bf16[12,96,768]{2,1,0:T(8,128)(2,1)}, f32[16,128]{1,0:T(8,128)}) custom-call(bf16[1024,768]{1,0:T(8,128)(2,1)} %x.5, bf16[3,1024,768]{2,1,0:T(8,128)(2,1)} %get-tuple-element.61.qkv_in, bf16[3,2,2,2,512,512]{5,4,3,2,1,0:T(8,128)(2,1)} %get-tuple-element.62.e_in, bf16[1024,768]{1,0:T(8,128)(2,1)} %get-tuple-element.63.att_in, ...), custom_call_target="tpu_custom_call" | custom-call | tf_op jit(solution)/shard_map/backward/pallas_call | solution.py:871
  267.8 4.3 %finish.1 = (f32[96,768]{1,0:T(8,128)}, f32[96,768]{1,0:T(8,128)}, f32[96,768]{1,0:T(8,128)}, f32[96,768]{1,0:T(8,128)}, f32[96,3072]{1,0:T(8,128)}, /*index=5*/...) custom-call(bf16[12,96,768]{2,1,0:T(8,128)(2,1)} %get-tuple-element., ...), custom_call_target="tpu_custom_call" | custom-call | tf_op jit(solution)/shard_map/finish/pallas_call | solution.py:924
  (2 shorter events, 0.0 us)

commit v4 on v3

--- a/solution.py
+++ b/solution.py
@@ -54,11 +54,14 @@
         self.ring_a, self.ring_b = (w, self.sa), (w, self.sb)
 
 
-def greet(p, devices):
+def call(devices):
     barrier = pltpu.get_barrier_semaphore()
     for device in devices:
         pl.semaphore_signal(barrier, inc=1, device_id=device, device_id_type=MESH)
-    pl.semaphore_wait(barrier, len(devices))
+
+
+def answer(devices):
+    pl.semaphore_wait(pltpu.get_barrier_semaphore(), len(devices))
 
 
 def others(p):
@@ -67,7 +70,7 @@
 
 class Net:
     def __init__(self, send, recv):
-        self.send, self.recv, self.made = send, recv, {}
+        self.send, self.recv, self.made, self.sent = send, recv, {}, set()
 
     def define(self, name, make):
         assert name not in self.made
@@ -91,7 +94,8 @@
 
     def finish(self):
         for name in self.made:
-            self.copy(name).wait_send()
+            if name not in self.sent:
+                self.copy(name).wait_send()
 
 
 def quarter(w):
@@ -136,20 +140,14 @@
     return pl.ds(pl.multiple_of(part * CW + pair * 128, 128), 128)
 
 
-def chunk_bias(rows, c):
-    lanes = slice(c * CW, (c + 1) * CW)
-    return jnp.concatenate([rows[0:1, lanes], jnp.zeros((1, CW), F32), rows[1:2, lanes]], axis=1)
-
-
-def project(x, fa, rows, qkv, block=256):
+def project(c, x, fa, rows, qkv, block=256):
+    lanes = pl.ds(pl.multiple_of(c * CW, CW), CW)
+    bias = jnp.concatenate([rows[0:1, lanes], jnp.zeros((1, CW), F32), rows[1:2, lanes]], axis=1)
     scale = jnp.where(lax.broadcasted_iota(jnp.int32, (1, D), 1) < CW, 0.125, 1.0)
 
     def one(i, _):
         at = rows_of(i, block)
-        xb = x[at]
-        for c in range(3):
-            weight = fa[c].reshape(D, D)
-            qkv[c, at] = ((mm(xb, weight) + chunk_bias(rows, c)) * scale).astype(BF)
+        qkv[c, at] = ((mm(x[at], fa[c].reshape(D, D)) + bias) * scale).astype(BF)
         return 0
 
     lax.fori_loop(0, x.shape[0] // block, one, 0)
@@ -206,23 +204,22 @@
     rows[...] = total[0:8]
 
 
-HIER = (True, False, True, False)
-GATHER_COPIES = sum(16 if hier else 7 for hier in HIER) + 7
+GROUPS = (slice(0, 1), slice(1, 2), slice(2, 3), slice(3, 4), slice(4, 8), slice(8, 12))
+WO, INNER, OUTER = 3, 4, 5
+GATHER_COPIES = 16 * len(GROUPS) + 7
 
 
 def gather_net(p, own, fa, fi, fo, vec, fv, ssem, rsem):
     net = Net(ssem, rsem)
-    units = (slice(0, 3), slice(3, 4), slice(4, 8), slice(8, 12))
     every = (slice(None), slice(None))
 
     def piece(g, s, part):
-        if g < 2:
-            return fa.at[(units[g], s, *part)]
-        return fi.at[(slice(None), s, *part)] if g == 2 else fo.at[(s, slice(None), *part)]
-
-    for g in range(4):
-        mine = quarter(p.w) if HIER[g] else every
-        first = quarter(p.wa)
+        if g <= WO:
+            return fa.at[(GROUPS[g], s, *part)]
+        return fi.at[(slice(None), s, *part)] if g == INNER else fo.at[(s, slice(None), *part)]
+
+    mine, first = quarter(p.w), quarter(p.wa)
+    for g in range(len(GROUPS)):
 
         def add(name, src, dst, device):
             net.define((g, *name), lambda: (src(), dst(), device))
@@ -230,15 +227,14 @@
         def same(name, g, s, part, device):
             add(name, lambda: piece(g, s, part), lambda: piece(g, s, part), device)
 
-        add(("zb",), lambda g=g, mine=mine: own.at[(units[g], *mine)], lambda g=g, mine=mine: piece(g, p.s, mine), p.ring_a)
-        add(("za",), lambda g=g, mine=mine: own.at[(units[g], *mine)], lambda g=g, mine=mine: piece(g, p.s, mine), p.ring_b)
+        for name, device in (("zb", p.ring_a), ("za", p.ring_b)):
+            add((name,), lambda g=g: own.at[(GROUPS[g], *mine)], lambda g=g: piece(g, p.s, mine), device)
         same(("zo",), g, p.sb, mine, p.ring_a)
-        add(("own", "c"), lambda g=g: own.at[units[g]], lambda g=g: piece(g, p.s, every), p.sib)
+        add(("own", "c"), lambda g=g: own.at[GROUPS[g]], lambda g=g: piece(g, p.s, every), p.sib)
         for name, s in (("zb", p.sb), ("za", p.sa), ("zo", p.so)):
-            if HIER[g]:
-                same((name, "xa"), g, s, mine, p.plane_a)
-                same((name, "xb"), g, s, mine, p.plane_b)
-                same((name, "xd"), g, s, first, p.plane_b)
+            same((name, "xa"), g, s, mine, p.plane_a)
+            same((name, "xb"), g, s, mine, p.plane_b)
+            same((name, "xd"), g, s, first, p.plane_b)
             same((name, "c"), g, s, every, p.sib)
     for k in range(1, 8):
         net.define(("v", k), lambda k=k: (vec, fv.at[p.s], (p.w, lax.rem(p.s + k, 8))))
@@ -246,19 +242,110 @@
     return net
 
 
+def ffn_inner(i, block, t1, rows, binner, kept, wi, hl, act, gp):
+    at = rows_of(i, block)
+    n1, _ = norm_rows(t1[at])
+    low = (n1 * rows[3:4] + rows[4:5]).astype(BF)
+    hl[at] = low
+    for j in range(4):
+        inner = mm(low, wi[j].reshape(D, D)) + binner[:, j * D : (j + 1) * D]
+        keep = column_mask(kept * 256 - j * D, (1, D), 1)
+        phi = 0.5 + 0.5 * lax.erf(inner * RSQRT2)
+        masked = inner * keep
+        act[j, at] = (masked * phi).astype(BF)
+        gp[j, at] = (keep * phi + masked * (RSQRT2PI * jnp.exp(-0.5 * (inner * inner)))).astype(BF)
+
+
+def ffn_outer(i, block, t1, grad, rows, kept, wi, wr, wo, inv, act, gp, y, bg, dos, og, sums, bsum):
+    at = rows_of(i, block)
+
+    def add(k, value):
+        sums[k : k + 1] += jnp.sum(value, axis=0, keepdims=True)
+
+    def outer_weight(j):
+        return wr[2 * j : 2 * j + 2].reshape(D, D)
+
+    outer = jnp.zeros((block, D), F32)
+    for j in range(4):
+        outer = outer + mm(act[j, at], outer_weight(j))
+    n1, inv1 = norm_rows(t1[at])
+    hidden = n1 * rows[3:4] + rows[4:5]
+    n2, inv2 = norm_rows(hidden + (outer + rows[5:6]))
+    y[at] = (n2 * rows[6:7] + rows[7:8]).astype(BF)
+    top = grad[at].astype(F32)
+    add(7, top)
+    add(6, top * n2)
+    res2 = norm_back(top * rows[6:7], n2, inv2)
+    o = res2.astype(BF)
+    og[at] = o
+    add(5, o.astype(F32))
+    hg = res2
+    for j in range(4):
+        cols = slice(j * D, (j + 1) * D)
+        g = (mm(o, outer_weight(j), NT) * gp[j, at].astype(F32)).astype(BF)
+        gp[j, at] = g
+        bsum[:, cols] += jnp.sum(g.astype(F32), axis=0, keepdims=True)
+        hg = hg + mm(g, wi[j].reshape(D, D), NT)
+    add(4, hg)
+    add(3, hg * n1)
+    res1 = norm_back(hg * rows[3:4], n1, inv1)
+    t1[at] = res1
+    b = res1.astype(BF)
+    bg[at] = b
+    add(2, b.astype(F32))
+    heads = column_mask(kept, (1, D), HEAD_DIM)
+    dos[at] = (mm(b, wo, NT) * (inv[at] * heads)).astype(BF)
+
+
 def forward_kernel(
-    x, seg, kept, wq, wk, wv, wo, wi, wr, vec,
-    fi, fo, fa_out, qkv_out, att_out, inv_out, e_out, t1_out, rows, binner,
-    own, fa, fv, qkv, att, inv, t1, segt, ebuf, ssem, rsem, lsem, esem,
+    x, seg, kept, wq, wk, wv, wo, wi, wr, vec, grad_in,
+    sums, bsum, fa_out, qkv_out, att_out, e_out, y_out, res_out, bg_out, dos_out, hl_out, og_out, ai_out,
+    own, fa, fi, fo, fv, rows, binner, att, inv, t1, segt, ebuf, grad, y, bg, dos, hl, og, act, gp,
+    ssem, rsem, lsem, esem,
 ):
+    qkv = gp.at[0:3]
     p = Place()
-    for c in range(3):
+    call(others(p))
+
+    def cast(c):
         for part, ref in enumerate((wq, wk, wv)):
             own[c, :, part * CW : (part + 1) * CW] = ref[:, c * CW : (c + 1) * CW].astype(BF)
-    greet(p, others(p))
+
+    cast(0)
+    answer(others(p))
     net = gather_net(p, own, fa, fi, fo, vec, fv, ssem, rsem)
     names = ("zb", "za", "zo")
-    net.start((0, "zb"), (0, "za"), (0, "own", "c"))
+
+    def ring(g):
+        net.start((g, "zb"), (g, "za"), (g, "own", "c"))
+
+    def onward(g):
+        net.wait((g, "zb"))
+        net.start((g, "zo"))
+
+    def plane(g, *which):
+        for name in which or names:
+            if name != "zb":
+                net.wait((g, name))
+            net.start((g, name, "xa"), (g, name, "xb"))
+
+    def relay(g, *which):
+        for name in which or names:
+            net.wait((g, name, "xa"))
+            net.start((g, name, "xd"))
+
+    def share(g, *which):
+        for name in which or names:
+            net.wait((g, name, "xb"), (g, name, "xd"))
+            net.start((g, name, "c"))
+
+    def landed(g):
+        net.wait((g, "own", "c"), *[(g, name, "c") for name in names])
+
+    ring(0)
+    cast(1)
+    ring(1)
+    cast(2)
     own[3] = wo[...].astype(BF)
     for q in range(4):
         own[4 + q] = wi[:, q * D : (q + 1) * D].astype(BF)
@@ -269,84 +356,97 @@
     def put(name, k, src, dst):
         local[name] = lambda: pltpu.make_async_copy(src(), dst(), lsem.at[k])
 
-    put("own a", 0, lambda: own.at[0:4], lambda: fa.at[:, p.s])
-    put("own i", 1, lambda: own.at[4:8], lambda: fi.at[:, p.s])
-    put("own o", 2, lambda: own.at[8:12], lambda: fo.at[p.s])
-    put("vec", 3, lambda: vec, lambda: fv.at[p.s])
-    put("qkv", 4, lambda: qkv, lambda: qkv_out)
-    put("fa", 5, lambda: fa, lambda: fa_out)
-    put("att", 6, lambda: att, lambda: att_out)
-    put("inv", 7, lambda: inv, lambda: inv_out)
-    put("t1", 8, lambda: t1, lambda: t1_out)
-    for name in ("own a", "own i", "own o", "vec"):
+    pieces = (
+        ("own a", lambda: own.at[0:4], lambda: fa.at[:, p.s]),
+        ("own i", lambda: own.at[4:8], lambda: fi.at[:, p.s]),
+        ("own o", lambda: own.at[8:12], lambda: fo.at[p.s]),
+        ("vec", lambda: vec, lambda: fv.at[p.s]),
+        ("grad", lambda: grad_in, lambda: grad),
+        ("qkv", lambda: qkv, lambda: qkv_out),
+        ("fa", lambda: fa.at[0:3], lambda: fa_out),
+        ("att", lambda: att, lambda: att_out),
+        ("hl", lambda: hl, lambda: hl_out),
+        ("act", lambda: act, lambda: ai_out.at[0:4]),
+        ("ig", lambda: gp, lambda: ai_out.at[4:8]),
+        ("og", lambda: og, lambda: og_out),
+        ("y", lambda: y, lambda: y_out),
+        ("res", lambda: t1, lambda: res_out),
+        ("bg", lambda: bg, lambda: bg_out),
+        ("dos", lambda: dos, lambda: dos_out),
+    )
+    for k, (name, src, dst) in enumerate(pieces):
+        put(name, k, src, dst)
+    for name in ("own a", "own i", "own o", "vec", "grad"):
         local[name]().start()
 
-    def ring1(g):
-        net.wait((g, "zb"))
-        net.start((g, "zo"))
-        if HIER[g]:
-            net.start((g, "zb", "xa"), (g, "zb", "xb"))
-        net.wait((g, "za"))
-        if HIER[g]:
-            net.start((g, "za", "xa"), (g, "za", "xb"))
-
-    def ring2(g):
-        net.wait((g, "zo"))
-        if HIER[g]:
-            net.start((g, "zo", "xa"), (g, "zo", "xb"))
-
-    def relay(g, name):
-        net.wait((g, name, "xa"))
-        net.start((g, name, "xd"))
-
-    def share(g, name):
-        if HIER[g]:
-            net.wait((g, name, "xb"), (g, name, "xd"))
-        net.start((g, name, "c"))
-
-    def landed(g):
-        net.wait((g, "own", "c"), *[(g, name, "c") for name in names])
-
-    ring1(0)
-    net.start((2, "zb"), (2, "za"), (1, "zb"), (1, "za"), (1, "own", "c"), (2, "own", "c"), (3, "own", "c"))
-    ring2(0)
+    onward(0)
+    plane(0, "zb", "za")
+    onward(1)
+    ring(2)
+    plane(1, "zb", "za")
+    plane(0, "zo")
     turn_ids(seg, segt)
-    relay(0, "zb")
-    relay(0, "za")
-    share(0, "zb")
-    net.start((3, "zb"), (3, "za"))
+    relay(0, "zb", "za")
+    plane(1, "zo")
+    relay(1, "zb")
+    onward(2)
+    ring(WO)
+    relay(1, "za")
+    plane(2, "zb", "za")
     relay(0, "zo")
-    share(0, "za")
+    share(0, "zb", "za")
+    relay(1, "zo")
+    plane(2, "zo")
+    share(1, "zb")
+    relay(2, "zb")
+    onward(WO)
+    ring(INNER)
+    share(1, "za")
+    relay(2, "za")
+    plane(WO, "zb")
+    share(0, "zo")
+    plane(WO, "za")
+    share(1, "zo")
+    relay(2, "zo")
     net.wait(*[("v", k) for k in range(1, 8)])
     local["vec"]().wait()
     expand_vectors(fv, rows, binner)
-    share(0, "zo")
-    ring1(2)
-    ring1(1)
+    share(2, "zb")
+    plane(WO, "zo")
     local["own a"]().wait()
-    landed(0)
-
-    project(x, fa, rows, qkv)
-    local["qkv"]().start()
-    ring2(2)
-    ring2(1)
-    for name in names:
-        share(1, name)
     keep = kept[0]
 
     def out_copy(i, slot):
         c, r, pair = place_of(i)
         return pltpu.make_async_copy(ebuf.at[slot], e_out.at[c, r, pair], esem.at[slot])
 
+    before = {0: lambda: landed(0), 4: lambda: landed(1), 8: lambda: landed(2)}
     steps = {
-        0: lambda: relay(2, "zb"),
-        1: lambda: relay(2, "za"),
-        2: lambda: (share(2, "zb"), ring1(3)),
-        3: lambda: relay(2, "zo"),
-        4: lambda: share(2, "za"),
-        6: lambda: (share(2, "zo"), share(3, "zb"), share(3, "za")),
-        9: lambda: (ring2(3), share(3, "zo")),
+        0: lambda: (share(2, "za", "zo"), relay(WO), onward(INNER), ring(OUTER), plane(INNER, "zb", "za"),),
+        1: lambda: (share(WO),),
+        2: lambda: (plane(INNER, "zo"),),
+        3: lambda: (relay(INNER, "zb"),),
+        4: lambda: (relay(INNER, "za"), onward(OUTER), plane(OUTER, "zb", "za"),),
+        5: lambda: (relay(INNER, "zo"),),
+        6: lambda: (share(INNER, "zb"),),
+        7: lambda: (share(INNER, "za"), relay(OUTER, "zb"), plane(OUTER, "zo"),),
+        8: lambda: (relay(OUTER, "za"),),
+        9: lambda: (relay(OUTER, "zo"),),
+        10: lambda: (share(INNER, "zo"),),
+        11: lambda: (share(OUTER, "zb"),),
     }
+    later = {
+        0: lambda: (share(OUTER, "zo"),),
+    }
+
+    def after_residual():
+        share(OUTER, "za")
+
+    def at_step(i, table):
+        for k, step in table.items():
+            @pl.when(i == k)
+            def _(step=step):
+                step()
 
     def one(i, _):
         slot = lax.rem(i, 2)
@@ -355,196 +455,102 @@
         def _():
             out_copy(i - 2, slot).wait()
 
+        at_step(i, before)
+
+        @pl.when(lax.rem(i, 4) == 0)
+        def _():
+            project(lax.div(i, 4), x, fa, rows, qkv)
+
         attend(i, qkv, seg, segt, keep, att, inv, ebuf.at[slot])
         out_copy(i, slot).start()
-        for k, step in steps.items():
-            @pl.when(i == k)
-            def _(step=step):
-                step()
+        at_step(i, steps)
         return 0
 
     n = 6 * (x.shape[0] // SEQ)
     lax.fori_loop(0, n, one, 0)
+    local["qkv"]().start()
     local["att"]().start()
-    local["inv"]().start()
-    landed(1)
     local["fa"]().start()
-
-    def last(i, _):
-        at = rows_of(i, 256)
+    sums[...] = jnp.zeros_like(sums)
+    bsum[...] = jnp.zeros_like(bsum)
+    landed(WO)
+    block = 256
+    blocks = x.shape[0] // block
+
+    def residual(i, _):
+        at = rows_of(i, block)
         t1[at] = x[at].astype(F32) + (mm(att[at], fa[3].reshape(D, D)) + rows[2:3])
         return 0
 
-    lax.fori_loop(0, x.shape[0] // 256, last, 0)
-    local["t1"]().start()
+    lax.fori_loop(0, blocks, residual, 0)
+    after_residual()
+    landed(INNER)
+    local["own i"]().wait()
+    local["qkv"]().wait()
+
+    def first(i, _):
+        ffn_inner(i, block, t1, rows, binner, keep, fi, hl, act, gp)
+        at_step(i, later)
+        return 0
+
+    lax.fori_loop(0, blocks, first, 0)
+    local["hl"]().start()
+    local["act"]().start()
+    landed(OUTER)
+    local["own o"]().wait()
+    local["grad"]().wait()
+
+    def second(i, _):
+        ffn_outer(i, block, t1, grad, rows, keep, fi, fo, fa[3].reshape(D, D), inv, act, gp, y, bg, dos, og, sums, bsum)
+        return 0
+
+    lax.fori_loop(0, blocks, second, 0)
+    for name in ("og", "ig", "dos", "bg", "res", "y"):
+        local[name]().start()
     out_copy(n - 2, (n - 2) % 2).wait()
     out_copy(n - 1, (n - 1) % 2).wait()
-    landed(2)
-    landed(3)
-    for name in ("own i", "own o", "qkv", "fa", "att", "inv", "t1"):
+    for name in ("fa", "att", "hl", "act", "og", "ig", "dos", "bg", "res", "y"):
         local[name]().wait()
     net.finish()
 
 
-def forward(x, seg, kept, wq, wk, wv, wo, wi, wr, vec):
+def forward(x, seg, kept, wq, wk, wv, wo, wi, wr, vec, grad):
     t = x.shape[0]
     n = t // SEQ
     return pl.pallas_call(
         forward_kernel,
         out_shape=(
-            shape(4, 8, TR, D), shape(8, 4, TR, D), shape(4, 8, TR, D), shape(3, t, D), shape(t, D), shape(t, D, dtype=F32),
-            shape(3, n, 2, 2, SEQ, SEQ), shape(t, D, dtype=F32), shape(8, D, dtype=F32), shape(1, FF, dtype=F32),
+            shape(8, D, dtype=F32), shape(1, FF, dtype=F32), shape(3, 8, TR, D), shape(3, t, D), shape(t, D),
+            shape(3, n, 2, 2, SEQ, SEQ), shape(t, D), shape(t, D, dtype=F32), shape(t, D), shape(t, D), shape(t, D),
+            shape(t, D), shape(8, t, D),
         ),
-        in_specs=[VM, VM, SM] + [VM] * 7,
-        out_specs=(ANY,) * 8 + (VM, VM),
+        in_specs=[VM, VM, SM] + [VM] * 7 + [ANY],
+        out_specs=(VM, VM) + (ANY,) * 11,
         scratch_shapes=[
             pltpu.VMEM((12, TR, D), BF),
             pltpu.VMEM((4, 8, TR, D), BF),
+            pltpu.VMEM((4, 8, TR, D), BF),
+            pltpu.VMEM((8, 4, TR, D), BF),
             pltpu.VMEM((8, 16, 128), BF),
-            pltpu.VMEM((3, t, D), BF),
+            pltpu.VMEM((8, D), F32),
+            pltpu.VMEM((1, FF), F32),
             pltpu.VMEM((t, D), BF),
             pltpu.VMEM((t, D), F32),
             pltpu.VMEM((t, D), F32),
             pltpu.VMEM((n, SEQ, 128), F32),
             pltpu.VMEM((2, 2, SEQ, SEQ), BF),
+        ]
+        + [pltpu.VMEM((t, D), BF)] * 6
+        + [pltpu.VMEM((4, t, D), BF)] * 2
+        + [
             pltpu.SemaphoreType.DMA((GATHER_COPIES,)),
             pltpu.SemaphoreType.DMA((GATHER_COPIES,)),
-            pltpu.SemaphoreType.DMA((9,)),
+            pltpu.SemaphoreType.DMA((16,)),
             pltpu.SemaphoreType.DMA((2,)),
         ],
         compiler_params=params(collective_id=0, has_side_effects=True),
         name="forward",
-    )(x, seg, kept, wq, wk, wv, wo, wi, wr, vec)
-
-
-def ffn_kernel(
-    t1, grad, rows, binner, kept, inv, fi, fo, fa,
-    y, res, bg, dos, sums, bsum, g_out,
-    wi, wr, wo, hl, act, ig, og, gp, gbuf, lsem, gsem, block=256,
-):
-    load = [
-        pltpu.make_async_copy(fi, wi, lsem.at[0]),
-        pltpu.make_async_copy(fo, wr, lsem.at[1]),
-        pltpu.make_async_copy(fa.at[3], wo, lsem.at[2]),
-    ]
-    for copy in load:
-        copy.start()
-    keep_heads = kept[0]
-    b_outer, gain_two, shift_two = rows[5:6], rows[6:7], rows[7:8]
-    gain_one, shift_one = rows[3:4], rows[4:5]
-    sums[...] = jnp.zeros_like(sums)
-    bsum[...] = jnp.zeros_like(bsum)
-    heads = column_mask(keep_heads, (1, D), HEAD_DIM)
-    for copy in load:
-        copy.wait()
-
-    def add(k, value):
-        sums[k : k + 1] += jnp.sum(value, axis=0, keepdims=True)
-
-    def inner_weight(j):
-        return wi[j].reshape(D, D)
-
-    def outer_weight(j):
-        return wr[2 * j : 2 * j + 2].reshape(D, D)
-
-    def one(i, _):
-        at = rows_of(i, block)
-        n1, inv1 = norm_rows(t1[at])
-        hidden = n1 * gain_one + shift_one
-        low = hidden.astype(BF)
-        hl[at] = low
-        outer = jnp.zeros((block, D), F32)
-        for j in range(4):
-            cols = slice(j * D, (j + 1) * D)
-            inner = mm(low, inner_weight(j)) + binner[:, cols]
-            keep = column_mask(keep_heads * 256 - j * D, (1, D), 1)
-            phi = 0.5 + 0.5 * lax.erf(inner * RSQRT2)
-            masked = inner * keep
-            a = (masked * phi).astype(BF)
-            gp[:, cols] = (keep * phi + masked * (RSQRT2PI * jnp.exp(-0.5 * (inner * inner)))).astype(BF)
-            act[at, cols] = a
-            outer = outer + mm(a, outer_weight(j))
-        n2, inv2 = norm_rows(hidden + (outer + b_outer))
-        y[at] = (n2 * gain_two + shift_two).astype(BF)
-        top = grad[at].astype(F32)
-        add(7, top)
-        add(6, top * n2)
-        res2 = norm_back(top * gain_two, n2, inv2)
-        o = res2.astype(BF)
-        og[at] = o
-        add(5, o.astype(F32))
-        hg = res2
-        for j in range(4):
-            cols = slice(j * D, (j + 1) * D)
-            g = (mm(o, outer_weight(j), NT) * gp[:, cols].astype(F32)).astype(BF)
-            ig[at, cols] = g
-            bsum[:, cols] += jnp.sum(g.astype(F32), axis=0, keepdims=True)
-            hg = hg + mm(g, inner_weight(j), NT)
-        add(4, hg)
-        n1, inv1 = norm_rows(t1[at])
-        add(3, hg * n1)
-        res1 = norm_back(hg * gain_one, n1, inv1)
-        res[at] = res1
-        b = res1.astype(BF)
-        bg[at] = b
-        add(2, b.astype(F32))
-        dos[at] = (mm(b, wo[...].reshape(D, D), NT) * (inv[at] * heads)).astype(BF)
-        return 0
-
-    lax.fori_loop(0, t1.shape[0] // block, one, 0)
-
-    def outer_out(j):
-        return pltpu.make_async_copy(gbuf.at[j], g_out.at[lax.div(j, 2), pl.ds(2 * lax.rem(j, 2), 2), 0:4], gsem.at[j])
-
-    def inner_out(j):
-        return pltpu.make_async_copy(gbuf.at[4 + j], g_out.at[:, :, 4 + j], gsem.at[4 + j])
-
-    def two(j, _):
-        cols = rows_of(j, D)
-        gbuf[j] = mm(act[:, cols], og[...], TN).astype(BF).reshape(2, 4, TR, D)
-        outer_out(j).start()
-        return 0
-
-    lax.fori_loop(0, 4, two, 0)
-
-    def three(j, _):
-        cols = rows_of(j, D)
-        gbuf[4 + j] = mm(hl[...], ig[:, cols], TN).astype(BF).reshape(2, 4, TR, D)
-        inner_out(j).start()
-        return 0
-
-    lax.fori_loop(0, 4, three, 0)
-    for j in range(4):
-        outer_out(j).wait()
-        inner_out(j).wait()
-
-
-def ffn(t1, grad, rows, binner, kept, inv, fi, fo, fa):
-    t = t1.shape[0]
-    return pl.pallas_call(
-        ffn_kernel,
-        out_shape=(
-            shape(t, D), shape(t, D, dtype=F32), shape(t, D), shape(t, D),
-            shape(8, D, dtype=F32), shape(1, FF, dtype=F32), shape(2, 4, 8, TR, D),
-        ),
-        in_specs=[VM] * 4 + [SM, VM] + [ANY] * 3,
-        out_specs=(VM,) * 6 + (ANY,),
-        scratch_shapes=[
-            pltpu.VMEM((4, 8, TR, D), BF),
-            pltpu.VMEM((8, 4, TR, D), BF),
-            pltpu.VMEM((8, TR, D), BF),
-            pltpu.VMEM((t, D), BF),
-            pltpu.VMEM((t, FF), BF),
-            pltpu.VMEM((t, FF), BF),
-            pltpu.VMEM((t, D), BF),
-            pltpu.VMEM((256, FF), BF),
-            pltpu.VMEM((8, 2, 4, TR, D), BF),
-            pltpu.SemaphoreType.DMA((3,)),
-            pltpu.SemaphoreType.DMA((8,)),
-        ],
-        compiler_params=params(),
-        name="ffn",
-    )(t1, grad, rows, binner, kept, inv, fi, fo, fa)
+    )(x, seg, kept, wq, wk, wv, wo, wi, wr, vec, grad)
 
 
 def attend_back(i, qkv, dos, att, ebuf, dqkv):
@@ -594,8 +600,8 @@
     lax.fori_loop(0, res.shape[0] // block, one, 0)
 
 
-JOBS = ((0, 4, True), (4, 4, False), (8, 1, True), (9, 1, False), (10, 1, True), (11, 1, False))
-REDUCE_COPIES = 10 * len(JOBS) + 7
+JOBS = ((0, 4, True), (4, 4, False), (8, 1, False), (9, 1, False), (10, 1, False), (11, 1, False))
+REDUCE_COPIES = 9 * len(JOBS) + (4 + 4 + 4) + 7
 JOB_BUFFERS = 7
 
 
@@ -634,7 +640,9 @@
         self.one, self.two = one, two
         self.own1 = z if ring_first else p.w
         self.own2 = p.w if ring_first else z
-        net.define((k, "c"), lambda: (source(1 - p.c), self.landed, p.sib))
+        self.parts = len(source)
+        for j, make in enumerate(source):
+            net.define((k, "c", j), lambda make=make: (*make(self.landed), p.sib))
         for stage, at, way, d, a, b in ((1, self.at1, one, self.d1, self.a1, self.b1), (2, self.at2, two, self.d2, self.a2, self.b2)):
             relayed, direct, opposite, dev_o, dev_r, dev_d = way
 
@@ -643,7 +651,7 @@
                     ref, where = at(index)
                     return ref.at[where], dst, device
 
-                net.define((k, name), make)
+                net.define((k, *name), make)
 
             send(("d", stage), opposite, d, dev_o)
             send(("b", stage), direct, b, dev_d)
@@ -660,17 +668,20 @@
         share("gb", p.w, p.plane_b)
         share("gd", p.wa, p.plane_b)
 
+    def names(self, names):
+        return [(self.k, *name) if isinstance(name, tuple) else (self.k, name) for name in names]
+
     def start(self, *names):
-        self.net.start(*[(self.k, name) for name in names])
+        self.net.start(*self.names(names))
 
     def wait(self, *names):
-        self.net.wait(*[(self.k, name) for name in names])
-
-    def send(self):
-        self.start("c")
+        self.net.wait(*self.names(names))
+
+    def send(self, j=0):
+        self.start(("c", j))
 
     def pair(self):
-        self.wait("c")
+        self.wait(*[("c", j) for j in range(self.parts)])
         held, landed = self.held, self.landed
 
         def one(t, _):
@@ -710,44 +721,62 @@
 
 
 def backward_kernel(
-    x, qkv_in, e_in, att_in, dos_in, bg_in, res_in, fa_in, g_in, sums_in, bsum,
+    x, qkv_in, e_in, att_in, dos_in, bg_in, res_in, fa_in, hl_in, og_in, ai_in, sums_in, bsum,
     out, result, ovec,
     qkv, att, dos, bg, res, fa, dqkv, gx, go, ebuf, sums, vt, vheld, vrecv, vplane, vz, *rest,
 ):
     bufs, (ssem, rsem, lsem, esem) = rest[:-4], rest[-4:]
     p = Place()
+    call(others(p))
     n = 6 * (x.shape[0] // SEQ)
-    load = {}
-
-    def get(name, k, src, dst):
-        load[name] = pltpu.make_async_copy(src, dst, lsem.at[k])
-        load[name].start()
+    og, hl = dqkv.at[0], dqkv.at[1]
+    loads = (
+        ("og", lambda: og_in, lambda: og),
+        ("hl", lambda: hl_in, lambda: hl),
+        ("att", lambda: att_in, lambda: att),
+        ("bg", lambda: bg_in, lambda: bg),
+        ("qkv", lambda: qkv_in, lambda: qkv),
+        ("dos", lambda: dos_in, lambda: dos),
+        ("res", lambda: res_in, lambda: res),
+        ("fa", lambda: fa_in, lambda: fa.at[0:3]),
+    )
+    load = {
+        name: lambda k=k, src=src, dst=dst: pltpu.make_async_copy(src(), dst(), lsem.at[k])
+        for k, (name, src, dst) in enumerate(loads)
+    }
+
+    def block_copy(j):
+        return pltpu.make_async_copy(ai_in.at[j], qkv.at[j % 3], lsem.at[len(loads) + j % 3])
 
     def in_copy(i, slot):
         c, r, pair = place_of(i)
         return pltpu.make_async_copy(e_in.at[c, r, pair], ebuf.at[slot], esem.at[slot])
 
+    load["og"]().start()
+    block_copy(0).start()
+    block_copy(1).start()
+    load["hl"]().start()
+    for name in ("att", "bg", "dos"):
+        load[name]().start()
+    in_copy(0, 0).start()
+    load["res"]().start()
+
+    def staged(k, j):
+        return fa.at[2 * k + j // 2, 4 * (j % 2) : 4 * (j % 2) + 4]
+
     jobs = []
     net = Net(ssem, rsem)
-    g4 = g_in
     per = 9
     for k, (first, units, ring_first) in enumerate(JOBS):
-        if k < 2:
-            source = lambda core, first=first, units=units: g4.at[:, core, first : first + units]
+        if k == 0:
+            source = [lambda landed, j=j: (staged(0, j), landed.at[j]) for j in range(4)]
+        elif k == 1:
+            source = [lambda landed, j=j: (staged(1, j), landed.at[:, j]) for j in range(4)]
         elif k == 2:
-            source = lambda core: go.at[:, core]
+            source = [lambda landed: (go.at[:, 1 - p.c], landed)]
         else:
-            source = lambda core, c=k - 3: gx.at[c, :, core]
+            source = [lambda landed, c=k - 3: (gx.at[c, :, 1 - p.c], landed)]
         jobs.append(Job(net, p, k, first, units, ring_first, source, bufs[per * k : per * (k + 1)], result))
-    get("att", 0, att_in, att)
-    get("bg", 1, bg_in, bg)
-    get("h0", 2, g4.at[:, p.c, 0:4], jobs[0].held)
-    get("h1", 3, g4.at[:, p.c, 4:8], jobs[1].held)
-    get("qkv", 4, qkv_in, qkv)
-    get("dos", 5, dos_in, dos)
-    in_copy(0, 0).start()
-    get("res", 6, res_in, res)
-    get("fa", 7, fa_in.at[0:3], fa)
     net.define(("v", "c"), lambda: (vt.at[:, 1 - p.c], vrecv, p.sib))
     for k, device in enumerate((p.plane_a, p.plane_b, (p.wd, p.s))):
         net.define(("v", "p", k), lambda device=device: (vheld.at[0], vplane.at[p.w], device))
@@ -756,25 +785,44 @@
         net.define(("v", "z", k), lambda to=to: (vheld.at[1, to], vz.at[p.z], (p.w, 2 * to + p.c)))
     assert len(net.made) == REDUCE_COPIES, len(net.made)
 
-    greet(p, others(p))
-    jobs[0].send()
-    jobs[1].send()
+    first_core = p.c == 0
+    for j in range(8):
+        if j == 0:
+            load["og"]().wait()
+        if j == 4:
+            load["hl"]().wait()
+        if j + 2 < 8:
+            block_copy(j + 2).start()
+        block_copy(j).wait()
+        block = qkv.at[j % 3]
+        if j < 4:
+            tiles = mm(block[...], og[...], TN).astype(BF).reshape(2, 4, TR, D)
+            zero, one = tiles[0], tiles[1]
+            jobs[0].held[j] = jnp.where(first_core, zero, one)
+        else:
+            tiles = mm(hl[...], block[...], TN).astype(BF).reshape(4, 2, TR, D)
+            zero, one = tiles[:, 0], tiles[:, 1]
+            jobs[1].held[:, j - 4] = jnp.where(first_core, zero, one)
+        staged(j // 4, j % 4)[...] = jnp.where(first_core, one, zero)
+        if j == 0:
+            answer(others(p))
+        jobs[j // 4].send(j % 4)
+        if j == 4:
+            jobs[0].pair()
+    load["qkv"]().start()
     sums[...] = sums_in[...]
-    load["att"].wait()
-    load["bg"].wait()
+    load["att"]().wait()
+    load["bg"]().wait()
     go[...] = mm(att[...], bg[...], TN).astype(BF).reshape(4, 2, 1, TR, D)
     jobs[2].send()
-    load["h0"].wait()
-    jobs[0].pair()
-    load["h1"].wait()
     jobs[1].pair()
 
     def own_half(k, source):
         jobs[k].held[...] = source[:, p.c]
 
     own_half(2, go)
-    load["qkv"].wait()
-    load["dos"].wait()
+    load["qkv"]().wait()
+    load["dos"]().wait()
     jobs[2].pair()
 
     def begin(k):
@@ -816,6 +864,12 @@
         return 0
 
     lax.fori_loop(0, n, one, 0)
+
+    for k in range(2):
+        for j in range(4):
+            net.copy((k, "c", j)).wait_send()
+            net.sent.add((k, "c", j))
+    load["fa"]().start()
 
     for s in range(8):
         vt[s // 2, s % 2] = jnp.zeros((16, 128), F32)
@@ -832,8 +886,8 @@
     vheld[0] = vt[:, p.c] + vrecv[...]
     vplane[p.w] = vheld[0]
     net.start(*[("v", "p", k) for k in range(3)])
-    load["res"].wait()
-    load["fa"].wait()
+    load["res"]().wait()
+    load["fa"]().wait()
     c2.relay(1)
 
     def back(i):
@@ -865,13 +919,13 @@
     net.finish()
 
 
-def backward(x, qkv, e, att, dos, bg, res, fa, g, sums, bsum):
+def backward(x, qkv, e, att, dos, bg, res, fa, hl, og, ai, sums, bsum):
     t = x.shape[0]
     job_scratch = [pltpu.VMEM(s, BF) for _, units, ring_first in JOBS for s in job_shapes(units, ring_first)]
     return pl.pallas_call(
         backward_kernel,
         out_shape=(shape(t, D), shape(12, TR, D), shape(16, 128, dtype=F32)),
-        in_specs=[VM] + [ANY] * 8 + [VM, VM],
+        in_specs=[VM] + [ANY] * 10 + [VM, VM],
         out_specs=(VM,) * 3,
         scratch_shapes=[
             pltpu.VMEM((3, t, D), BF),
@@ -879,7 +933,7 @@
             pltpu.VMEM((t, D), BF),
             pltpu.VMEM((t, D), BF),
             pltpu.VMEM((t, D), F32),
-            pltpu.VMEM((3, 8, TR, D), BF),
+            pltpu.VMEM((4, 8, TR, D), BF),
             pltpu.VMEM((3, t, D), BF),
             pltpu.VMEM((3, 4, 2, 1, TR, D), BF),
             pltpu.VMEM((4, 2, 1, TR, D), BF),
@@ -895,12 +949,12 @@
         + [
             pltpu.SemaphoreType.DMA((REDUCE_COPIES,)),
             pltpu.SemaphoreType.DMA((REDUCE_COPIES,)),
-            pltpu.SemaphoreType.DMA((8,)),
+            pltpu.SemaphoreType.DMA((11,)),
             pltpu.SemaphoreType.DMA((2,)),
         ],
         compiler_params=params(collective_id=1, has_side_effects=True),
         name="backward",
-    )(x, qkv, e, att, dos, bg, res, fa, g.reshape(4, 2, 8, TR, D), sums, bsum)
+    )(x, qkv, e, att, dos, bg, res, fa, hl, og, ai, sums, bsum)
 
 
 def finish_kernel(result, ovec, inp, oq, ok, ov, oo, oi, our, out, *vectors):
@@ -936,7 +990,8 @@
 
 def forward_local_kernel(x, seg, kept, fa, rows, qkv, att, inv, e_out, t1, segt, ebuf, esem):
     turn_ids(seg, segt)
-    project(x, fa, rows, qkv)
+    for c in range(3):
+        project(c, x, fa, rows, qkv)
     keep = kept[0]
 
     def one(i, _):
@@ -967,6 +1022,60 @@
     )(x, seg, kept, fa, rows)
 
 
+def ffn_local_kernel(
+    t1, grad, rows, binner, kept, inv, fi, fo, fa, y, res, bg, dos, sums, bsum, g, hl, og, act, gp, t2, tile, gsem, block=256
+):
+    sums[...] = jnp.zeros_like(sums)
+    bsum[...] = jnp.zeros_like(bsum)
+    t2[...] = t1[...]
+    blocks = t1.shape[0] // block
+
+    def first(i, _):
+        ffn_inner(i, block, t2, rows, binner, kept[0], fi, hl, act, gp)
+        return 0
+
+    def second(i, _):
+        wo = fa[3].reshape(D, D)
+        ffn_outer(i, block, t2, grad, rows, kept[0], fi, fo, wo, inv, act, gp, y, bg, dos, og, sums, bsum)
+        return 0
+
+    lax.fori_loop(0, blocks, first, 0)
+    lax.fori_loop(0, blocks, second, 0)
+    res[...] = t2[...]
+
+    def one(j, _):
+        tile[...] = mm(act[j], og[...], TN).astype(BF).reshape(2, 4, TR, D)
+        copy = pltpu.make_async_copy(tile, g.at[lax.div(j, 2), pl.ds(2 * lax.rem(j, 2), 2), 0:4], gsem.at[0])
+        copy.start()
+        copy.wait()
+        tile[...] = mm(hl[...], gp[j], TN).astype(BF).reshape(2, 4, TR, D)
+        copy = pltpu.make_async_copy(tile, g.at[:, :, 4 + j], gsem.at[0])
+        copy.start()
+        copy.wait()
+        return 0
+
+    lax.fori_loop(0, 4, one, 0)
+
+
+def ffn_local(t1, grad, rows, binner, kept, inv, fi, fo, fa):
+    t = t1.shape[0]
+    return pl.pallas_call(
+        ffn_local_kernel,
+        out_shape=(
+            shape(t, D), shape(t, D, dtype=F32), shape(t, D), shape(t, D),
+            shape(8, D, dtype=F32), shape(1, FF, dtype=F32), shape(2, 4, 8, TR, D),
+        ),
+        in_specs=[VM] * 4 + [SM] + [VM] * 4,
+        out_specs=(VM,) * 6 + (ANY,),
+        scratch_shapes=[
+            pltpu.VMEM((t, D), BF), pltpu.VMEM((t, D), BF), pltpu.VMEM((4, t, D), BF), pltpu.VMEM((4, t, D), BF),
+            pltpu.VMEM((t, D), F32), pltpu.VMEM((2, 4, TR, D), BF), pltpu.SemaphoreType.DMA((1,)),
+        ],
+        compiler_params=params(),
+        name="ffn_local",
+    )(t1, grad, rows, binner, kept, inv, fi, fo, fa)
+
+
 def backward_local_kernel(x, qkv, e_in, att, dos, bg, res, fa, sums_in, out, gx, go, sums, dqkv, ebuf, esem):
     sums[...] = sums_in[...]
     go[...] = mm(att[...], bg[...], TN).astype(BF).reshape(4, 2, 1, TR, D)
@@ -1039,13 +1148,15 @@
     if own_kernels:
         vec = jnp.concatenate([jnp.stack(eight), jnp.zeros((8, 128 - TR), F32)], axis=1)
         vec = jnp.concatenate([vec, b_inner.reshape(3, 128), jnp.zeros((5, 128), F32)], axis=0).astype(BF)
-        fi, fo, fa, qkv, att, inv, e, t1, rows, binner = forward(layer_input, segment_ids, group_heads, *weights, vec)
+        sums, bsum, fa, qkv, att, e, y, res, bg, dos, hl, og, ai = forward(
+            layer_input, segment_ids, group_heads, *weights, vec, out_grad
+        )
     else:
         fa, fi, fo, rows, binner = gather_lax(*weights, eight, b_inner)
         qkv, att, inv, e, t1 = forward_local(layer_input, segment_ids, group_heads, fa, rows)
-    y, res, bg, dos, sums, bsum, g = ffn(t1, out_grad, rows, binner, group_heads, inv, fi, fo, fa)
+        y, res, bg, dos, sums, bsum, g = ffn_local(t1, out_grad, rows, binner, group_heads, inv, fi, fo, fa)
     if own_kernels:
-        input_grad, result, ovec = backward(layer_input, qkv, e, att, dos, bg, res, fa, g, sums, bsum)
+        input_grad, result, ovec = backward(layer_input, qkv, e, att, dos, bg, res, fa, hl, og, ai, sums, bsum)
         gq, gk, gv, go, gi, gr, input_grad, *vectors = finish(result, ovec, input_grad)
     else:
         input_grad, gx, go, sums = backward_local(layer_input, qkv, e, att, dos, bg, res, fa[0:3], sums)

time: 273 us -> 222 us (0.81)
  Pallas kernels: 267 us -> 215 us
    pallas_call x2 -> x1, Pallas kernels: 145 us -> 100 us  [forward(): pl.pallas_call(forward_kernel, out_shape=(shape(8, D, dtype=F32), shape(1...]
    pallas_call x1, Pallas kernels: 118 us -> 110 us  [backward(): pl.pallas_call(backward_kernel, out_shape=(shape(t, D), shape(12, TR, D),...]
where the time goes in v4:
time: 222 us
  Pallas kernels  215 us (97%)
  other arithmetic  4.05 us (2%)
    pallas_call x1, Pallas kernels, backward(): pl.pallas_call(backward_kernel, out_shape=(shape(t, D), shape(12, TR, D),...  110 us
    pallas_call x1, Pallas kernels, forward(): pl.pallas_call(forward_kernel, out_shape=(shape(8, D, dtype=F32), shape(1...  100 us

profile of v4, /device:TPU:0, one launch (start us, length us, event | category | flops | bytes accessed | tf_op | source)
XLA Modules:
  0.0 221.9 jit_solution(10398858627995947633)
XLA Ops:
  1.3 0.1 pad.4.clone
  1.4 0.7 convert_bitcast_fusion
  2.1 0.7 convert_bitcast_fusion.7
  2.7 0.7 convert_bitcast_fusion.5
  3.4 0.7 convert_bitcast_fusion.3
  4.1 0.7 convert_bitcast_fusion.1
  4.8 0.7 fusion.2.vec
  5.5 100.4 %forward.1 = (f32[8,768]{1,0:T(8,128)}, f32[1,3072]{1,0:T(1,128)}, bf16[3,8,96,768]{3,2,1,0:T(8,128)(2,1)}, bf16[3,1024,768]{2,1,0:T(8,128)(2,1)}, bf16[1024,768...) custom-call(bf16[1024,768]{1,0:T(8,128)(2,1)} %x.5, ...), custom_call_target="tpu_custom_call" | custom-call | tf_op jit(solution)/shard_map/forward/pallas_call | solution.py:520
  105.9 110.5 %backward.1 = (bf16[1024,768]{1,0:T(8,128)(2,1)}, bf16[12,96,768]{2,1,0:T(8,128)(2,1)}, f32[16,128]{1,0:T(8,128)}) custom-call(bf16[1024,768]{1,0:T(8,128)(2,1)} %x.5, bf16[3,1024,768]{2,1,0:T(8,128)(2,1)} %get-tuple-element.50.qkv_in, bf16[3,2,2,2,512,512]{5,4,3,2,1,0:T(8,128)(2,1)} %get-tuple-element.51.e_in, bf16[1024,768]{1,0:T(8,128)(2,1)} %get-tuple-element.52.att_in, ...), custom_call_target="tpu_custom_call" | custom-call | tf_op jit(solution)/shard_map/backward/pallas_call | solution.py:925
  216.3 0.0 copy-start
  216.3 4.4 %finish.1 = (f32[96,768]{1,0:T(8,128)}, f32[96,768]{1,0:T(8,128)}, f32[96,768]{1,0:T(8,128)}, f32[96,768]{1,0:T(8,128)}, f32[96,3072]{1,0:T(8,128)}, /*index=5*/...) custom-call(bf16[12,96,768]{2,1,0:T(8,128)(2,1)} %get-tuple-element., ...), custom_call_target="tpu_custom_call" | custom-call | tf_op jit(solution)/shard_map/finish/pallas_call | solution.py:978
  220.8 0.0 copy-done
  220.8 1.1 copy.38
  (2 shorter events, 0.0 us)
Async XLA Ops:
  216.3 4.5 %copy-start = (bf16[1024,768]{1,0:T(8,128)(2,1)S(1)}, bf16[1024,768]{1,0:T(8,128)(2,1)}, u32[]{:S(2)}) copy-start(bf16[1024,768]{1,0:T(8,128)(2,1)} %get-tuple-element.106) | copy-start | bytes 4718596

commit v5 on v4

--- a/solution.py
+++ b/solution.py
@@ -390,29 +390,27 @@
     plane(1, "zo")
     relay(1, "zb")
     onward(2)
-    ring(WO)
+    ring(INNER)
     relay(1, "za")
     plane(2, "zb", "za")
     relay(0, "zo")
     share(0, "zb", "za")
     relay(1, "zo")
+    share(1, "zb")
     plane(2, "zo")
-    share(1, "zb")
-    relay(2, "zb")
-    onward(WO)
-    ring(INNER)
     share(1, "za")
-    relay(2, "za")
-    plane(WO, "zb")
+    relay(2, "zb", "za")
     share(0, "zo")
-    plane(WO, "za")
+    onward(INNER)
+    ring(WO)
     share(1, "zo")
+    plane(INNER, "zb")
     relay(2, "zo")
     net.wait(*[("v", k) for k in range(1, 8)])
     local["vec"]().wait()
     expand_vectors(fv, rows, binner)
-    share(2, "zb")
-    plane(WO, "zo")
+    share(2, "zb", "za")
+    plane(INNER, "za")
     local["own a"]().wait()
     keep = kept[0]
 
@@ -422,25 +420,23 @@
 
     before = {0: lambda: landed(0), 4: lambda: landed(1), 8: lambda: landed(2)}
     steps = {
-        0: lambda: (share(2, "za", "zo"), relay(WO), onward(INNER), ring(OUTER), plane(INNER, "zb", "za"),),
-        1: lambda: (share(WO),),
-        2: lambda: (plane(INNER, "zo"),),
-        3: lambda: (relay(INNER, "zb"),),
-        4: lambda: (relay(INNER, "za"), onward(OUTER), plane(OUTER, "zb", "za"),),
-        5: lambda: (relay(INNER, "zo"),),
+        1: lambda: (plane(INNER, "zo"), relay(INNER, "zb"), onward(WO), ring(OUTER), share(2, "zo"), plane(WO, "zb", "za"),),
+        2: lambda: (relay(INNER, "za"),),
+        4: lambda: (relay(INNER, "zo"), plane(WO, "zo"), relay(WO, "zb"),),
+        5: lambda: (relay(WO, "za"), onward(OUTER), plane(OUTER, "zb"),),
         6: lambda: (share(INNER, "zb"),),
-        7: lambda: (share(INNER, "za"), relay(OUTER, "zb"), plane(OUTER, "zo"),),
-        8: lambda: (relay(OUTER, "za"),),
-        9: lambda: (relay(OUTER, "zo"),),
-        10: lambda: (share(INNER, "zo"),),
-        11: lambda: (share(OUTER, "zb"),),
+        7: lambda: (relay(WO, "zo"), plane(OUTER, "za"),),
+        8: lambda: (share(INNER, "za"),),
+        9: lambda: (share(INNER, "zo"), relay(OUTER, "zb"), plane(OUTER, "zo"),),
+        10: lambda: (share(WO, "zb", "za"),),
+        11: lambda: (relay(OUTER, "za"), share(WO, "zo"), relay(OUTER, "zo"),),
     }
     later = {
-        0: lambda: (share(OUTER, "zo"),),
+        1: lambda: (share(OUTER, "za", "zo"),),
     }
 
     def after_residual():
-        share(OUTER, "za")
+        share(OUTER, "zb")
 
     def at_step(i, table):
         for k, step in table.items():
@@ -600,21 +596,33 @@
     lax.fori_loop(0, res.shape[0] // block, one, 0)
 
 
-JOBS = ((0, 4, True), (4, 4, False), (8, 1, False), (9, 1, False), (10, 1, False), (11, 1, False))
-REDUCE_COPIES = 9 * len(JOBS) + (4 + 4 + 4) + 7
-JOB_BUFFERS = 7
+JOBS = (
+    (4, 1, False),
+    (5, 1, True),
+    (6, 1, True),
+    (7, 1, False),
+    (0, 2, True),
+    (2, 2, False),
+    (8, 1, False),
+    (9, 1, False),
+    (10, 1, False),
+    (11, 1, False),
+)
+OUTER_UNITS = 4
+REDUCE_COPIES = 9 * len(JOBS) + sum(first >= OUTER_UNITS for first, _, _ in JOBS) + 4 + 7
 
 
 def job_shapes(units, ring_first):
-    big, part, tile = (4, units, TR, D), (units, 48, 384), (units, TR, D)
+    part, tile = (units, 48, 384), (units, TR, D)
     first = tile if ring_first else (4, *part)
-    return [big, big, first, first, first, first, part, part, part]
+    return [first, first, first, first, part, part, part]
 
 
 class Job:
-    def __init__(self, net, p, k, first, units, ring_first, source, bufs, result):
-        self.net, self.p, self.k, self.ring_first = net, p, k, ring_first
-        self.held, self.landed, self.d1, self.a1, self.b1, self.mid, self.d2, self.a2, self.b2 = bufs
+    def __init__(self, net, p, k, first, units, ring_first, held, landed, arrivals, bufs, result):
+        self.net, self.p, self.k = net, p, k
+        self.held, self.landed, self.arrivals = held, landed, arrivals
+        self.d1, self.a1, self.b1, self.mid, self.d2, self.a2, self.b2 = bufs
         self.result = result
         self.units = slice(first, first + units)
         held, mid = self.held, self.mid
@@ -640,9 +648,6 @@
         self.one, self.two = one, two
         self.own1 = z if ring_first else p.w
         self.own2 = p.w if ring_first else z
-        self.parts = len(source)
-        for j, make in enumerate(source):
-            net.define((k, "c", j), lambda make=make: (*make(self.landed), p.sib))
         for stage, at, way, d, a, b in ((1, self.at1, one, self.d1, self.a1, self.b1), (2, self.at2, two, self.d2, self.a2, self.b2)):
             relayed, direct, opposite, dev_o, dev_r, dev_d = way
 
@@ -677,11 +682,11 @@
     def wait(self, *names):
         self.net.wait(*self.names(names))
 
-    def send(self, j=0):
-        self.start(("c", j))
+    def send(self):
+        self.net.start(*self.arrivals)
 
     def pair(self):
-        self.wait(*[("c", j) for j in range(self.parts)])
+        self.net.wait(*self.arrivals)
         held, landed = self.held, self.landed
 
         def one(t, _):
@@ -746,37 +751,49 @@
     }
 
     def block_copy(j):
-        return pltpu.make_async_copy(ai_in.at[j], qkv.at[j % 3], lsem.at[len(loads) + j % 3])
+        return pltpu.make_async_copy(ai_in.at[(j + 4) % 8], qkv.at[j % 3], lsem.at[len(loads) + j % 3])
 
     def in_copy(i, slot):
         c, r, pair = place_of(i)
         return pltpu.make_async_copy(e_in.at[c, r, pair], ebuf.at[slot], esem.at[slot])
 
-    load["og"]().start()
+    load["hl"]().start()
     block_copy(0).start()
     block_copy(1).start()
-    load["hl"]().start()
+    load["og"]().start()
     for name in ("att", "bg", "dos"):
         load[name]().start()
     in_copy(0, 0).start()
     load["res"]().start()
 
-    def staged(k, j):
-        return fa.at[2 * k + j // 2, 4 * (j % 2) : 4 * (j % 2) + 4]
-
+    def staged(j):
+        return fa.at[j // 2, 4 * (j % 2) : 4 * (j % 2) + 4]
+
+    net = Net(ssem, rsem)
+    held_outer, landed_outer, held_rest, landed_rest = bufs[0:4]
     jobs = []
-    net = Net(ssem, rsem)
-    per = 9
+    per = 7
+    outer_arrivals = [("o", j) for j in range(4)]
+    for j in range(4):
+        net.define(("o", j), lambda j=j: (staged(4 + j), landed_outer.at[j], p.sib))
     for k, (first, units, ring_first) in enumerate(JOBS):
-        if k == 0:
-            source = [lambda landed, j=j: (staged(0, j), landed.at[j]) for j in range(4)]
-        elif k == 1:
-            source = [lambda landed, j=j: (staged(1, j), landed.at[:, j]) for j in range(4)]
-        elif k == 2:
-            source = [lambda landed: (go.at[:, 1 - p.c], landed)]
+        if first < OUTER_UNITS:
+            held, landed = held_outer.at[:, first : first + units], landed_outer.at[:, first : first + units]
+            arrivals = outer_arrivals
+            outer_arrivals = []
         else:
-            source = [lambda landed, c=k - 3: (gx.at[c, :, 1 - p.c], landed)]
-        jobs.append(Job(net, p, k, first, units, ring_first, source, bufs[per * k : per * (k + 1)], result))
+            r = first - OUTER_UNITS
+            held, landed = held_rest.at[r], landed_rest.at[r]
+            arrivals = [(k, "c")]
+            if r < 4:
+                source = lambda r=r: staged(r)
+            elif r == 4:
+                source = lambda: go.at[:, 1 - p.c, 0]
+            else:
+                source = lambda c=r - 5: gx.at[c, :, 1 - p.c, 0]
+            net.define((k, "c"), lambda source=source, landed=landed: (source(), landed.at[:, 0], p.sib))
+        job_bufs = bufs[4 + per * k : 4 + per * (k + 1)]
+        jobs.append(Job(net, p, k, first, units, ring_first, held, landed, arrivals, job_bufs, result))
     net.define(("v", "c"), lambda: (vt.at[:, 1 - p.c], vrecv, p.sib))
     for k, device in enumerate((p.plane_a, p.plane_b, (p.wd, p.s))):
         net.define(("v", "p", k), lambda device=device: (vheld.at[0], vplane.at[p.w], device))
@@ -785,62 +802,66 @@
         net.define(("v", "z", k), lambda to=to: (vheld.at[1, to], vz.at[p.z], (p.w, 2 * to + p.c)))
     assert len(net.made) == REDUCE_COPIES, len(net.made)
 
+    def own_half(k, source):
+        jobs[k].held[...] = source[:, p.c]
+
+    def begin(k):
+        first = JOBS[k][0]
+        if first == 8:
+            own_half(k, go)
+        elif first > 8:
+            own_half(k, gx.at[first - 9])
+        jobs[k].pair()
+
     first_core = p.c == 0
+    after = {
+        0: lambda: (jobs[0].send(),),
+        1: lambda: (jobs[1].send(),),
+        2: lambda: (jobs[2].send(),),
+        3: lambda: (jobs[3].send(), begin(0),),
+        4: lambda: (net.start(("o", 0)), begin(1),),
+        5: lambda: (net.start(("o", 1)), begin(2),),
+        6: lambda: (net.start(("o", 2)), jobs[0].relay(1), begin(3),),
+        7: lambda: (net.start(("o", 3)),),
+    }
     for j in range(8):
         if j == 0:
+            load["hl"]().wait()
+        if j == 4:
             load["og"]().wait()
-        if j == 4:
-            load["hl"]().wait()
         if j + 2 < 8:
             block_copy(j + 2).start()
         block_copy(j).wait()
         block = qkv.at[j % 3]
         if j < 4:
+            tiles = mm(hl[...], block[...], TN).astype(BF).reshape(4, 2, TR, D)
+            zero, one = tiles[:, 0], tiles[:, 1]
+            held_rest[j, :, 0] = jnp.where(first_core, zero, one)
+        else:
             tiles = mm(block[...], og[...], TN).astype(BF).reshape(2, 4, TR, D)
             zero, one = tiles[0], tiles[1]
-            jobs[0].held[j] = jnp.where(first_core, zero, one)
-        else:
-            tiles = mm(hl[...], block[...], TN).astype(BF).reshape(4, 2, TR, D)
-            zero, one = tiles[:, 0], tiles[:, 1]
-            jobs[1].held[:, j - 4] = jnp.where(first_core, zero, one)
-        staged(j // 4, j % 4)[...] = jnp.where(first_core, one, zero)
+            held_outer[j - 4] = jnp.where(first_core, zero, one)
+        staged(j)[...] = jnp.where(first_core, one, zero)
         if j == 0:
             answer(others(p))
-        jobs[j // 4].send(j % 4)
-        if j == 4:
-            jobs[0].pair()
+        if j in after:
+            after[j]()
     load["qkv"]().start()
     sums[...] = sums_in[...]
     load["att"]().wait()
     load["bg"]().wait()
     go[...] = mm(att[...], bg[...], TN).astype(BF).reshape(4, 2, 1, TR, D)
-    jobs[2].send()
-    jobs[1].pair()
-
-    def own_half(k, source):
-        jobs[k].held[...] = source[:, p.c]
-
-    own_half(2, go)
+    jobs[6].send()
     load["qkv"]().wait()
     load["dos"]().wait()
-    jobs[2].pair()
-
-    def begin(k):
-        own_half(k, gx.at[k - 3])
-        jobs[k].pair()
-
-    a, b, w, c0, c1, c2 = jobs
     steps = {
-        2: lambda: w.relay(1),
-        3: lambda: c0.send(),
-        4: lambda: (b.relay(1), begin(3), w.turn()),
-        5: lambda: a.relay(1),
-        6: lambda: (w.relay(2), c0.relay(1)),
-        7: lambda: (c1.send(), w.share()),
-        8: lambda: (b.turn(), begin(4), c0.turn()),
-        9: lambda: (a.turn(), b.relay(2), w.pass_on()),
-        10: lambda: (c1.relay(1), c0.relay(2), b.share()),
-        11: lambda: (c2.send(), a.relay(2), c0.share(), c1.turn()),
+        1: lambda: (jobs[0].turn(), jobs[1].relay(1), jobs[3].relay(1), begin(4), begin(5),),
+        2: lambda: (begin(6),),
+        3: lambda: (jobs[7].send(), jobs[2].relay(1), jobs[0].relay(2), jobs[3].turn(),),
+        5: lambda: (jobs[5].relay(1),),
+        6: lambda: (begin(7),),
+        7: lambda: (jobs[8].send(), jobs[1].turn(),),
+        8: lambda: (jobs[6].relay(1),),
     }
 
     def one(i, _):
@@ -864,11 +885,16 @@
         return 0
 
     lax.fori_loop(0, n, one, 0)
-
-    for k in range(2):
-        for j in range(4):
-            net.copy((k, "c", j)).wait_send()
-            net.sent.add((k, "c", j))
+    jobs[9].send()
+    jobs[5].turn()
+    jobs[7].relay(1)
+    begin(8)
+    jobs[4].relay(1)
+    jobs[6].turn()
+    staged_names = [(k, "c") for k, job in enumerate(JOBS) if 4 <= job[0] < 8] + [("o", j) for j in range(4)]
+    for name in staged_names:
+        net.copy(name).wait_send()
+        net.sent.add(name)
     load["fa"]().start()
 
     for s in range(8):
@@ -877,18 +903,7 @@
         for r in range(3):
             vt[s // 2, s % 2, 8 + r : 9 + r] = bsum[0:1, 128 * (3 * s + r) : 128 * (3 * s + r + 1)]
     net.start(("v", "c"))
-    begin(5)
-    a.share()
-    b.pass_on()
-    c0.pass_on()
-    c1.relay(2)
-    net.wait(("v", "c"))
-    vheld[0] = vt[:, p.c] + vrecv[...]
-    vplane[p.w] = vheld[0]
-    net.start(*[("v", "p", k) for k in range(3)])
     load["res"]().wait()
-    load["fa"]().wait()
-    c2.relay(1)
 
     def back(i):
         at = pl.ds(256 * i, 256)
@@ -897,23 +912,58 @@
             total = total + mm(dqkv[c, at], fa[c].reshape(D, D), NT)
         out[at] = total.astype(BF)
 
+    load["fa"]().wait()
     back(0)
-    a.pass_on()
-    c1.share()
-    c2.turn()
+    jobs[1].relay(2)
+    net.wait(("v", "c"))
+    vheld[0] = vt[:, p.c] + vrecv[...]
+    vplane[p.w] = vheld[0]
+    net.start(*[("v", "p", k) for k in range(3)])
+    back(1)
+    jobs[2].turn()
+    back(2)
+    jobs[0].share()
+    begin(9)
     net.wait(*[("v", "p", k) for k in range(3)])
     vheld[1] = (vplane[0] + vplane[1]) + (vplane[2] + vplane[3])
     vz[p.z] = vheld[1, p.z]
     net.start(*[("v", "z", k) for k in range(1, 4)])
-    back(1)
-    c1.pass_on()
-    c2.relay(2)
-    back(2)
-    c2.share()
     back(3)
+    jobs[3].relay(2)
+    jobs[7].turn()
+    jobs[8].relay(1)
+    jobs[1].share()
+    jobs[5].relay(2)
+    jobs[2].relay(2)
+    jobs[0].pass_on()
+    jobs[9].relay(1)
+    jobs[8].turn()
+    jobs[2].share()
+    jobs[4].turn()
+    jobs[6].relay(2)
+    jobs[1].pass_on()
+    jobs[3].share()
+    jobs[7].relay(2)
+    jobs[9].turn()
+    jobs[2].pass_on()
+    jobs[5].share()
+    jobs[4].relay(2)
+    jobs[8].relay(2)
+    jobs[6].share()
+    jobs[7].share()
+    jobs[3].pass_on()
+    jobs[9].relay(2)
+    jobs[5].pass_on()
+    jobs[8].share()
+    jobs[6].pass_on()
+    jobs[4].share()
+    jobs[7].pass_on()
     net.wait(*[("v", "z", k) for k in range(1, 4)])
     ovec[...] = (vz[0] + vz[1]) + (vz[2] + vz[3])
-    c2.pass_on()
+    jobs[9].share()
+    jobs[8].pass_on()
+    jobs[4].pass_on()
+    jobs[9].pass_on()
     for job in jobs:
         job.end()
     net.finish()
@@ -921,7 +971,8 @@
 
 def backward(x, qkv, e, att, dos, bg, res, fa, hl, og, ai, sums, bsum):
     t = x.shape[0]
-    job_scratch = [pltpu.VMEM(s, BF) for _, units, ring_first in JOBS for s in job_shapes(units, ring_first)]
+    job_scratch = [pltpu.VMEM(s, BF) for s in ((4, 4, TR, D),) * 2 + ((8, 4, 1, TR, D),) * 2]
+    job_scratch += [pltpu.VMEM(s, BF) for _, units, ring_first in JOBS for s in job_shapes(units, ring_first)]
     return pl.pallas_call(
         backward_kernel,
         out_shape=(shape(t, D), shape(12, TR, D), shape(16, 128, dtype=F32)),

time: 222 us -> 195 us (0.88)
  Pallas kernels: 215 us -> 188 us
    pallas_call x1, Pallas kernels: 110 us -> 87.2 us  [backward(): pl.pallas_call(backward_kernel, out_shape=(shape(t, D), shape(12, TR, D),...]
    pallas_call x1, Pallas kernels: 100 us -> 96.8 us  [forward(): pl.pallas_call(forward_kernel, out_shape=(shape(8, D, dtype=F32), shape(1...]
where the time goes in v5:
time: 195 us
  Pallas kernels  188 us (96%)
  other arithmetic  4.05 us (2%)
    pallas_call x1, Pallas kernels, forward(): pl.pallas_call(forward_kernel, out_shape=(shape(8, D, dtype=F32), shape(1...  96.8 us
    pallas_call x1, Pallas kernels, backward(): pl.pallas_call(backward_kernel, out_shape=(shape(t, D), shape(12, TR, D),...  87.2 us
    pallas_call x1, Pallas kernels, finish(): pl.pallas_call(finish_kernel, out_shape=tuple((shape(TR, D, dtype=F32) fo...  4.44 us

profile of v5, /device:TPU:0, one launch (start us, length us, event | category | flops | bytes accessed | tf_op | source)
XLA Modules:
  0.0 195.1 jit_solution(11188192111580465737)
XLA Ops:
  1.3 0.1 pad.4.clone
  1.4 0.7 convert_bitcast_fusion
  2.1 0.7 convert_bitcast_fusion.7
  2.7 0.7 convert_bitcast_fusion.5
  3.4 0.7 convert_bitcast_fusion.3
  4.1 0.7 convert_bitcast_fusion.1
  4.8 0.7 fusion.2.vec
  5.5 96.8 %forward.1 = (f32[8,768]{1,0:T(8,128)}, f32[1,3072]{1,0:T(1,128)}, bf16[3,8,96,768]{3,2,1,0:T(8,128)(2,1)}, bf16[3,1024,768]{2,1,0:T(8,128)(2,1)}, bf16[1024,768...) custom-call(bf16[1024,768]{1,0:T(8,128)(2,1)} %x.5, ...), custom_call_target="tpu_custom_call" | custom-call | tf_op jit(solution)/shard_map/forward/pallas_call | solution.py:516
  102.3 87.2 %backward.1 = (bf16[1024,768]{1,0:T(8,128)(2,1)}, bf16[12,96,768]{2,1,0:T(8,128)(2,1)}, f32[16,128]{1,0:T(8,128)}) custom-call(bf16[1024,768]{1,0:T(8,128)(2,1)} %x.5, bf16[3,1024,768]{2,1,0:T(8,128)(2,1)} %get-tuple-element.50.qkv_in, bf16[3,2,2,2,512,512]{5,4,3,2,1,0:T(8,128)(2,1)} %get-tuple-element.51.e_in, bf16[1024,768]{1,0:T(8,128)(2,1)} %get-tuple-element.52.att_in, ...), custom_call_target="tpu_custom_call" | custom-call | tf_op jit(solution)/shard_map/backward/pallas_call | solution.py:976
  189.5 0.0 copy-start
  189.5 4.4 %finish.1 = (f32[96,768]{1,0:T(8,128)}, f32[96,768]{1,0:T(8,128)}, f32[96,768]{1,0:T(8,128)}, f32[96,768]{1,0:T(8,128)}, f32[96,3072]{1,0:T(8,128)}, /*index=5*/...) custom-call(bf16[12,96,768]{2,1,0:T(8,128)(2,1)} %get-tuple-element., ...), custom_call_target="tpu_custom_call" | custom-call | tf_op jit(solution)/shard_map/finish/pallas_call | solution.py:1029
  194.0 0.0 copy-done
  194.0 1.1 copy.38
  (2 shorter events, 0.0 us)
Async XLA Ops:
  189.5 4.5 %copy-start = (bf16[1024,768]{1,0:T(8,128)(2,1)S(1)}, bf16[1024,768]{1,0:T(8,128)(2,1)}, u32[]{:S(2)}) copy-start(bf16[1024,768]{1,0:T(8,128)(2,1)} %get-tuple-element.106) | copy-start | bytes 4718596

commit v6 on v5

--- a/solution.py
+++ b/solution.py
@@ -256,7 +256,15 @@
         gp[j, at] = (keep * phi + masked * (RSQRT2PI * jnp.exp(-0.5 * (inner * inner)))).astype(BF)
 
 
-def ffn_outer(i, block, t1, grad, rows, kept, wi, wr, wo, inv, act, gp, y, bg, dos, og, sums, bsum):
+def outer_product(i, block, wr, act, ob):
+    at = rows_of(i, block)
+    outer = jnp.zeros((block, D), F32)
+    for j in range(4):
+        outer = outer + mm(act[j, at], wr[2 * j : 2 * j + 2].reshape(D, D))
+    ob[...] = outer
+
+
+def ffn_outer(i, block, blocks, t1, grad, rows, kept, wi, wr, wo, inv, act, gp, ob, y, bg, dos, og, sums, bsum):
     at = rows_of(i, block)
 
     def add(k, value):
@@ -265,12 +273,10 @@
     def outer_weight(j):
         return wr[2 * j : 2 * j + 2].reshape(D, D)
 
-    outer = jnp.zeros((block, D), F32)
-    for j in range(4):
-        outer = outer + mm(act[j, at], outer_weight(j))
     n1, inv1 = norm_rows(t1[at])
     hidden = n1 * rows[3:4] + rows[4:5]
-    n2, inv2 = norm_rows(hidden + (outer + rows[5:6]))
+    n2, inv2 = norm_rows(hidden + (ob[...] + rows[5:6]))
+    outer_product(jnp.minimum(i + 1, blocks - 1), block, wr, act, ob)
     y[at] = (n2 * rows[6:7] + rows[7:8]).astype(BF)
     top = grad[at].astype(F32)
     add(7, top)
@@ -298,10 +304,10 @@
 
 
 def forward_kernel(
-    x, seg, kept, wq, wk, wv, wo, wi, wr, vec, grad_in,
+    x, seg, kept, wq, wk, wv, wo, wi, wr, v0, v1, v2, v3, v4, v5, v6, v7, v_inner, grad_in,
     sums, bsum, fa_out, qkv_out, att_out, e_out, y_out, res_out, bg_out, dos_out, hl_out, og_out, ai_out,
-    own, fa, fi, fo, fv, rows, binner, att, inv, t1, segt, ebuf, grad, y, bg, dos, hl, og, act, gp,
-    ssem, rsem, lsem, esem,
+    own, vtile, vec, fa, fi, fo, fv, rows, binner, att, inv, t1, segt, ebuf, grad, y, bg, dos, hl, og, act, gp, ob,
+    ssem, rsem, lsem, esem, fsem,
 ):
     qkv = gp.at[0:3]
     p = Place()
@@ -312,6 +318,12 @@
             own[c, :, part * CW : (part + 1) * CW] = ref[:, c * CW : (c + 1) * CW].astype(BF)
 
     cast(0)
+    vtile[...] = jnp.zeros_like(vtile)
+    for k, ref in enumerate((v0, v1, v2, v3, v4, v5, v6, v7)):
+        vtile[k : k + 1, 0:TR] = ref[...]
+    for r in range(3):
+        vtile[8 + r : 9 + r] = v_inner[128 * r : 128 * (r + 1)].reshape(1, 128)
+    vec[...] = vtile[...].astype(BF)
     answer(others(p))
     net = gather_net(p, own, fa, fi, fo, vec, fv, ssem, rsem)
     names = ("zb", "za", "zo")
@@ -367,12 +379,6 @@
         ("att", lambda: att, lambda: att_out),
         ("hl", lambda: hl, lambda: hl_out),
         ("act", lambda: act, lambda: ai_out.at[0:4]),
-        ("ig", lambda: gp, lambda: ai_out.at[4:8]),
-        ("og", lambda: og, lambda: og_out),
-        ("y", lambda: y, lambda: y_out),
-        ("res", lambda: t1, lambda: res_out),
-        ("bg", lambda: bg, lambda: bg_out),
-        ("dos", lambda: dos, lambda: dos_out),
     )
     for k, (name, src, dst) in enumerate(pieces):
         put(name, k, src, dst)
@@ -496,21 +502,34 @@
     local["own o"]().wait()
     local["grad"]().wait()
 
+    def flush(i):
+        at = rows_of(i, block)
+        pairs = (
+            (gp.at[:, at], ai_out.at[4:8, at]), (og.at[at], og_out.at[at]), (dos.at[at], dos_out.at[at]),
+            (bg.at[at], bg_out.at[at]), (t1.at[at], res_out.at[at]), (y.at[at], y_out.at[at]),
+        )
+        return [pltpu.make_async_copy(src, dst, fsem.at[i, k]) for k, (src, dst) in enumerate(pairs)]
+
     def second(i, _):
-        ffn_outer(i, block, t1, grad, rows, keep, fi, fo, fa[3].reshape(D, D), inv, act, gp, y, bg, dos, og, sums, bsum)
+        wo = fa[3].reshape(D, D)
+        ffn_outer(i, block, blocks, t1, grad, rows, keep, fi, fo, wo, inv, act, gp, ob, y, bg, dos, og, sums, bsum)
+        for copy in flush(i):
+            copy.start()
         return 0
 
+    outer_product(0, block, fo, act, ob)
     lax.fori_loop(0, blocks, second, 0)
-    for name in ("og", "ig", "dos", "bg", "res", "y"):
-        local[name]().start()
     out_copy(n - 2, (n - 2) % 2).wait()
     out_copy(n - 1, (n - 1) % 2).wait()
-    for name in ("fa", "att", "hl", "act", "og", "ig", "dos", "bg", "res", "y"):
+    for name in ("fa", "att", "hl", "act"):
         local[name]().wait()
+    for i in range(blocks):
+        for copy in flush(i):
+            copy.wait()
     net.finish()
 
 
-def forward(x, seg, kept, wq, wk, wv, wo, wi, wr, vec, grad):
+def forward(x, seg, kept, wq, wk, wv, wo, wi, wr, eight, b_inner, grad):
     t = x.shape[0]
     n = t // SEQ
     return pl.pallas_call(
@@ -520,10 +539,12 @@
             shape(3, n, 2, 2, SEQ, SEQ), shape(t, D), shape(t, D, dtype=F32), shape(t, D), shape(t, D), shape(t, D),
             shape(t, D), shape(8, t, D),
         ),
-        in_specs=[VM, VM, SM] + [VM] * 7 + [ANY],
+        in_specs=[VM, VM, SM] + [VM] * 15 + [ANY],
         out_specs=(VM, VM) + (ANY,) * 11,
         scratch_shapes=[
             pltpu.VMEM((12, TR, D), BF),
+            pltpu.VMEM((16, 128), F32),
+            pltpu.VMEM((16, 128), BF),
             pltpu.VMEM((4, 8, TR, D), BF),
             pltpu.VMEM((4, 8, TR, D), BF),
             pltpu.VMEM((8, 4, TR, D), BF),
@@ -539,14 +560,16 @@
         + [pltpu.VMEM((t, D), BF)] * 6
         + [pltpu.VMEM((4, t, D), BF)] * 2
         + [
+            pltpu.VMEM((256, D), F32),
             pltpu.SemaphoreType.DMA((GATHER_COPIES,)),
             pltpu.SemaphoreType.DMA((GATHER_COPIES,)),
-            pltpu.SemaphoreType.DMA((16,)),
+            pltpu.SemaphoreType.DMA((10,)),
             pltpu.SemaphoreType.DMA((2,)),
+            pltpu.SemaphoreType.DMA((t // 256, 6)),
         ],
         compiler_params=params(collective_id=0, has_side_effects=True),
         name="forward",
-    )(x, seg, kept, wq, wk, wv, wo, wi, wr, vec, grad)
+    )(x, seg, kept, wq, wk, wv, wo, wi, wr, *(a.reshape(1, TR) for a in eight), b_inner, grad)
 
 
 def attend_back(i, qkv, dos, att, ebuf, dqkv):
@@ -1008,7 +1031,7 @@
     )(x, qkv, e, att, dos, bg, res, fa, hl, og, ai, sums, bsum)
 
 
-def finish_kernel(result, ovec, inp, oq, ok, ov, oo, oi, our, out, *vectors):
+def finish_kernel(result, ovec, inp, y, oq, ok, ov, oo, oi, our, out, y_out, *vectors):
     for c in range(3):
         tile = result[9 + c].astype(F32)
         for part, ref in enumerate((oq, ok, ov)):
@@ -1016,27 +1039,43 @@
     oo[...] = result[8].astype(F32)
     for q in range(4):
         oi[:, q * D : (q + 1) * D] = result[4 + q].astype(F32)
-        our[q * TR : (q + 1) * TR, :] = result[q].astype(F32)
+        our[q] = result[q].astype(F32)
     out[...] = inp[...]
+    y_out[...] = y[...]
     for k in range(8):
         vectors[k][...] = ovec[k, 0:TR]
     for r in range(3):
         vectors[8][128 * r : 128 * (r + 1)] = ovec[8 + r]
 
 
-def finish(result, ovec, inp):
+def finish(result, ovec, inp, y):
     t = inp.shape[0]
-    return pl.pallas_call(
+    steps = 2
+    rows = TR // steps
+
+    def part(*dims):
+        at = len(dims) - 2
+        return pl.BlockSpec(dims, lambda h: tuple(h if k == at else 0 for k in range(len(dims))))
+
+    def vector(n):
+        return pl.BlockSpec((n,), lambda h: (0,))
+
+    *outs, gr, out, y, v0, v1, v2, v3, v4, v5, v6, v7, v8 = pl.pallas_call(
         finish_kernel,
+        grid=(steps,),
         out_shape=tuple(shape(TR, D, dtype=F32) for _ in range(4))
-        + (shape(TR, FF, dtype=F32), shape(4 * TR, D, dtype=F32), shape(t, D))
+        + (shape(TR, FF, dtype=F32), shape(4, TR, D, dtype=F32), shape(t, D), shape(t, D))
         + tuple(shape(TR, dtype=F32) for _ in range(8))
         + (shape(4 * TR, dtype=F32),),
-        in_specs=[VM] * 3,
-        out_specs=(VM,) * 16,
+        in_specs=[part(12, rows, D), pl.BlockSpec((16, 128), lambda h: (0, 0)), part(t // steps, D), part(t // steps, D)],
+        out_specs=(part(rows, D),) * 4
+        + (part(rows, FF), part(4, rows, D), part(t // steps, D), part(t // steps, D))
+        + (vector(TR),) * 8
+        + (vector(4 * TR),),
         compiler_params=params(),
         name="finish",
-    )(result, ovec, inp)
+    )(result, ovec, inp, y)
+    return *outs, gr.reshape(4 * TR, D), out, y, v0, v1, v2, v3, v4, v5, v6, v7, v8
 
 
 def forward_local_kernel(x, seg, kept, fa, rows, qkv, att, inv, e_out, t1, segt, ebuf, esem):
@@ -1074,7 +1113,7 @@
 
 
 def ffn_local_kernel(
-    t1, grad, rows, binner, kept, inv, fi, fo, fa, y, res, bg, dos, sums, bsum, g, hl, og, act, gp, t2, tile, gsem, block=256
+    t1, grad, rows, binner, kept, inv, fi, fo, fa, y, res, bg, dos, sums, bsum, g, hl, og, act, gp, t2, ob, tile, gsem, block=256
 ):
     sums[...] = jnp.zeros_like(sums)
     bsum[...] = jnp.zeros_like(bsum)
@@ -1087,10 +1126,11 @@
 
     def second(i, _):
         wo = fa[3].reshape(D, D)
-        ffn_outer(i, block, t2, grad, rows, kept[0], fi, fo, wo, inv, act, gp, y, bg, dos, og, sums, bsum)
+        ffn_outer(i, block, blocks, t2, grad, rows, kept[0], fi, fo, wo, inv, act, gp, ob, y, bg, dos, og, sums, bsum)
         return 0
 
     lax.fori_loop(0, blocks, first, 0)
+    outer_product(0, block, fo, act, ob)
     lax.fori_loop(0, blocks, second, 0)
     res[...] = t2[...]
 
@@ -1120,7 +1160,8 @@
         out_specs=(VM,) * 6 + (ANY,),
         scratch_shapes=[
             pltpu.VMEM((t, D), BF), pltpu.VMEM((t, D), BF), pltpu.VMEM((4, t, D), BF), pltpu.VMEM((4, t, D), BF),
-            pltpu.VMEM((t, D), F32), pltpu.VMEM((2, 4, TR, D), BF), pltpu.SemaphoreType.DMA((1,)),
+            pltpu.VMEM((t, D), F32), pltpu.VMEM((256, D), F32), pltpu.VMEM((2, 4, TR, D), BF),
+            pltpu.SemaphoreType.DMA((1,)),
         ],
         compiler_params=params(),
         name="ffn_local",
@@ -1197,10 +1238,8 @@
     weights = (w_query, w_key, w_value, w_out, w_inner, w_outer)
     own_kernels = lax.axis_size("width") == 4 and lax.axis_size("shard") == 8
     if own_kernels:
-        vec = jnp.concatenate([jnp.stack(eight), jnp.zeros((8, 128 - TR), F32)], axis=1)
-        vec = jnp.concatenate([vec, b_inner.reshape(3, 128), jnp.zeros((5, 128), F32)], axis=0).astype(BF)
         sums, bsum, fa, qkv, att, e, y, res, bg, dos, hl, og, ai = forward(
-            layer_input, segment_ids, group_heads, *weights, vec, out_grad
+            layer_input, segment_ids, group_heads, *weights, eight, b_inner, out_grad
         )
     else:
         fa, fi, fo, rows, binner = gather_lax(*weights, eight, b_inner)
@@ -1208,7 +1247,7 @@
         y, res, bg, dos, sums, bsum, g = ffn_local(t1, out_grad, rows, binner, group_heads, inv, fi, fo, fa)
     if own_kernels:
         input_grad, result, ovec = backward(layer_input, qkv, e, att, dos, bg, res, fa, hl, og, ai, sums, bsum)
-        gq, gk, gv, go, gi, gr, input_grad, *vectors = finish(result, ovec, input_grad)
+        gq, gk, gv, go, gi, gr, input_grad, y, *vectors = finish(result, ovec, input_grad, y)
     else:
         input_grad, gx, go, sums = backward_local(layer_input, qkv, e, att, dos, bg, res, fa[0:3], sums)
         (gq, gk, gv, go, gi, gr), vectors = reduce_lax(g, gx, go, sums, bsum)

time: 195 us -> 185 us (0.949)
  other arithmetic: 4.05 us -> 0 us
  Pallas kernels: 188 us -> 184 us
    pallas_call x1, Pallas kernels: 96.8 us -> 91.8 us  [forward(): pl.pallas_call(forward_kernel, out_shape=(shape(8, D, dtype=F32), shape(1...]
    another operation x4 -> x0, other arithmetic: 2.7 us -> none  [body(): jnp.stack(eight)]
where the time goes in v6:
time: 185 us
  Pallas kernels  184 us (99%)
    pallas_call x1, Pallas kernels, forward(): pl.pallas_call(forward_kernel, out_shape=(shape(8, D, dtype=F32), shape(1...  91.8 us
    pallas_call x1, Pallas kernels, backward(): pl.pallas_call(backward_kernel, out_shape=(shape(t, D), shape(12, TR, D),...  87.3 us
    pallas_call x1, Pallas kernels, finish(): pl.pallas_call(finish_kernel, grid=(steps,), out_shape=tuple((shape(TR, D...  4.6 us

profile of v6, /device:TPU:0, one launch (start us, length us, event | category | flops | bytes accessed | tf_op | source)
XLA Modules:
  0.0 185.2 jit_solution(5423328539838229704)
XLA Ops:
  1.3 91.8 %forward.1 = (f32[8,768]{1,0:T(8,128)}, f32[1,3072]{1,0:T(1,128)}, bf16[3,8,96,768]{3,2,1,0:T(8,128)(2,1)}, bf16[3,1024,768]{2,1,0:T(8,128)(2,1)}, bf16[1024,768...) custom-call(bf16[1024,768]{1,0:T(8,128)(2,1)} %x.3, ...), custom_call_target="tpu_custom_call" | custom-call | tf_op jit(solution)/shard_map/forward/pallas_call | solution.py:535
  93.1 87.3 %backward.1 = (bf16[1024,768]{1,0:T(8,128)(2,1)}, bf16[12,96,768]{2,1,0:T(8,128)(2,1)}, f32[16,128]{1,0:T(8,128)}) custom-call(bf16[1024,768]{1,0:T(8,128)(2,1)} %x.3, bf16[3,1024,768]{2,1,0:T(8,128)(2,1)} %get-tuple-element.50.qkv_in, bf16[3,2,2,2,512,512]{5,4,3,2,1,0:T(8,128)(2,1)} %get-tuple-element.51.e_in, bf16[1024,768]{1,0:T(8,128)(2,1)} %get-tuple-element.52.att_in, ...), custom_call_target="tpu_custom_call" | custom-call | tf_op jit(solution)/shard_map/backward/pallas_call | solution.py:999
  180.4 4.6 %finish.1 = (f32[96,768]{1,0:T(8,128)}, f32[96,768]{1,0:T(8,128)}, f32[96,768]{1,0:T(8,128)}, f32[96,768]{1,0:T(8,128)}, f32[96,3072]{1,0:T(8,128)}, /*index=5*/...) custom-call(bf16[12,96,768]{2,1,0:T(8,128)(2,1)} %get-tuple-element., ...), custom_call_target="tpu_custom_call" | custom-call | tf_op jit(solution)/shard_map/finish/pallas_call | solution.py:1063

commit v7 on v6

--- a/solution.py
+++ b/solution.py
@@ -304,19 +304,29 @@
 
 
 def forward_kernel(
-    x, seg, kept, wq, wk, wv, wo, wi, wr, v0, v1, v2, v3, v4, v5, v6, v7, v_inner, grad_in,
+    x_in, seg, kept, wq_in, wk_in, wv_in, wo_in, wi_in, wr_in, v0, v1, v2, v3, v4, v5, v6, v7, v_inner, grad_in,
     sums, bsum, fa_out, qkv_out, att_out, e_out, y_out, res_out, bg_out, dos_out, hl_out, og_out, ai_out,
     own, vtile, vec, fa, fi, fo, fv, rows, binner, att, inv, t1, segt, ebuf, grad, y, bg, dos, hl, og, act, gp, ob,
-    ssem, rsem, lsem, esem, fsem,
+    x, wq, wk, wv, wo, wi, wr, ssem, rsem, lsem, esem, fsem, isem,
 ):
     qkv = gp.at[0:3]
     p = Place()
     call(others(p))
+    arriving = [
+        pltpu.make_async_copy(src, dst, isem.at[k])
+        for k, (src, dst) in enumerate(
+            ((wq_in, wq), (wk_in, wk), (wv_in, wv), (wo_in, wo), (wi_in, wi), (wr_in, wr), (x_in, x))
+        )
+    ]
+    for copy in arriving:
+        copy.start()
 
     def cast(c):
         for part, ref in enumerate((wq, wk, wv)):
             own[c, :, part * CW : (part + 1) * CW] = ref[:, c * CW : (c + 1) * CW].astype(BF)
 
+    for copy in arriving[0:3]:
+        copy.wait()
     cast(0)
     vtile[...] = jnp.zeros_like(vtile)
     for k, ref in enumerate((v0, v1, v2, v3, v4, v5, v6, v7)):
@@ -358,6 +368,8 @@
     cast(1)
     ring(1)
     cast(2)
+    for copy in arriving[3:]:
+        copy.wait()
     own[3] = wo[...].astype(BF)
     for q in range(4):
         own[4 + q] = wi[:, q * D : (q + 1) * D].astype(BF)
@@ -539,7 +551,7 @@
             shape(3, n, 2, 2, SEQ, SEQ), shape(t, D), shape(t, D, dtype=F32), shape(t, D), shape(t, D), shape(t, D),
             shape(t, D), shape(8, t, D),
         ),
-        in_specs=[VM, VM, SM] + [VM] * 15 + [ANY],
+        in_specs=[ANY, VM, SM] + [ANY] * 6 + [VM] * 9 + [ANY],
         out_specs=(VM, VM) + (ANY,) * 11,
         scratch_shapes=[
             pltpu.VMEM((12, TR, D), BF),
@@ -561,11 +573,16 @@
         + [pltpu.VMEM((4, t, D), BF)] * 2
         + [
             pltpu.VMEM((256, D), F32),
+            pltpu.VMEM((t, D), BF),
+            *[pltpu.VMEM((TR, D), F32)] * 4,
+            pltpu.VMEM((TR, FF), F32),
+            pltpu.VMEM((4 * TR, D), F32),
             pltpu.SemaphoreType.DMA((GATHER_COPIES,)),
             pltpu.SemaphoreType.DMA((GATHER_COPIES,)),
             pltpu.SemaphoreType.DMA((10,)),
             pltpu.SemaphoreType.DMA((2,)),
             pltpu.SemaphoreType.DMA((t // 256, 6)),
+            pltpu.SemaphoreType.DMA((7,)),
         ],
         compiler_params=params(collective_id=0, has_side_effects=True),
         name="forward",
@@ -749,9 +766,9 @@
 
 
 def backward_kernel(
-    x, qkv_in, e_in, att_in, dos_in, bg_in, res_in, fa_in, hl_in, og_in, ai_in, sums_in, bsum,
+    x_in, qkv_in, e_in, att_in, dos_in, bg_in, res_in, fa_in, hl_in, og_in, ai_in, sums_in, bsum,
     out, result, ovec,
-    qkv, att, dos, bg, res, fa, dqkv, gx, go, ebuf, sums, vt, vheld, vrecv, vplane, vz, *rest,
+    x, qkv, att, dos, bg, res, fa, dqkv, gx, go, ebuf, sums, vt, vheld, vrecv, vplane, vz, *rest,
 ):
     bufs, (ssem, rsem, lsem, esem) = rest[:-4], rest[-4:]
     p = Place()
@@ -767,6 +784,7 @@
         ("dos", lambda: dos_in, lambda: dos),
         ("res", lambda: res_in, lambda: res),
         ("fa", lambda: fa_in, lambda: fa.at[0:3]),
+        ("x", lambda: x_in, lambda: x),
     )
     load = {
         name: lambda k=k, src=src, dst=dst: pltpu.make_async_copy(src(), dst(), lsem.at[k])
@@ -788,6 +806,7 @@
         load[name]().start()
     in_copy(0, 0).start()
     load["res"]().start()
+    load["x"]().start()
 
     def staged(j):
         return fa.at[j // 2, 4 * (j % 2) : 4 * (j % 2) + 4]
@@ -877,6 +896,7 @@
     jobs[6].send()
     load["qkv"]().wait()
     load["dos"]().wait()
+    load["x"]().wait()
     steps = {
         1: lambda: (jobs[0].turn(), jobs[1].relay(1), jobs[3].relay(1), begin(4), begin(5),),
         2: lambda: (begin(6),),
@@ -999,9 +1019,10 @@
     return pl.pallas_call(
         backward_kernel,
         out_shape=(shape(t, D), shape(12, TR, D), shape(16, 128, dtype=F32)),
-        in_specs=[VM] + [ANY] * 10 + [VM, VM],
+        in_specs=[ANY] * 11 + [VM, VM],
         out_specs=(VM,) * 3,
         scratch_shapes=[
+            pltpu.VMEM((t, D), BF),
             pltpu.VMEM((3, t, D), BF),
             pltpu.VMEM((t, D), BF),
             pltpu.VMEM((t, D), BF),
@@ -1023,7 +1044,7 @@
         + [
             pltpu.SemaphoreType.DMA((REDUCE_COPIES,)),
             pltpu.SemaphoreType.DMA((REDUCE_COPIES,)),
-            pltpu.SemaphoreType.DMA((11,)),
+            pltpu.SemaphoreType.DMA((12,)),
             pltpu.SemaphoreType.DMA((2,)),
         ],
         compiler_params=params(collective_id=1, has_side_effects=True),

time: 185 us -> 184 us (level)
  Pallas kernels: 184 us -> 182 us
where the time goes in v7:
time: 184 us; the launch traced here: 183 us
  Pallas kernels  182 us (99%)
    pallas_call x1, Pallas kernels, forward(): pl.pallas_call(forward_kernel, out_shape=(shape(8, D, dtype=F32), shape(1...  91.7 us
    pallas_call x1, Pallas kernels, backward(): pl.pallas_call(backward_kernel, out_shape=(shape(t, D), shape(12, TR, D),...  85.5 us
    pallas_call x1, Pallas kernels, finish(): pl.pallas_call(finish_kernel, grid=(steps,), out_shape=tuple((shape(TR, D...  4.6 us

profile of v7, /device:TPU:0, one launch (start us, length us, event | category | flops | bytes accessed | tf_op | source)
XLA Modules:
  0.0 183.3 jit_solution(10615469733958518809)
XLA Ops:
  1.3 91.7 %forward.1 = (f32[8,768]{1,0:T(8,128)}, f32[1,3072]{1,0:T(1,128)}, bf16[3,8,96,768]{3,2,1,0:T(8,128)(2,1)}, bf16[3,1024,768]{2,1,0:T(8,128)(2,1)}, bf16[1024,768...) custom-call(bf16[1024,768]{1,0:T(8,128)(2,1)} %x_in.3, ...), custom_call_target="tpu_custom_call" | custom-call | tf_op jit(solution)/shard_map/forward/pallas_call | solution.py:547
  93.0 85.5 %backward.1 = (bf16[1024,768]{1,0:T(8,128)(2,1)}, bf16[12,96,768]{2,1,0:T(8,128)(2,1)}, f32[16,128]{1,0:T(8,128)}) custom-call(bf16[1024,768]{1,0:T(8,128)(2,1)} %x_in.3, bf16[3,1024,768]{2,1,0:T(8,128)(2,1)} %get-tuple-element.50.qkv_in, bf16[3,2,2,2,512,512]{5,4,3,2,1,0:T(8,128)(2,1)} %get-tuple-element.51.e_in, ...), custom_call_target="tpu_custom_call" | custom-call | tf_op jit(solution)/shard_map/backward/pallas_call | solution.py:1019
  178.5 4.6 %finish.1 = (f32[96,768]{1,0:T(8,128)}, f32[96,768]{1,0:T(8,128)}, f32[96,768]{1,0:T(8,128)}, f32[96,768]{1,0:T(8,128)}, f32[96,3072]{1,0:T(8,128)}, /*index=5*/...) custom-call(bf16[12,96,768]{2,1,0:T(8,128)(2,1)} %get-tuple-element., ...), custom_call_target="tpu_custom_call" | custom-call | tf_op jit(solution)/shard_map/finish/pallas_call | solution.py:1084

commit v8 on v7

--- a/solution.py
+++ b/solution.py
@@ -408,7 +408,7 @@
     plane(1, "zo")
     relay(1, "zb")
     onward(2)
-    ring(INNER)
+    ring(WO)
     relay(1, "za")
     plane(2, "zb", "za")
     relay(0, "zo")
@@ -417,18 +417,19 @@
     share(1, "zb")
     plane(2, "zo")
     share(1, "za")
-    relay(2, "zb", "za")
+    relay(2, "zb")
+    onward(WO)
+    ring(INNER)
+    relay(2, "za")
     share(0, "zo")
-    onward(INNER)
-    ring(WO)
+    plane(WO, "zb", "za")
     share(1, "zo")
-    plane(INNER, "zb")
     relay(2, "zo")
     net.wait(*[("v", k) for k in range(1, 8)])
     local["vec"]().wait()
     expand_vectors(fv, rows, binner)
-    share(2, "zb", "za")
-    plane(INNER, "za")
+    share(2, "zb")
+    plane(WO, "zo")
     local["own a"]().wait()
     keep = kept[0]
 
@@ -438,23 +439,26 @@
 
     before = {0: lambda: landed(0), 4: lambda: landed(1), 8: lambda: landed(2)}
     steps = {
-        1: lambda: (plane(INNER, "zo"), relay(INNER, "zb"), onward(WO), ring(OUTER), share(2, "zo"), plane(WO, "zb", "za"),),
-        2: lambda: (relay(INNER, "za"),),
-        4: lambda: (relay(INNER, "zo"), plane(WO, "zo"), relay(WO, "zb"),),
-        5: lambda: (relay(WO, "za"), onward(OUTER), plane(OUTER, "zb"),),
-        6: lambda: (share(INNER, "zb"),),
-        7: lambda: (relay(WO, "zo"), plane(OUTER, "za"),),
-        8: lambda: (share(INNER, "za"),),
-        9: lambda: (share(INNER, "zo"), relay(OUTER, "zb"), plane(OUTER, "zo"),),
-        10: lambda: (share(WO, "zb", "za"),),
-        11: lambda: (relay(OUTER, "za"), share(WO, "zo"), relay(OUTER, "zo"),),
+        0: lambda: (share(2, "za", "zo"), relay(WO), onward(INNER), ring(OUTER), plane(INNER, "zb"),),
+        1: lambda: (plane(INNER, "za"),),
+        2: lambda: (share(WO),),
+        4: lambda: (relay(INNER, "zb"), plane(INNER, "zo"),),
+        5: lambda: (onward(OUTER), plane(OUTER, "zb"),),
+        6: lambda: (relay(INNER, "za"),),
+        8: lambda: (share(INNER, "zb"), relay(INNER, "zo"), plane(OUTER, "za"),),
+        9: lambda: (plane(OUTER, "zo"),),
+        10: lambda: (relay(OUTER, "zb"),),
     }
     later = {
+        0: lambda: (share(OUTER, "zb"),),
         1: lambda: (share(OUTER, "za", "zo"),),
     }
 
     def after_residual():
-        share(OUTER, "zb")
+        relay(OUTER, "za")
+        share(INNER, "za")
+        relay(OUTER, "zo")
+        share(INNER, "zo")
 
     def at_step(i, table):
         for k, step in table.items():

time: 184 us -> 181 us (0.984)
  Pallas kernels: 182 us -> 180 us
where the time goes in v8:
time: 181 us
  Pallas kernels  180 us (99%)
    pallas_call x1, Pallas kernels, forward(): pl.pallas_call(forward_kernel, out_shape=(shape(8, D, dtype=F32), shape(1...  90.1 us
    pallas_call x1, Pallas kernels, backward(): pl.pallas_call(backward_kernel, out_shape=(shape(t, D), shape(12, TR, D),...  84.9 us
    pallas_call x1, Pallas kernels, finish(): pl.pallas_call(finish_kernel, grid=(steps,), out_shape=tuple((shape(TR, D...  4.6 us

profile of v8, /device:TPU:0, one launch (start us, length us, event | category | flops | bytes accessed | tf_op | source)
XLA Modules:
  0.0 181.1 jit_solution(1682480047320259418)
XLA Ops:
  1.3 90.1 %forward.1 = (f32[8,768]{1,0:T(8,128)}, f32[1,3072]{1,0:T(1,128)}, bf16[3,8,96,768]{3,2,1,0:T(8,128)(2,1)}, bf16[3,1024,768]{2,1,0:T(8,128)(2,1)}, bf16[1024,768...) custom-call(bf16[1024,768]{1,0:T(8,128)(2,1)} %x_in.3, ...), custom_call_target="tpu_custom_call" | custom-call | tf_op jit(solution)/shard_map/forward/pallas_call | solution.py:551
  91.4 84.9 %backward.1 = (bf16[1024,768]{1,0:T(8,128)(2,1)}, bf16[12,96,768]{2,1,0:T(8,128)(2,1)}, f32[16,128]{1,0:T(8,128)}) custom-call(bf16[1024,768]{1,0:T(8,128)(2,1)} %x_in.3, bf16[3,1024,768]{2,1,0:T(8,128)(2,1)} %get-tuple-element.50.qkv_in, bf16[3,2,2,2,512,512]{5,4,3,2,1,0:T(8,128)(2,1)} %get-tuple-element.51.e_in, ...), custom_call_target="tpu_custom_call" | custom-call | tf_op jit(solution)/shard_map/backward/pallas_call | solution.py:1023
  176.3 4.6 %finish.1 = (f32[96,768]{1,0:T(8,128)}, f32[96,768]{1,0:T(8,128)}, f32[96,768]{1,0:T(8,128)}, f32[96,768]{1,0:T(8,128)}, f32[96,3072]{1,0:T(8,128)}, /*index=5*/...) custom-call(bf16[12,96,768]{2,1,0:T(8,128)(2,1)} %get-tuple-element., ...), custom_call_target="tpu_custom_call" | custom-call | tf_op jit(solution)/shard_map/finish/pallas_call | solution.py:1088

commit v9 on v8

--- a/solution.py
+++ b/solution.py
@@ -318,7 +318,7 @@
             ((wq_in, wq), (wk_in, wk), (wv_in, wv), (wo_in, wo), (wi_in, wi), (wr_in, wr), (x_in, x))
         )
     ]
-    for copy in arriving:
+    for copy in arriving[0:3]:
         copy.start()
 
     def cast(c):
@@ -327,6 +327,8 @@
 
     for copy in arriving[0:3]:
         copy.wait()
+    for copy in arriving[3:]:
+        copy.start()
     cast(0)
     vtile[...] = jnp.zeros_like(vtile)
     for k, ref in enumerate((v0, v1, v2, v3, v4, v5, v6, v7)):
@@ -806,11 +808,6 @@
     block_copy(0).start()
     block_copy(1).start()
     load["og"]().start()
-    for name in ("att", "bg", "dos"):
-        load[name]().start()
-    in_copy(0, 0).start()
-    load["res"]().start()
-    load["x"]().start()
 
     def staged(j):
         return fa.at[j // 2, 4 * (j % 2) : 4 * (j % 2) + 4]
@@ -875,9 +872,16 @@
             load["hl"]().wait()
         if j == 4:
             load["og"]().wait()
+        block_copy(j).wait()
         if j + 2 < 8:
             block_copy(j + 2).start()
-        block_copy(j).wait()
+        if j == 2:
+            for name in ("att", "bg", "dos"):
+                load[name]().start()
+            in_copy(0, 0).start()
+        if j == 4:
+            load["res"]().start()
+            load["x"]().start()
         block = qkv.at[j % 3]
         if j < 4:
             tiles = mm(hl[...], block[...], TN).astype(BF).reshape(4, 2, TR, D)

time: 181 us -> 181 us (level)
  no operation moved by 1% of the time
where the time goes in v9:
time: 181 us
  Pallas kernels  179 us (99%)
    pallas_call x1, Pallas kernels, forward(): pl.pallas_call(forward_kernel, out_shape=(shape(8, D, dtype=F32), shape(1...  90.1 us
    pallas_call x1, Pallas kernels, backward(): pl.pallas_call(backward_kernel, out_shape=(shape(t, D), shape(12, TR, D),...  84.6 us
    pallas_call x1, Pallas kernels, finish(): pl.pallas_call(finish_kernel, grid=(steps,), out_shape=tuple((shape(TR, D...  4.6 us

profile of v9, /device:TPU:0, one launch (start us, length us, event | category | flops | bytes accessed | tf_op | source)
XLA Modules:
  0.0 180.8 jit_solution(10645766504954262130)
XLA Ops:
  1.3 90.1 %forward.1 = (f32[8,768]{1,0:T(8,128)}, f32[1,3072]{1,0:T(1,128)}, bf16[3,8,96,768]{3,2,1,0:T(8,128)(2,1)}, bf16[3,1024,768]{2,1,0:T(8,128)(2,1)}, bf16[1024,768...) custom-call(bf16[1024,768]{1,0:T(8,128)(2,1)} %x_in.3, ...), custom_call_target="tpu_custom_call" | custom-call | tf_op jit(solution)/shard_map/forward/pallas_call | solution.py:553
  91.4 84.6 %backward.1 = (bf16[1024,768]{1,0:T(8,128)(2,1)}, bf16[12,96,768]{2,1,0:T(8,128)(2,1)}, f32[16,128]{1,0:T(8,128)}) custom-call(bf16[1024,768]{1,0:T(8,128)(2,1)} %x_in.3, bf16[3,1024,768]{2,1,0:T(8,128)(2,1)} %get-tuple-element.50.qkv_in, bf16[3,2,2,2,512,512]{5,4,3,2,1,0:T(8,128)(2,1)} %get-tuple-element.51.e_in, ...), custom_call_target="tpu_custom_call" | custom-call | tf_op jit(solution)/shard_map/backward/pallas_call | solution.py:1027
  176.0 4.6 %finish.1 = (f32[96,768]{1,0:T(8,128)}, f32[96,768]{1,0:T(8,128)}, f32[96,768]{1,0:T(8,128)}, f32[96,768]{1,0:T(8,128)}, f32[96,3072]{1,0:T(8,128)}, /*index=5*/...) custom-call(bf16[12,96,768]{2,1,0:T(8,128)(2,1)} %get-tuple-element., ...), custom_call_target="tpu_custom_call" | custom-call | tf_op jit(solution)/shard_map/finish/pallas_call | solution.py:1092
